TPU v7x, 32 devices: a whole 2x2x4 slice. The times are simulated.
32 devices in a mesh: dp: 4 (over z), seq: 2 (over y), tile: 4 (over x, core).
Axes of the slice: x: 2, y: 2, z: 4, core: 2. Of those that a mesh axis runs over, the one named last changes fastest.
Arguments:
- latents: bfloat16 [4, 2, 512, 1152], P('dp', 'seq', 'tile'), may hold values from -6 to 6
- upstream: bfloat16 [4, 2, 512, 1152], P('dp', 'seq', 'tile'), may hold values from -6 to 6
- modulation: float32 [4, 2, 1152], P('dp'), may hold values from -0.5 to 6
- space_qkv: bfloat16 [1152, 1728], P(('dp', 'tile')), may hold values from -1 to 1
- space_out: bfloat16 [576, 1152], P(('dp', 'tile')), may hold values from -0.25 to 0.25
- time_qkv: bfloat16 [1152, 1728], P(('dp', 'tile')), may hold values from -1 to 1
- time_out: bfloat16 [576, 1152], P(('dp', 'tile')), may hold values from -0.25 to 0.25
- space_pattern: int32 [8, 4], P('tile'), may hold values 0 or 1
- time_mask: int32 [2, 2], replicated, may hold values 0 or 1
Outputs:
- result: bfloat16 [4, 2, 512, 1152], P('dp', 'seq', 'tile')
- start_grad: bfloat16 [4, 2, 512, 1152], P('dp', 'seq', 'tile')
- time_out_grad: float32 [576, 1152], P(('dp', 'tile'))
All inputs are finite; a program needn't handle non-finite values. No bound on the sum of `space_pattern` on one device may be relied on, other than what follows from the above.
Results may differ from a plain program's by a relative error of at most 0.035.
Values may be sent and summed in bfloat16 or wider, within the bound.
No kernel may reach another device: no remote copies, remote signals or barrier semaphores. Data moves between devices by JAX's collectives and lax.ppermute only.
A program may use at most 64 MiB of HBM per device.

v0:
```python
import jax
import jax.numpy as jnp
from jax import lax
from jax.sharding import PartitionSpec as P

HEADS = 8
HEAD_DIM = 72


EPSILON = 1e-06
MASKED = -1e30


def extended(block, sides, width):
    for axis, dim in sides:
        count = lax.axis_size(axis)
        forward = [(i, i + 1) for i in range(count - 1)]
        backward = [(target, source) for source, target in forward]
        low = lax.ppermute(
            lax.slice_in_dim(block, block.shape[dim] - width, None, axis=dim), axis, forward
        )
        high = lax.ppermute(lax.slice_in_dim(block, 0, width, axis=dim), axis, backward)
        block = jnp.concatenate([low, block, high], axis=dim)
    return block


def shifted(array, axis, by):
    devices = lax.axis_size(axis)
    pairs = [(i, i + by) for i in range(devices) if 0 <= i + by < devices]
    return lax.ppermute(array, axis, pairs)


def heads(rows):
    return rows.reshape(rows.shape[:-1] + (HEADS, HEAD_DIM))


def merged(rows):
    return rows.reshape(rows.shape[:-2] + (HEADS * HEAD_DIM,))


def split(rows):
    width = HEADS * HEAD_DIM
    return (
        heads(rows[..., :width]),
        heads(rows[..., width : 2 * width]),
        heads(rows[..., 2 * width :]),
    )


def project(rows, weight):
    flat = rows.reshape(-1, rows.shape[-1])
    out = jnp.dot(flat, weight, preferred_element_type=jnp.float32)
    return out.reshape(rows.shape[:-1] + (weight.shape[1],))


def project_back(rows, weight):
    flat = rows.reshape(-1, rows.shape[-1])
    out = jnp.einsum("rk,dk->rd", flat, weight, preferred_element_type=jnp.float32)
    return out.reshape(rows.shape[:-1] + (weight.shape[0],))


def norm_scale(values, gain):
    inverse = lax.rsqrt(jnp.mean(values * values, axis=-1, keepdims=True) + EPSILON)
    return (inverse, values * inverse * gain)


def norm_back(values, inverse, gain, grad):
    scaled = grad * gain
    cubed = inverse * inverse * inverse
    return inverse * scaled - values * cubed * jnp.mean(scaled * values, axis=-1, keepdims=True)


def forms(lead):
    if lead:
        return ("cbqhe", "cbkhe")
    return ("cqbhe", "ckbhe")


def weights_of(query, keys, allowed, lead):
    qform, kform = forms(lead)
    scores = jnp.einsum(
        qform + "," + kform + "->cbhqk", query, keys, preferred_element_type=jnp.float32
    )
    scores = jnp.where(allowed, scores * HEAD_DIM ** (-0.5), MASKED)
    top = jnp.max(scores, axis=-1, keepdims=True)
    raised = jnp.exp(scores - top)
    return raised / jnp.sum(raised, axis=-1, keepdims=True)


def attend(query, keys, values, allowed, lead):
    qform, kform = forms(lead)
    probs = weights_of(query, keys, allowed, lead)
    out = jnp.einsum(
        "cbhqk," + kform + "->" + qform,
        probs.astype(jnp.bfloat16),
        values,
        preferred_element_type=jnp.float32,
    )
    return (out.astype(jnp.bfloat16), probs)


def attend_back(query, keys, values, probs, grad_out, lead):
    qform, kform = forms(lead)
    dprob = jnp.einsum(
        qform + "," + kform + "->cbhqk", grad_out, values, preferred_element_type=jnp.float32
    )
    delta = jnp.sum(probs * dprob, axis=-1, keepdims=True)
    dscore = (probs * (dprob - delta) * HEAD_DIM ** (-0.5)).astype(jnp.bfloat16)
    dquery = jnp.einsum(
        "cbhqk," + kform + "->" + qform, dscore, keys, preferred_element_type=jnp.float32
    )
    dkeys = jnp.einsum(
        "cbhqk," + qform + "->" + kform, dscore, query, preferred_element_type=jnp.float32
    )
    dvalues = jnp.einsum(
        "cbhqk," + qform + "->" + kform,
        probs.astype(jnp.bfloat16),
        grad_out,
        preferred_element_type=jnp.float32,
    )
    return (dquery, dkeys, dvalues)


def time_ok(time_mask):
    frame = jnp.arange(time_mask.shape[0])
    return (frame[None, :] == frame[:, None]) | (frame[None, :] < frame[:, None]) & (time_mask == 1)


def local(
    latents,
    upstream,
    modulation,
    space_qkv,
    space_out,
    time_qkv,
    time_out,
    space_pattern,
    time_mask,
):
    width = HEADS * HEAD_DIM
    own = latents.shape[2]
    span = own // 2
    space_qkv_all, space_out_all = (
        lax.all_gather(space_qkv, ("dp", "tile"), axis=0, tiled=True),
        lax.all_gather(space_out, ("dp", "tile"), axis=0, tiled=True),
    )
    start = latents.astype(jnp.float32)
    gain_space = 1.0 + modulation[:, 0][:, None, None, :]
    gain_time = 1.0 + modulation[:, 1][:, None, None, :]
    inverse_space, normed = norm_scale(start, gain_space)
    space_rows = project(normed.astype(jnp.bfloat16), space_qkv_all).astype(jnp.bfloat16)
    query = heads(space_rows[..., :width])
    window = extended(space_rows[..., width:], (("tile", 2),), span)
    keys = heads(window[..., :width])
    values = heads(window[..., width:])
    tile_at = lax.axis_index("tile")
    tiles = lax.axis_size("tile")
    slots = jnp.arange(4)
    block_ok = (space_pattern == 1) | (slots[None, :] == jnp.arange(2)[:, None] + 1)
    global_block = 2 * tile_at - 1 + slots
    block_ok = block_ok & ((global_block >= 0) & (global_block < 2 * tiles))[None, :]
    allowed = jnp.repeat(jnp.repeat(block_ok, span, axis=0), span, axis=1)[None, None, None]
    space_heads, space_probs = attend(query, keys, values, allowed, True)
    space_att = merged(space_heads)
    middle = start + project(space_att, space_out_all)
    time_qkv_all, time_out_all = (
        lax.all_gather(time_qkv, ("dp", "tile"), axis=0, tiled=True),
        lax.all_gather(time_out, ("dp", "tile"), axis=0, tiled=True),
    )
    inverse_time, normed_time = norm_scale(middle, gain_time)
    normed_time = normed_time.astype(jnp.bfloat16)
    frame_mask = time_ok(time_mask)[None, None, None]
    time_local = project(normed_time, time_qkv_all).astype(jnp.bfloat16)
    rows = lax.all_to_all(time_local, "seq", split_axis=2, concat_axis=1, tiled=True)
    time_query, time_keys, time_values = split(rows)
    out, probs = attend(time_query, time_keys, time_values, frame_mask, False)
    time_patches = merged(out)
    time_att = lax.all_to_all(time_patches, "seq", split_axis=1, concat_axis=2, tiled=True)
    result = (middle + project(time_att, time_out_all)).astype(jnp.bfloat16)
    flat_up = upstream.reshape(-1, upstream.shape[-1])
    term = jnp.einsum(
        "rh,rd->hd", time_att.reshape(-1, width), flat_up, preferred_element_type=jnp.float32
    )
    rows_part = lax.psum_scatter(
        term.astype(jnp.bfloat16), ("dp", "tile"), scatter_dimension=0, tiled=True
    )
    time_out_grad = lax.psum(rows_part, "seq").astype(jnp.float32)
    grad_att = project_back(upstream, time_out_all).astype(jnp.bfloat16)
    grad_patches = lax.all_to_all(grad_att, "seq", split_axis=2, concat_axis=1, tiled=True)
    time_query, time_keys, time_values = split(rows)
    time_probs = weights_of(time_query, time_keys, frame_mask, False)
    gq, gk, gv = attend_back(
        time_query, time_keys, time_values, time_probs, heads(grad_patches), False
    )
    patch_grads = jnp.concatenate([merged(gq), merged(gk), merged(gv)], axis=-1).astype(
        jnp.bfloat16
    )
    time_grads = lax.all_to_all(patch_grads, "seq", split_axis=1, concat_axis=2, tiled=True)
    middle_grad = upstream.astype(jnp.float32) + norm_back(
        middle, inverse_time, gain_time, project_back(time_grads, time_qkv_all)
    )
    space_grad_att = project_back(middle_grad.astype(jnp.bfloat16), space_out_all).astype(
        jnp.bfloat16
    )
    dq, dk, dv = attend_back(query, keys, values, space_probs, heads(space_grad_att), True)
    rim = jnp.concatenate([merged(dk), merged(dv)], axis=-1)
    from_right = shifted(rim[:, :, :span].astype(jnp.bfloat16), "tile", -1).astype(jnp.float32)
    from_left = shifted(rim[:, :, span + own :].astype(jnp.bfloat16), "tile", 1).astype(jnp.float32)
    own_grads = rim[:, :, span : span + own] + jnp.concatenate([from_left, from_right], axis=2)
    space_grads = jnp.concatenate([merged(dq), own_grads], axis=-1).astype(jnp.bfloat16)
    start_grad = middle_grad + norm_back(
        start, inverse_space, gain_space, project_back(space_grads, space_qkv_all)
    )
    return (result, start_grad.astype(jnp.bfloat16), time_out_grad)


def solution(mesh):
    in_specs = (
        P("dp", "seq", "tile", None),
        P("dp", "seq", "tile", None),
        P("dp", None, None),
        P(("dp", "tile"), None),
        P(("dp", "tile"), None),
        P(("dp", "tile"), None),
        P(("dp", "tile"), None),
        P("tile", None),
        P(),
    )
    out_specs = (
        P("dp", "seq", "tile", None),
        P("dp", "seq", "tile", None),
        P(("dp", "tile"), None),
    )
    return jax.shard_map(local, mesh=mesh, in_specs=in_specs, out_specs=out_specs, check_vma=False)
```

profile of v0, /device:TPU:0, one launch (start us, length us, event | category | flops | bytes accessed | tf_op | source)
XLA Modules:
  0.0 383.9 jit_solution(4737822609849031013)
XLA Ops:
  14.2 38.0 %all-gather.13.cloned.1.call-done = bf16[16,36,1152]{2,1,0:T(8,128)(2,1)} async-done(((bf16[1,36,1152]{2,1,0:T(8,128)(2,1)}), bf16[16,36,1152]{2,1,0:T(8,128)(2,1)}) %all-gather.13.cloned.1.call-update) | async-done | bytes 1327120 | tf_op jit(solution)/shard_map/all_gather | solution.py:168
  52.2 2.2 reshape.419
  54.5 49.2 %all-gather.7.cloned.1.call-done = bf16[1152,1728]{1,0:T(8,128)(2,1)} async-done(((bf16[72,1728]{1,0:T(8,128)(2,1)}), bf16[1152,1728]{1,0:T(8,128)(2,1)}) %all-gather.7.cloned.1.call-update) | async-done | bytes 3981328 | tf_op jit(solution)/shard_map/all_gather | solution.py:144
  103.6 3.8 %fusion.8 = bf16[1,1,128,1728]{2,3,1,0:T(8,128)(2,1)S(1)} fusion(bf16[1152,1728]{1,0:T(8,128)(2,1)} %all-gather.7.cloned.1.call-done, bf16[1,1,128,1152]{3,2,1,0:T(8,128)(2,1)S(1)} %copy-done, f32[1152]{0:T(1024)S(1)} %get-tuple-element.4, f32[128]{0:T(128)S(1)} %get-tuple-element.15), kind=kOutput, calls=%fused_computation.14 | convolution fusion | flops 510418944 | bytes 4723712 | tf_op jit(solution)/shard_map/dot_general | solution.py:52
  108.4 2.9 collective-permute-start
  114.0 1.7 reduce.23
  116.5 4.2 %all-to-all-start.2 = ((bf16[2,2,18432]{2,1,0:T(2,128)(2,1)}), bf16[2,2,18432]{2,1,0:T(2,128)(2,1)}, u32[]{:S(2)}, u32[]{:S(2)}) async-start(bf16[2,2,18432]{2,1,0:T(2,128)(2,1)} %reshape.426), calls=%async_computation.2 | async-start | bytes 294912 | tf_op jit(solution)/shard_map/all_to_all | solution.py:189
  120.7 23.1 %all-gather.11.cloned.1.call-done = bf16[16,36,1152]{2,1,0:T(8,128)(2,1)} async-done(((bf16[1,36,1152]{2,1,0:T(8,128)(2,1)}), bf16[16,36,1152]{2,1,0:T(8,128)(2,1)}) %all-gather.11.cloned.1.call-update) | async-done | bytes 1327120 | tf_op jit(solution)/shard_map/all_gather | solution.py:145
  143.8 2.2 reshape.417
  149.1 3.3 fusion.94
  152.3 2.4 convolution_convert_fusion.8
  156.8 38.3 %all-gather.9.cloned.1.call-done = bf16[1152,1728]{1,0:T(8,128)(2,1)} async-done(((bf16[72,1728]{1,0:T(8,128)(2,1)}), bf16[1152,1728]{1,0:T(8,128)(2,1)}) %all-gather.9.cloned.1.call-update) | async-done | bytes 3981328 | tf_op jit(solution)/shard_map/all_gather | solution.py:167
  195.1 4.6 %fusion.9 = bf16[1,1,128,1728]{2,3,1,0:T(8,128)(2,1)} fusion(bf16[1152,1728]{1,0:T(8,128)(2,1)} %all-gather.9.cloned.1.call-done, f32[1,1,128,1152]{3,2,1,0:T(8,128)S(1)} %get-tuple-element.21, f32[1152]{0:T(1024)S(1)} %get-tuple-element.3, f32[128]{0:T(128)} %get-tuple-element.17), kind=kOutput, calls=%fused_computation.15 | convolution fusion | flops 510271488 | bytes 5018624 | tf_op jit(solution)/shard_map/dot_general | solution.py:52
  199.7 3.1 copy.57
  202.8 5.3 %reduce.22 = bf16[128,1728]{1,0:T(8,128)(2,1)} reduce(bf16[128,1,1,1728]{3,2,1,0:T(2,128)(2,1)} %bitcast.147, bf16[]{:T(256)} %broadcast.216), dimensions={1,2}, to_apply=%bitcast.116.reduce_sub_computation | reduce | bytes 884738
  208.1 2.2 reshape.424
  210.3 4.4 %all-to-all-start = ((bf16[2,2,55296]{2,1,0:T(2,128)(2,1)}), bf16[2,2,55296]{2,1,0:T(2,128)(2,1)}, u32[]{:S(2)}, u32[]{:S(2)}) async-start(bf16[2,2,55296]{2,1,0:T(2,128)(2,1)} %reshape.424), calls=%async_computation | async-start | bytes 884736 | tf_op jit(solution)/shard_map/all_to_all | solution.py:174
  219.1 1.9 reshape.427
  221.0 2.6 bitcast_reduce_fusion
  223.6 1.9 reshape.410
  225.5 2.5 reshape.425
  230.0 1.9 reshape.404
  231.9 1.9 reshape.405
  233.8 1.9 reshape.403
  235.7 2.5 fusion.71
  238.3 4.3 %fusion.95 = (f32[64,8,2]{2,1,0:T(8,128)}, f32[64,8,2,2]{2,3,1,0:T(2,128)}) fusion(pred[2,2]{0,1:T(4,128)(4,1)} %copy.58, bf16[2,64,8,72]{3,2,1,0:T(8,128)(2,1)} %reshape.405, bf16[2,64,8,72]{3,2,1,0:T(8,128)(2,1)} %reshape.404), kind=kOutput, calls=%fused_computation.135 | convolution fusion | flops 303105 | bytes 307204 | tf_op jit(solution)/shard_map/sub | solution.py:86
  244.0 2.5 fusion.28
  248.1 3.7 fusion.26
  253.5 1.9 reshape.406
  255.3 4.1 %all-to-all-start.1 = ((bf16[1,2,64,576]{3,2,0,1:T(8,128)(2,1)}), bf16[1,2,64,576]{3,2,0,1:T(8,128)(2,1)}, u32[]{:S(2)}, u32[]{:S(2)}) async-start(bf16[1,2,64,576]{3,2,0,1:T(8,128)(2,1)} %bitcast.158), calls=%async_computation.1 | async-start | bytes 327680 | tf_op jit(solution)/shard_map/all_to_all | solution.py:178
  259.4 3.5 fusion.27
  262.9 1.7 copy.70
  264.6 1.9 concatenate.42
  268.2 1.9 concatenate.43
  271.7 1.9 concatenate.44
  273.6 2.0 concatenate.45
  275.6 4.2 %all-to-all-start.3 = ((bf16[1,2,64,1728]{3,2,0,1:T(8,128)(2,1)}), bf16[1,2,64,1728]{3,2,0,1:T(8,128)(2,1)}, u32[]{:S(2)}, u32[]{:S(2)}) async-start(bf16[1,2,64,1728]{3,2,0,1:T(8,128)(2,1)} %bitcast.154), calls=%async_computation.3 | async-start | bytes 917504 | tf_op jit(solution)/shard_map/all_to_all | solution.py:198
  279.9 2.7 convolution_convert_fusion
  282.5 40.7 %fusion = bf16[48,1152]{1,0:T(8,128)(2,1)} fusion(bf16[576,1152]{1,0:T(8,128)(2,1)} %convolution_convert_fusion), kind=kCustom, calls=%all-reduce-scatter | all-reduce-scatter fusion | flops 884737 | bytes 1438208
  327.0 1.9 collective-permute-start.4
  330.2 2.0 fusion.7
  333.7 5.0 %concatenate.52 = bf16[228,1152]{1,0:T(8,128)(2,1)S(1)} concatenate(bf16[36,1152]{1,0:T(8,128)(2,1)} %copy-done.13, bf16[48,1152]{1,0:T(8,128)(2,1)} %copy-done.11, bf16[48,1152]{1,0:T(8,128)(2,1)} %copy-done.12, bf16[48,1152]{1,0:T(8,128)(2,1)} %collective-permute-done.4, bf16[48,1152]{1,0:T(8,128)(2,1)} %fusion), dimensions={0} | concatenate | bytes 1050624
  339.4 3.8 %fusion.46 = (f32[128]{0:T(128)S(1)}, f32[128,1152]{1,0:T(8,128)S(1)}) fusion(f32[1,1,128,1152]{3,2,1,0:T(8,128)S(1)} %get-tuple-element.21, f32[1152]{0:T(1024)S(1)} %get-tuple-element.3, bf16[128,1728]{1,0:T(8,128)(2,1)} %bitcast.28, bf16[1152,1728]{1,0:T(8,128)(2,1)} %all-gather.9.cloned.1.call-done), kind=kOutput, calls=%fused_computation.70 | convolution fusion | flops 510050176 | bytes 5608448 | tf_op jit(solution)/shard_map/rk,dk->rd/dot_general | solution.py:58
  344.3 1.8 fusion.67
  347.5 8.7 %fusion.30 = f32[8,72,256]{2,1,0:T(8,128)} fusion(bf16[128,8,72]{0,2,1:T(8,128)(2,1)S(1)} %bitcast.170, f32[8,128,256]{2,1,0:T(8,128)} %fusion.100, f32[8,128,256]{2,1,0:T(8,128)} %get-tuple-element.19, f32[8,128]{1,0:T(8,128)S(1)} %copy-done.21), kind=kOutput, calls=%fused_computation.53 | convolution fusion | flops 39585024 | bytes 2838528 | tf_op jit(solution)/shard_map/cbhqk,cbqhe->cbkhe/dot_general | solution.py:112
  358.2 2.0 collective-permute-start.2
  361.7 7.9 %convolution_convert_fusion.7 = bf16[8,72,128]{2,1,0:T(8,128)(2,1)S(1)} fusion(bf16[256,8,72]{0,2,1:T(8,128)(2,1)S(1)} %bitcast.164, f32[8,128,256]{2,1,0:T(8,128)} %fusion.100, f32[8,128,256]{2,1,0:T(8,128)} %get-tuple-element.19, f32[8,128]{1,0:T(8,128)S(1)} %copy-done.21), kind=kOutput, calls=%fused_computation.48 | convolution fusion | flops 39658752 | bytes 2543616 | tf_op jit(solution)/shard_map/cbhqk,cbkhe->cbqhe/dot_general | solution.py:109
  372.5 3.7 fusion.42
  (115 shorter events, 47.1 us)
Async XLA Ops:
  7.2 45.1 %all-gather.13.cloned.1.call-start = ((), (), s32[]{:S(2)}) async-start(), calls=%async_computation.8 | async-start | bytes 1566720 | tf_op jit(solution)/shard_map/all_gather | solution.py:168
  7.9 95.7 %all-gather.7.cloned.1.call-start = ((), (), s32[]{:S(2)}) async-start(), calls=%async_computation.4 | async-start | bytes 4386816 | tf_op jit(solution)/shard_map/all_gather | solution.py:144
  8.6 135.2 %all-gather.11.cloned.1.call-start = ((), (), s32[]{:S(2)}) async-start(), calls=%async_computation.7 | async-start | bytes 1566720 | tf_op jit(solution)/shard_map/all_gather | solution.py:145
  9.4 185.7 %all-gather.9.cloned.1.call-start = ((), (), s32[]{:S(2)}) async-start(), calls=%async_computation.5 | async-start | bytes 4386816 | tf_op jit(solution)/shard_map/all_gather | solution.py:167
  14.2 89.4 %copy-start.16 = (f32[128]{0:T(128)}, f32[128]{0:T(128)S(1)}, u32[]{:S(2)}) copy-start(f32[128]{0:T(128)S(1)} %get-tuple-element.15) | copy-start | bytes 1540
  14.2 89.4 %copy-start = (bf16[1,1,128,1152]{3,2,1,0:T(8,128)(2,1)S(1)}, bf16[1,1,128,1152]{3,2,1,0:T(8,128)(2,1)}, u32[]{:S(2)}) copy-start(bf16[1,1,128,1152]{3,2,1,0:T(8,128)(2,1)} %param.9) | copy-start | bytes 884740
  107.5 5.1 %copy-start.1 = (bf16[1,1,128,1152]{3,2,1,0:T(8,128)(2,1)S(1)}, bf16[1,1,128,1152]{3,2,1,0:T(8,128)(2,1)}, u32[]{:S(2)}) copy-start(bf16[1,1,128,1152]{3,2,1,0:T(8,128)(2,1)} %param.10) | copy-start | bytes 884740
  108.4 38.4 %collective-permute-start = (bf16[1,1,64,1152]{2,3,1,0:T(8,128)(2,1)}, bf16[1,1,64,1152]{2,3,1,0:T(8,128)(2,1)}, u32[]{:S(2)}, u32[]{:S(2)}) collective-permute-start(bf16[1,1,64,1152]{2,3,1,0:T(8,128)(2,1)} %get-tuple-element.12), channel_id=1, source_target_pairs={{0,1},{1,2},{2,3},{4,5},{5,6},{6,7},{8,9},{9,10},{10,11},{12,13},{... | collective-permute-start | bytes 442376 | tf_op jit(solution)/shard_map/ppermute | solution.py:19
  111.3 35.5 %collective-permute-start.1 = (bf16[1,1,64,1152]{2,3,1,0:T(8,128)(2,1)}, bf16[1,1,64,1152]{2,3,1,0:T(8,128)(2,1)}, u32[]{:S(2)}, u32[]{:S(2)}) collective-permute-start(bf16[1,1,64,1152]{2,3,1,0:T(8,128)(2,1)} %get-tuple-element.13), channel_id=1, source_target_pairs={{1,0},{2,1},{3,2},{5,4},{6,5},{7,6},{9,8},{10,9},{11,10},{13,12},{... | collective-permute-start | bytes 442376 | tf_op jit(solution)/shard_map/ppermute | solution.py:22
  116.5 93.8 %all-to-all-start.2 = ((bf16[2,2,18432]{2,1,0:T(2,128)(2,1)}), bf16[2,2,18432]{2,1,0:T(2,128)(2,1)}, u32[]{:S(2)}, u32[]{:S(2)}) async-start(bf16[2,2,18432]{2,1,0:T(2,128)(2,1)} %reshape.426), calls=%async_computation.2 | async-start | bytes 294912 | tf_op jit(solution)/shard_map/all_to_all | solution.py:189
  149.1 3.3 copy-start.4
  149.1 3.3 copy-start.7
  210.3 15.1 %all-to-all-start = ((bf16[2,2,55296]{2,1,0:T(2,128)(2,1)}), bf16[2,2,55296]{2,1,0:T(2,128)(2,1)}, u32[]{:S(2)}, u32[]{:S(2)}) async-start(bf16[2,2,55296]{2,1,0:T(2,128)(2,1)} %reshape.424), calls=%async_computation | async-start | bytes 884736 | tf_op jit(solution)/shard_map/all_to_all | solution.py:174
  242.6 4.0 %copy-start.9 = (bf16[2,64,8,72]{3,2,1,0:T(8,128)(2,1)S(1)}, bf16[2,64,8,72]{3,2,1,0:T(8,128)(2,1)}, u32[]{:S(2)}) copy-start(bf16[2,64,8,72]{3,2,1,0:T(8,128)(2,1)} %reshape.403) | copy-start | bytes 442372
  244.0 2.6 copy-start.6
  255.3 20.3 %all-to-all-start.1 = ((bf16[1,2,64,576]{3,2,0,1:T(8,128)(2,1)}), bf16[1,2,64,576]{3,2,0,1:T(8,128)(2,1)}, u32[]{:S(2)}, u32[]{:S(2)}) async-start(bf16[1,2,64,576]{3,2,0,1:T(8,128)(2,1)} %bitcast.158), calls=%async_computation.1 | async-start | bytes 327680 | tf_op jit(solution)/shard_map/all_to_all | solution.py:178
  275.6 63.8 %all-to-all-start.3 = ((bf16[1,2,64,1728]{3,2,0,1:T(8,128)(2,1)}), bf16[1,2,64,1728]{3,2,0,1:T(8,128)(2,1)}, u32[]{:S(2)}, u32[]{:S(2)}) async-start(bf16[1,2,64,1728]{3,2,0,1:T(8,128)(2,1)} %bitcast.154), calls=%async_computation.3 | async-start | bytes 917504 | tf_op jit(solution)/shard_map/all_to_all | solution.py:198
  279.8 89.7 %all-reduce.4.cloned.1.call-start = ((), (), s32[]{:S(2)}) async-start(), calls=%async_computation.6 | async-start | bytes 184320 | tf_op jit(solution)/shard_map/psum | solution.py:187
  324.1 8.2 %collective-permute-start.6 = (bf16[48,1152]{1,0:T(8,128)(2,1)}, bf16[48,1152]{1,0:T(8,128)(2,1)S(1)}, u32[]{:S(2)}, u32[]{:S(2)}) collective-permute-start(bf16[48,1152]{1,0:T(8,128)(2,1)} %fusion), channel_id=1, source_target_pairs={{0,3},{1,8},{2,9},{3,10},{8,11},{9,16},{10,17},{11,18},{16,19},{17... | collective-permute-start | bytes 331784
  325.4 6.9 %collective-permute-start.5 = (bf16[48,1152]{1,0:T(8,128)(2,1)}, bf16[48,1152]{1,0:T(8,128)(2,1)S(1)}, u32[]{:S(2)}, u32[]{:S(2)}) collective-permute-start(bf16[48,1152]{1,0:T(8,128)(2,1)} %fusion), channel_id=1, source_target_pairs={{0,2},{1,3},{2,8},{3,9},{8,10},{9,11},{10,16},{11,17},{16,18},{17,... | collective-permute-start | bytes 331784
  327.0 6.7 %collective-permute-start.4 = (bf16[48,1152]{1,0:T(8,128)(2,1)}, bf16[48,1152]{1,0:T(8,128)(2,1)}, u32[]{:S(2)}, u32[]{:S(2)}) collective-permute-start(bf16[48,1152]{1,0:T(8,128)(2,1)} %fusion), channel_id=1, source_target_pairs={{0,1},{1,2},{2,3},{3,8},{8,9},{9,10},{10,11},{11,16},{16,17},{17,1... | collective-permute-start | bytes 331784
  328.9 3.4 collective-permute-start.7
  332.3 0.6 copy-start.13
  332.3 0.7 copy-start.11
  333.0 0.7 copy-start.12
  339.4 3.9 %copy-start.2 = (bf16[1,1,128,1152]{3,2,1,0:T(8,128)(2,1)S(1)}, bf16[1,1,128,1152]{3,2,1,0:T(8,128)(2,1)}, u32[]{:S(2)}) copy-start(bf16[1,1,128,1152]{3,2,1,0:T(8,128)(2,1)} %param.10) | copy-start | bytes 884740
  339.4 3.9 %copy-start.14 = (f32[128]{0:T(128)S(1)}, f32[128]{0:T(128)}, u32[]{:S(2)}) copy-start(f32[128]{0:T(128)} %get-tuple-element.17) | copy-start | bytes 1540
  339.4 3.9 %copy-start.18 = (f32[128]{0:T(128)S(1)}, f32[128]{0:T(128)}, u32[]{:S(2)}) copy-start(f32[128]{0:T(128)} %get-tuple-element.16) | copy-start | bytes 1540
  343.3 1.0 copy-start.8
  343.3 1.0 copy-start.21
  344.3 1.8 copy-start.5
  346.1 1.4 copy-start.10
  358.2 12.9 %collective-permute-start.2 = (bf16[1,1,64,1152]{2,3,1,0:T(8,128)(2,1)}, bf16[1,1,64,1152]{2,3,1,0:T(8,128)(2,1)}, u32[]{:S(2)}, u32[]{:S(2)}) collective-permute-start(bf16[1,1,64,1152]{2,3,1,0:T(8,128)(2,1)} %get-tuple-element.5), channel_id=1, source_target_pairs={{0,1},{1,2},{2,3},{4,5},{5,6},{6,7},{8,9},{9,10},{10,11},{12,13},{... | collective-permute-start | bytes 442376 | tf_op jit(solution)/shard_map/ppermute | solution.py:30
  360.3 10.9 %copy-start.3 = (f32[8,72,256]{2,1,0:T(8,128)S(1)}, f32[8,72,256]{2,1,0:T(8,128)}, u32[]{:S(2)}) copy-start(f32[8,72,256]{2,1,0:T(8,128)} %fusion.30) | copy-start | bytes 1769476
  360.3 10.9 %collective-permute-start.3 = (bf16[1,1,64,1152]{2,3,1,0:T(8,128)(2,1)}, bf16[1,1,64,1152]{2,3,1,0:T(8,128)(2,1)}, u32[]{:S(2)}, u32[]{:S(2)}) collective-permute-start(bf16[1,1,64,1152]{2,3,1,0:T(8,128)(2,1)} %get-tuple-element.6), channel_id=1, source_target_pairs={{1,0},{2,1},{3,2},{5,4},{6,5},{7,6},{9,8},{10,9},{11,10},{13,12},{... | collective-permute-start | bytes 442376 | tf_op jit(solution)/shard_map/ppermute | solution.py:30
  372.5 3.8 copy-start.15
  372.5 3.8 copy-start.17
  372.5 3.8 copy-start.19
  372.5 3.8 copy-start.20
Sparse Core Ops, SparseCore 0:
  10.1 42.0 all-gather.12
  54.5 49.0 all-gather.6
  105.8 38.0 all-gather.10
  146.0 49.0 all-gather.8
  339.5 23.5 all-reduce.3
where the time goes:
time: 389 us; the launch traced here: 384 us
  waiting for transfers between devices  151 us (39%)
  matrix products  66.8 us (17%)
  local copies, waits for them, and re-layouts  59.6 us (15%)
  blocking collectives  40.7 us (10%)
  starting transfers between devices  30.8 us (8%)
  other arithmetic  19.9 us (5%)
  between operations  14.9 us (4%)
    all_gather x1, waiting for transfers between devices, local(): lax.all_gather(space_qkv, ('dp', 'tile'), axis=0, tiled=True)  49.2 us
    unnamed x1, blocking collectives  40.7 us
    all_gather x1, waiting for transfers between devices, local(): lax.all_gather(time_qkv, ('dp', 'tile'), axis=0, tiled=True)  38.3 us
    all_gather x1, waiting for transfers between devices, local(): lax.all_gather(time_out, ('dp', 'tile'), axis=0, tiled=True)  38 us
    unnamed x56, local copies, waits for them, and re-layouts  23.3 us
    all_gather x1, waiting for transfers between devices, local(): lax.all_gather(space_out, ('dp', 'tile'), axis=0, tiled=True)  23.1 us
    dot_general x2, matrix products, attend_back(): jnp.einsum('cbhqk,' + qform + '->' + kform, dscore, query, preferred_elem...  12.2 us
    dot_general x4, matrix products, project(): out = jnp.dot(flat, weight, preferred_element_type=jnp.float32)  11.9 us
  transfers between devices with their start and end apart: 17, of which 5 were waited for; matrix products, arithmetic and copies ran while one was open for 39% of the time, Pallas kernels for 0%

commit v1 on v0

v1 whole, which is shorter than its diff:
```python
import functools

import jax
import jax.numpy as jnp
import numpy as np
from jax import lax
from jax.experimental import pallas as pl
from jax.experimental.pallas import tpu as pltpu
from jax.sharding import PartitionSpec as P

HEADS = 8
HEAD_DIM = 72
WIDTH = HEADS * HEAD_DIM
EPSILON = 1e-06
MASKED = -1e30
SCALE = HEAD_DIM ** (-0.5)
BF16 = jnp.bfloat16
F32 = jnp.float32
VMEM_LIMIT = 16 * 1024 * 1024
PACK_LIMIT = 63 * 1024 * 1024


def mm(a, b):
    return jnp.dot(a, b, preferred_element_type=F32)


def mm_nt(a, b):
    return lax.dot_general(a, b, (((1,), (1,)), ((), ())), preferred_element_type=F32)


def mm_tn(a, b):
    return lax.dot_general(a, b, (((0,), (0,)), ((), ())), preferred_element_type=F32)


def head_masks(kind):
    lane = lax.broadcasted_iota(jnp.int32, (1, WIDTH), 1)
    inside = [(lane >= HEAD_DIM * h) & (lane < HEAD_DIM * (h + 1)) for h in range(HEADS)]
    return [jnp.where(hit, 1.0, 0.0).astype(kind) for hit in inside]


def spread(rows):
    return jnp.concatenate([rows * mask for mask in head_masks(rows.dtype)], axis=0)


def collect(big):
    n = big.shape[0] // HEADS
    masks = head_masks(F32)
    total = big[:n] * masks[0]
    for h in range(1, HEADS):
        total = total + big[h * n : (h + 1) * n] * masks[h]
    return total


def softmax_of(spread_q, keys, allowed):
    n, m = allowed.shape
    scores = (mm_nt(spread_q, keys) * SCALE).reshape(HEADS, n, m)
    scores = jnp.where((allowed > 0)[None], scores, MASKED)
    raised = jnp.exp(scores - jnp.max(scores, axis=-1, keepdims=True))
    probs = raised / jnp.sum(raised, axis=-1, keepdims=True)
    return probs.reshape(HEADS * n, m)


def attention_back(spread_q, keys, values, probs, grad):
    spread_g = spread(grad)
    dprob = mm_nt(spread_g, values)
    delta = jnp.sum(probs * dprob, axis=-1, keepdims=True)
    dscore = (probs * (dprob - delta) * SCALE).astype(BF16)
    dquery = collect(mm(dscore, keys))
    dkeys = mm_tn(dscore, spread_q)
    dvalues = mm_tn(probs.astype(BF16), spread_g)
    return dquery, dkeys, dvalues


def inverse_of(values):
    return lax.rsqrt(jnp.mean(values * values, axis=-1, keepdims=True) + EPSILON)


def norm_back(values, gain, grad):
    inverse = inverse_of(values)
    scaled = grad * gain
    cubed = inverse * inverse * inverse
    return inverse * scaled - values * cubed * jnp.mean(scaled * values, axis=-1, keepdims=True)


def expander(source, rows=WIDTH):
    row = lax.broadcasted_iota(jnp.int32, (rows, source.shape[1]), 0)
    return jnp.where(row == source, 1.0, 0.0).astype(BF16)


def ahead(rows, weight, start, stop, slots):
    total = None
    for (at, count), ref in zip(slots, weight):
        term = mm(rows[:, at : at + count], ref[:, start:stop])
        total = term if total is None else total + term
    return total


def behind(grad, weight, start, stop, select, rounded=False):
    count = grad.shape[0]
    turned = grad.astype(F32).T.astype(BF16)
    parts = [mm(ref[:, start:stop], turned) for ref in weight]
    part = jnp.concatenate(parts, axis=0)
    high = part.astype(BF16)
    if rounded:
        return mm(select[...], high).T.astype(BF16)
    low = (part - high.astype(F32)).astype(BF16)
    both = mm(select[...], jnp.concatenate([high, low], axis=1))
    return (both[:, :count] + both[:, count:]).T


def space_allowed(place, pattern, span, tiles):
    own = 2 * span
    row = lax.broadcasted_iota(jnp.int32, (own, 4 * span), 0)
    column = lax.broadcasted_iota(jnp.int32, (own, 4 * span), 1)
    tile_at = place[0]
    allowed = jnp.zeros((own, 4 * span), jnp.int32)
    for b in range(2):
        for r in range(4):
            block = 2 * tile_at - 1 + r
            inside = (block >= 0) & (block < 2 * tiles)
            seen = inside if r == b + 1 else inside & (pattern[b, r] == 1)
            here = (row >= b * span) & (row < (b + 1) * span)
            here = here & (column >= r * span) & (column < (r + 1) * span)
            allowed = allowed + jnp.where(here, seen.astype(jnp.int32), 0)
    return allowed


def fetch(sources, buffers, semaphores):
    copies = [
        pltpu.make_async_copy(source, buffer, semaphores.at[number])
        for number, (source, buffer) in enumerate(zip(sources, buffers))
    ]
    for copy in copies:
        copy.start()
    for copy in copies:
        copy.wait()


def columns(model):
    wide = -(-3 * WIDTH // 128) * 128
    return 0, wide, 2 * wide, 2 * wide + model


def pack_kernel(
    space_hbm, time_hbm, space_out_hbm, time_out_hbm, packed, half_ref,
    space_qkv, time_qkv, space_out, time_out, ready,
):
    fetch(
        (space_hbm, time_hbm, space_out_hbm, time_out_hbm),
        (space_qkv, time_qkv, space_out, time_out), ready,
    )
    outs = jnp.concatenate([space_out[...].astype(F32), time_out[...].astype(F32)], axis=0)
    parts = [space_qkv[...].astype(F32), time_qkv[...].astype(F32), outs]
    packed[...] = jnp.concatenate(parts, axis=1).astype(BF16)
    lanes = half_ref.shape[1]
    first = lax.axis_index("seq") == 0

    @pl.when(first)
    def _():
        half_ref[...] = packed[:, :lanes]

    @pl.when(jnp.logical_not(first))
    def _():
        half_ref[...] = packed[:, lanes:]


def send_kernel(cut, piece, by_tile, by_seq, over_tile, over_seq):
    at, lanes = 0, cut[1]
    if piece is not None:
        at = piece.shape[1]
        over_tile[:, :at] = piece[...]
        over_seq[:, :at] = piece[...]
    over_tile[:, at:] = by_seq[:, : cut[0]]
    over_seq[:, at:] = by_tile[:, cut[0] : lanes]


def place_columns(out_ref, row, full):
    rows = slice(row, row + full.shape[0])
    space, time, out, stop = columns(full.shape[1] - 6 * WIDTH)
    pad = jnp.zeros((full.shape[0], time - space - 3 * WIDTH), BF16)
    out_ref[rows, space : space + 3 * WIDTH] = full[:, : 3 * WIDTH].astype(BF16)
    out_ref[rows, space + 3 * WIDTH : time] = pad
    out_ref[rows, time : time + 3 * WIDTH] = full[:, 3 * WIDTH : 6 * WIDTH].astype(BF16)
    out_ref[rows, time + 3 * WIDTH : out] = pad
    out_ref[rows, out:stop] = full[:, 6 * WIDTH :].astype(BF16)


def join_kernel(owned, place, *refs):
    whole, parts, out_ref = refs[:owned], refs[owned:-1], refs[-1]
    top = 0
    if whole:
        rows = [ref[...].astype(F32) for ref in whole]
        place_columns(out_ref, 0, jnp.concatenate(rows, axis=0))
        top = sum(ref.shape[0] for ref in whole)
    if not parts:
        return
    near, by_tile, by_seq, corner_low, corner_high = parts
    lanes = near.shape[1]
    mine = [near[...].astype(F32), by_tile[:, :lanes].astype(F32)]
    mine = jnp.concatenate(mine, axis=0)
    low, high = corner_low.shape[1] % lanes, corner_high.shape[1] % lanes
    corner = [
        corner_low[:, corner_low.shape[1] - low :].astype(F32),
        corner_high[:, corner_high.shape[1] - high :].astype(F32),
    ]
    corner = jnp.concatenate(corner, axis=1)
    other = jnp.concatenate([by_seq[:, :lanes].astype(F32), corner], axis=0)

    @pl.when(place[1] == 0)
    def _():
        place_columns(out_ref, top, jnp.concatenate([mine, other], axis=1))

    @pl.when(place[1] != 0)
    def _():
        place_columns(out_ref, top, jnp.concatenate([other, mine], axis=1))


def order_kernel(index_ref, order_ref):
    order_ref[...] = expander(index_ref[0:1, :], order_ref.shape[0])


def normed_kernel(order_ref, before, x_ref, after, mod_ref, normed_ref):
    x = jnp.concatenate([before[...], x_ref[...], after[...]], axis=0).astype(F32)
    normed = (x * inverse_of(x) * (1.0 + mod_ref[0:1, :])).astype(BF16)
    normed_ref[...] = mm(normed, order_ref[...]).astype(BF16)


def early_kernel(slots, normed_ref, weight, partial_ref):
    partial_ref[...] = ahead(normed_ref, weight, 0, 3 * WIDTH, slots)


def forward_kernel(tiles, slots, late, place, pattern, normed_ref, *refs):
    *partial, weight, q_ref, kv_ref, att_ref = refs
    own = q_ref.shape[0]
    span = own // 2
    rows = ahead(
        normed_ref, [weight[n] for n in late], 0, 3 * WIDTH, [slots[n] for n in late]
    )
    for earlier in partial:
        rows = rows + earlier[...]
    rows = rows.astype(BF16)
    query, kv = rows[span : span + own, :WIDTH], rows[:, WIDTH:]
    keys, values = kv[:, :WIDTH], kv[:, WIDTH:]
    q_ref[...] = query
    kv_ref[...] = kv
    allowed = space_allowed(place, pattern, span, tiles)
    probs = softmax_of(spread(query), keys, allowed)
    att_ref[...] = collect(mm(probs.astype(BF16), values)).astype(BF16)


def middle_of(slots, index_ref, order_ref, x_ref, mod_ref, att, weight):
    _, time, out, stop = columns(x_ref.shape[1])
    att = mm(att, expander(index_ref[1:2, :])).astype(BF16)
    middle = x_ref[...].astype(F32) + ahead(att, weight, out, stop, slots)
    normed = (middle * inverse_of(middle) * (1.0 + mod_ref[1:2, :])).astype(BF16)
    normed = mm(normed, order_ref[...]).astype(BF16)
    return middle, ahead(normed, weight, time, time + 3 * WIDTH, slots).astype(BF16)


def middle_kernel(slots, index_ref, order_ref, x_ref, mod_ref, att_ref, weight, middle_ref, rows_ref):
    middle, rows = middle_of(slots, index_ref, order_ref, x_ref, mod_ref, att_ref[...], weight)
    middle_ref[...] = middle
    rows_ref[...] = rows


def att_grad_kernel(parts, row, index_ref, *refs):
    upstream = jnp.concatenate([ref[...] for ref in refs[:parts]], axis=0).astype(BF16)
    weight, grad_ref = refs[parts:]
    *_, out, stop = columns(upstream.shape[1])
    grad_ref[...] = behind(
        upstream, weight, out, stop, expander(index_ref[row : row + 1, :]), rounded=True
    )


def time_att_kernel(allowed_ref, rows_ref, grad_ref, out_ref):
    rows = rows_ref[...]
    query, keys, values = rows[:, :WIDTH], rows[:, WIDTH : 2 * WIDTH], rows[:, 2 * WIDTH :]
    spread_q = spread(query)
    probs = softmax_of(spread_q, keys, allowed_ref[...])
    att = collect(mm(probs.astype(BF16), values))
    grads = attention_back(spread_q, keys, values, probs, grad_ref[...])
    out_ref[...] = jnp.concatenate(grads + (att,), axis=1).astype(BF16)


def time_pair_kernel(
    slots, place, time_mask, index_ref, order_ref, mod_ref, x_ref, space_ref, own_ref, grad_ref,
    weight, out_ref, att_ref,
):
    count = own_ref.shape[0]
    first = place[1] == 0

    def frames(own, other):
        own, other = own.astype(F32), other.astype(F32)
        return jnp.where(first, own, other), jnp.where(first, other, own)

    _, other = middle_of(slots, index_ref, order_ref, x_ref, mod_ref, space_ref[...], weight)
    own = own_ref[...]
    row = lax.broadcasted_iota(jnp.int32, (WIDTH, 128), 0)
    low = lax.broadcasted_iota(jnp.int32, (WIDTH, 128), 1) * HEAD_DIM
    heads = jnp.where((row >= low) & (row < low + HEAD_DIM), 1.0, 0.0).astype(BF16)

    def summed(product):
        high = product.astype(BF16)
        return mm(high, heads) + mm((product - high.astype(F32)).astype(BF16), heads)

    def widened(value):
        return mm_nt(value.astype(BF16), heads)

    _, q1 = frames(own[:, :WIDTH], other[:, :WIDTH])
    k0, k1 = frames(own[:, WIDTH : 2 * WIDTH], other[:, WIDTH : 2 * WIDTH])
    v0, v1 = frames(own[:, 2 * WIDTH :], other[:, 2 * WIDTH :])
    g0, g1 = frames(grad_ref[:count, :], grad_ref[count:, :])
    s10 = jnp.where(time_mask[1, 0] == 1, summed(q1 * k0) * SCALE, MASKED)
    s11 = summed(q1 * k1) * SCALE
    top = jnp.maximum(s10, s11)
    e10, e11 = jnp.exp(s10 - top), jnp.exp(s11 - top)
    total = e10 + e11
    p10, p11 = e10 / total, e11 / total
    dp10, dp11 = summed(g1 * v0), summed(g1 * v1)
    delta = p10 * dp10 + p11 * dp11
    d10, d11 = widened(p10 * (dp10 - delta) * SCALE), widened(p11 * (dp11 - delta) * SCALE)
    w10, w11 = widened(p10), widened(p11)
    att1 = w10 * v0 + w11 * v1
    zero = jnp.zeros_like(q1)
    of_frame0 = (zero, d10 * q1, g0 + w10 * g1, v0)
    of_frame1 = (d10 * k0 + d11 * k1, d11 * q1, w11 * g1, att1)
    mine = [jnp.where(first, a, b) for a, b in zip(of_frame0, of_frame1)]
    out_ref[...] = jnp.concatenate(mine, axis=1).astype(BF16)
    theirs = jnp.where(first, att1, v0)
    att_ref[...] = jnp.concatenate([mine[3], theirs], axis=0).astype(BF16)


def term_kernel(parts, index_ref, att_ref, *refs):
    upstream = jnp.concatenate([ref[...] for ref in refs[:parts]], axis=0)
    mine_ref, theirs_ref = refs[parts:]
    att = mm(att_ref[...], expander(index_ref[...])).astype(BF16)
    half = mine_ref.shape[0]
    term = mm_tn(att, upstream).astype(BF16)
    mine_ref[...] = term[:half]
    theirs_ref[...] = term[half:]


def middle_back_kernel(
    order_ref, up_ref, mod_ref, middle_ref, rows_ref, weight, grad_ref
):
    middle = middle_ref[...]
    _, time, *_ = columns(middle.shape[1])
    back = behind(rows_ref[:, : 3 * WIDTH], weight, time, time + 3 * WIDTH, order_ref)
    gain = 1.0 + mod_ref[1:2, :]
    grad = up_ref[...].astype(F32) + norm_back(middle, gain, back)
    grad_ref[...] = grad


def result_kernel(slots, index_ref, middle_ref, rows_ref, weight, result_ref):
    att = mm(rows_ref[:, 3 * WIDTH :], expander(index_ref[2:3, :])).astype(BF16)
    *_, out, stop = columns(middle_ref.shape[1])
    grown = ahead(att, weight, out, stop, slots)
    result_ref[...] = (middle_ref[...] + grown).astype(BF16)


def space_back_kernel(
    tiles, place, pattern, q_ref, kv_ref, att_grad_ref, dq_ref, own_ref, low_ref, high_ref
):
    span = low_ref.shape[0]
    keys, values = kv_ref[:, :WIDTH], kv_ref[:, WIDTH:]
    allowed = space_allowed(place, pattern, span, tiles)
    spread_q = spread(q_ref[...])
    probs = softmax_of(spread_q, keys, allowed)
    dquery, dkeys, dvalues = attention_back(spread_q, keys, values, probs, att_grad_ref[...])
    dq_ref[...] = dquery.astype(BF16)
    both = jnp.concatenate([dkeys, dvalues], axis=1)
    low_ref[...] = both[:span].astype(BF16)
    own_ref[...] = both[span : 3 * span]
    high_ref[...] = both[3 * span :].astype(BF16)


def start_back_kernel(
    order_ref, x_ref, mod_ref, grad_ref, dq_ref, own_ref, left, right, weight, out_ref
):
    x = x_ref[...].astype(F32)
    rim = jnp.concatenate([left[...], right[...]], axis=0).astype(F32)
    dkv = own_ref[...] + rim
    grads = jnp.concatenate([dq_ref[...].astype(F32), dkv], axis=1).astype(BF16)
    back = behind(grads, weight, 0, 3 * WIDTH, order_ref)
    gain = 1.0 + mod_ref[0:1, :]
    out_ref[...] = (grad_ref[...] + norm_back(x, gain, back)).astype(BF16)


VMEM = pl.BlockSpec(memory_space=pltpu.VMEM)
SMEM = pl.BlockSpec(memory_space=pltpu.SMEM)


HBM = pl.BlockSpec(memory_space=pltpu.HBM)


def call(kernel, name, scalars, arrays, weight, outs, scratch=(), far=(), grant=VMEM_LIMIT):
    plain = len(scalars) + len(arrays) + len(far)
    weight, tree = jax.tree.flatten(list(weight))

    def body(*refs):
        fixed, pieces = refs[:plain], refs[plain : plain + len(weight)]
        pieces = (jax.tree.unflatten(tree, pieces),) if pieces else ()
        kernel(*fixed, *pieces, *refs[plain + len(weight) :])

    outs = [jax.ShapeDtypeStruct(shape, kind) for shape, kind in outs]
    near = [pltpu.VMEM(array.shape, array.dtype) for array in far]
    if far:
        near.append(pltpu.SemaphoreType.DMA((len(far),)))
    specs = [SMEM] * len(scalars) + [VMEM] * len(arrays) + [HBM] * len(far) + [VMEM] * len(weight)
    return pl.pallas_call(
        body,
        name=name,
        in_specs=specs,
        out_specs=[VMEM] * len(outs),
        out_shape=outs,
        scratch_shapes=near + list(scratch),
        compiler_params=pltpu.CompilerParams(vmem_limit_bytes=grant),
    )(*scalars, *arrays, *far, *weight)


def swapped(array, axis, bit):
    count = lax.axis_size(axis)
    return lax.ppermute(array, axis, [(i, i ^ bit) for i in range(count)])


def added(a, b):
    return (a.astype(F32) + b.astype(F32)).astype(BF16)


def relative_rows(shard, tile_at, clip_at, tiles, clips):
    block, inner = np.arange(clips * tiles * shard) // shard, np.arange(clips * tiles * shard) % shard
    low, apart, high = block // (2 * clips), block // 2 % clips, block % 2
    tile, clip = tile_at ^ (low + 2 * high), (clip_at + clips - apart) % clips
    return (clip * tiles + tile) * shard + inner


def local(
    latents,
    upstream,
    modulation,
    space_qkv,
    space_out,
    time_qkv,
    time_out,
    space_pattern,
    time_mask,
):
    seq, tiles, clips = lax.axis_size("seq"), lax.axis_size("tile"), lax.axis_size("dp")
    own, model = latents.shape[2], latents.shape[3]
    span, half = own // 2, own // 2
    shard = space_out.shape[0]
    x = latents.reshape(own, model)
    up = upstream.reshape(own, model)
    mod = modulation.reshape(modulation.shape[1:])
    tile_at, seq_at, clip_at = lax.axis_index("tile"), lax.axis_index("seq"), lax.axis_index("dp")
    side = seq_at if seq == 2 else jnp.zeros((), jnp.int32)
    place = jnp.stack([tile_at, side]).astype(jnp.int32)

    square = seq == 2 and tiles == 4
    hold = lax.optimization_barrier
    apart = range(1, clips)
    width = 6 * WIDTH + model
    own_w, half_w = call(
        pack_kernel, "pack", (), (), (),
        (((2 * shard, width), BF16), ((2 * shard, width // 2), BF16)),
        far=(space_qkv, time_qkv, space_out, time_out), grant=PACK_LIMIT,
    )
    if square:
        order = relative_rows(2 * shard, tile_at, clip_at, tiles, clips)
    else:
        order = jnp.arange(model)

    inner = order // (2 * shard) * shard + order % shard
    later = order % (2 * shard) >= shard
    space_rows = jnp.where((order >= 0) & ~later, inner, -1)
    time_rows = jnp.where((order >= 0) & later, inner, -1)
    index = jnp.stack([order, space_rows, time_rows]).astype(jnp.int32)
    near = np.arange(WIDTH) // shard
    bits = tiles.bit_length() - 1
    first = near // clips
    rel_tile = sum(((first >> b) & 1) << (bits - 1 - b) for b in range(bits))
    owner = (clip_at ^ (near % clips)) * tiles + (tile_at ^ rel_tile)
    terms = (owner * shard + np.arange(WIDTH) % shard).astype(jnp.int32).reshape(1, WIDTH)

    rise = [(i, i + 1) for i in range(tiles - 1)]
    fall = [(i + 1, i) for i in range(tiles - 1)]

    def rims(rows):
        before = lax.ppermute(rows[span:], "tile", rise)
        return before, lax.ppermute(rows[:span], "tile", fall)

    def joined(owned, pieces):
        rows = owned * 2 * shard + (4 * shard if len(pieces) > owned else 0)
        return call(
            functools.partial(join_kernel, owned), "join", (place,), pieces, (),
            (((rows, columns(model)[-1]), BF16),),
        )[0]

    (made,) = call(order_kernel, "order", (), (index,), (), (((model, model), BF16),))

    def normed_of(order, before, rows, after):
        return call(
            normed_kernel, "normed", (), (order, before, rows, after, mod), (),
            (((2 * own, model), BF16),),
        )[0]

    if square:
        lanes = width // 2
        cut = lanes // 256 * 128

        def onward(piece):
            return lax.ppermute(piece, "dp", [(i, (i + 1) % clips) for i in range(clips)])

        def sends(piece, by_tile, by_seq, owned=(), parts=()):
            arrays = [by_tile, by_seq] if piece is None else [piece, by_tile, by_seq]
            at, count, joins = (0 if piece is None else lanes), len(arrays), len(owned) + len(parts)

            def kernel(place_ref, *refs):
                sides, earlier, outs = refs[:count], refs[count : count + joins], refs[count + joins :]
                sides = sides if piece is not None else (None,) + sides
                send_kernel((cut, lanes), *sides, *outs[:2])
                if joins:
                    join_kernel(len(owned), place_ref, *earlier, outs[2])

            outs = [((2 * shard, at + cut), BF16), ((2 * shard, at + lanes - cut), BF16)]
            if joins:
                rows = len(owned) * 2 * shard + 4 * shard
                outs.append(((rows, columns(model)[-1]), BF16))
            over_tile, over_seq, *group = call(
                kernel, "send", (place,), (*arrays, *owned, *parts), (), outs
            )
            return group, (swapped(over_tile, "tile", 2), swapped(over_seq, "seq", 1))

        across = swapped(own_w, "tile", 2)
        piece, other_x, early = hold((onward(half_w), swapped(x, "seq", 1), x))
        pieces, came, groups, others = [piece], [], [], []
        for step in range(clips):
            piece = pieces[step] if step < clips - 1 else None
            following = onward(piece) if step < clips - 2 else ()
            if step == 0:
                moves = swapped(piece, "tile", 2), swapped(piece, "seq", 1)
                moves, across = hold((moves, across))
            else:
                owned = [own_w, across] if step == 2 else []
                parts = [pieces[step - 2], *came[step - 2], *came[step - 1]] if step > 1 else []
                group, moves = sends(piece, *came[-1], owned, parts)
                if group:
                    groups += group
                    others.append(swapped(groups[-1], "tile", 1))
            if step == 1:
                moves, made = hold((moves, made))
            if step == clips - 1:
                early, *_ = hold((early, came[-1]))
                before, after = rims(early)
            moves, following, others = hold((moves, following, others))
            came.append(moves)
            if step < clips - 2:
                pieces.append(following)
        order = made
        late_up, _ = hold((up, came[-1]))
        other_up = swapped(late_up, "seq", 1)
        last, before, after = hold(
            (joined(0, [pieces[-1], *came[-2], *came[-1]]), before, after)
        )
        groups.append(last)
        others.append(swapped(groups[-1], "tile", 1))
        normed = normed_of(order, before, x, after)
        weight = groups + others
        late = [len(groups) - 1, len(weight) - 1]
    else:
        before, after = rims(x)
        order = made
        normed = normed_of(order, before, x, after)
        weight = [lax.all_gather(joined(1, [own_w]), ("dp", "tile"), axis=0, tiled=True)]
        late = [0]
    ends = np.cumsum([0] + [part.shape[0] for part in weight]).tolist()
    slots = [(at, part.shape[0]) for at, part in zip(ends, weight)]
    first = [n for n in range(len(weight)) if n not in late]
    partial = ()
    if first:
        partial = tuple(call(
            functools.partial(early_kernel, [slots[n] for n in first]), "space_early", (),
            (normed,), [weight[n] for n in first], (((2 * own, 3 * WIDTH), F32),),
        ))

    query, window, att = call(
        functools.partial(forward_kernel, tiles, slots, late), "forward", (place, space_pattern),
        (normed,) + partial, weight,
        (((own, WIDTH), BF16), ((2 * own, 2 * WIDTH), BF16), ((own, WIDTH), BF16)),
    )
    middle, rows = call(
        functools.partial(middle_kernel, slots), "middle", (), (index, order, x, mod, att), weight,
        (((own, model), F32), ((own, 3 * WIDTH), BF16)),
    )
    if square:
        att, other_up = hold((att, other_up))
        ups = (up, other_up)
        other_att = swapped(att, "seq", 1)
    else:
        def turned(array):
            parts = array.reshape(seq, own // seq, array.shape[1])
            parts = lax.all_to_all(parts, "seq", split_axis=0, concat_axis=0, tiled=True)
            return parts.reshape(array.shape)

        ups = (turned(up),)
    (time_att_grad,) = call(
        functools.partial(att_grad_kernel, len(ups), 2), "att_grad", (), (index,) + ups, weight,
        (((len(ups) * own, WIDTH), BF16),),
    )
    if square:
        rows, att = call(
            functools.partial(time_pair_kernel, slots), "time_att", (place, time_mask),
            (index, order, mod, other_x, other_att, rows, time_att_grad), weight,
            (((own, 4 * WIDTH), BF16), ((2 * own, WIDTH), BF16)),
        )
    else:
        token = jnp.arange(own)
        frame, patch = token // (own // seq), token % (own // seq)
        seen = jnp.take(jnp.take(time_mask, frame, axis=0), frame, axis=1) == 1
        seen = (seen & (frame[None, :] < frame[:, None])) | (frame[None, :] == frame[:, None])
        allowed = (seen & (patch[None, :] == patch[:, None])).astype(jnp.int32)
        (rows,) = call(
            time_att_kernel, "time_att", (), (allowed, turned(rows), time_att_grad), (),
            (((own, 4 * WIDTH), BF16),),
        )
        att = rows[:, 3 * WIDTH :]
        rows = turned(rows)
    mine, theirs = call(
        functools.partial(term_kernel, len(ups)), "term", (), (terms, att) + ups, (),
        (((WIDTH // 2, model), BF16),) * 2,
    )

    (grad,) = call(
        middle_back_kernel, "middle_back", (), (order, up, mod, middle, rows), weight,
        (((own, model), F32),),
    )
    (att_grad,) = call(
        functools.partial(att_grad_kernel, 1, 1), "space_grad", (), (index, grad), weight,
        (((own, WIDTH), BF16),),
    )
    dq, own_grads, to_left, to_right = call(
        functools.partial(space_back_kernel, tiles), "space_back", (place, space_pattern),
        (query, window, att_grad), (),
        (
            ((own, WIDTH), BF16), ((own, 2 * WIDTH), F32),
            ((span, 2 * WIDTH), BF16), ((span, 2 * WIDTH), BF16),
        ),
    )
    from_left = lax.ppermute(to_right, "tile", rise)
    from_right = lax.ppermute(to_left, "tile", fall)
    (start_grad,) = call(
        start_back_kernel, "start_back", (),
        (order, x, mod, grad, dq, own_grads, from_left, from_right), weight,
        (((own, model), BF16),),
    )
    late, _ = hold((rows, start_grad))
    (result,) = call(
        functools.partial(result_kernel, slots), "result", (),
        (index, middle, late), weight, (((own, model), BF16),),
    )

    def ended(came, kernel):
        return hold((came, kernel))[0]

    ends, bit = [grad], 1
    while bit < tiles:
        came = ended(swapped(theirs, "tile", bit), ends.pop(0) if ends else dq)
        mine = added(mine, came)
        bit *= 2
        if bit < tiles:
            rows = mine.shape[0] // 2
            mine, theirs = mine[:rows], mine[rows:]
    came = [swapped(mine[by * shard : (by + 1) * shard], "dp", by) for by in apart]
    came = ended(came, result)
    total = mine[:shard].astype(F32)
    for part in came:
        total = total + part.astype(F32)
    if not square:
        total = lax.psum(total.astype(BF16), "seq").astype(F32)
    return (result.reshape(latents.shape), start_grad.reshape(latents.shape), total)


def solution(mesh):
    in_specs = (
        P("dp", "seq", "tile", None),
        P("dp", "seq", "tile", None),
        P("dp", None, None),
        P(("dp", "tile"), None),
        P(("dp", "tile"), None),
        P(("dp", "tile"), None),
        P(("dp", "tile"), None),
        P("tile", None),
        P(),
    )
    out_specs = (
        P("dp", "seq", "tile", None),
        P("dp", "seq", "tile", None),
        P(("dp", "tile"), None),
    )
    return jax.shard_map(local, mesh=mesh, in_specs=in_specs, out_specs=out_specs, check_vma=False)
```

time: 389 us -> 119 us (0.31); the launches traced: 384 us -> 119 us
  waiting for transfers between devices: 151 us -> 45 us
  matrix products: 66.8 us -> 0 us
  local copies, waits for them, and re-layouts: 59.6 us -> 0.19 us
  blocking collectives: 40.7 us -> 0 us
  Pallas kernels: 0 us -> 36 us
  other arithmetic: 19.9 us -> 1.12 us
  between operations: 14.9 us -> 1.02 us
  starting transfers between devices: 30.8 us -> 35.8 us
    all_gather x4 -> x0, waiting for transfers between devices: 149 us -> none  [the longest x1 49.2 us: local(): lax.all_gather(space_qkv, ('dp', 'tile'), axis=0, tiled=True)]
    dot_general x19 -> x0, matrix products: 59.2 us -> none  [the longest x2 12.2 us: attend_back(): jnp.einsum('cbhqk,' + qform + '->' + kform, dscore, query, preferred_elem...]
    ppermute x4 -> x27, waiting for transfers between devices: 0.01 us -> 45 us  [the longest x20 44.8 us: swapped(): return lax.ppermute(array, axis, [(i, i ^ bit) for i in range(count)])]
    unnamed x1 -> x0, blocking collectives: 40.7 us -> none
    pallas_call x0 -> x18, Pallas kernels: none -> 36 us  [call(): pl.pallas_call(body, name=name, in_specs=specs, out_specs=[VMEM] * len(ou...]
    ppermute x4 -> x27, starting transfers between devices: 7.58 us -> 35.8 us  [the longest x20 24.1 us: swapped(): return lax.ppermute(array, axis, [(i, i ^ bit) for i in range(count)])]
    unnamed x56 -> x24, local copies, waits for them, and re-layouts: 23.3 us -> 0.07 us
    all_to_all x4 -> x0, starting transfers between devices: 16.9 us -> none  [the longest x1 4.41 us: local(): lax.all_to_all(time_local, 'seq', split_axis=2, concat_axis=1, tiled=True)]
  transfers between devices with their start and end apart: 17 -> 27, of which waited for: 5 -> 13; matrix products, arithmetic and copies ran while one was open for 39% -> 0% of each run, Pallas kernels for 0% -> 20%
where the time goes in v1:
time: 119 us
  waiting for transfers between devices  45 us (38%)
  Pallas kernels  36 us (30%)
  starting transfers between devices  35.8 us (30%)
    ppermute x20, waiting for transfers between devices, swapped(): return lax.ppermute(array, axis, [(i, i ^ bit) for i in range(count)])  44.8 us
    pallas_call x18, Pallas kernels, call(): pl.pallas_call(body, name=name, in_specs=specs, out_specs=[VMEM] * len(ou...  36 us
    ppermute x20, starting transfers between devices, swapped(): return lax.ppermute(array, axis, [(i, i ^ bit) for i in range(count)])  24.1 us
    ppermute x3, starting transfers between devices, onward(): lax.ppermute(piece, 'dp', [(i, (i + 1) % clips) for i in range(clips)])  5.13 us
  transfers between devices with their start and end apart: 27, of which 13 were waited for; matrix products, arithmetic and copies ran while one was open for 0% of the time, Pallas kernels for 20%

profile of v1, /device:TPU:0, one launch (start us, length us, event | category | flops | bytes accessed | tf_op | source)
XLA Modules:
  0.0 119.2 jit_solution(15598716312139619225)
XLA Ops:
  0.7 2.4 %pack.1 = (bf16[72,4608]{1,0:T(8,128)(2,1)}, bf16[72,2304]{1,0:T(8,128)(2,1)}) custom-call(bf16[72,1728]{1,0:T(8,128)(2,1)} %refs_0_.1, bf16[72,1728]{1,0:T(8,128)(2,1)} %refs_1_.4, bf16[36,1152]{1,0:T(8,128)(2,1)} %refs_2_.1, bf16[36,1152]{1,0:T(8,128)(2,1)} %refs_3_.1), custom_call_target="tpu_custom_call" | custom-call | tf_op jit(solution)/shard_map/pack/pallas_call | solution.py:410
  3.1 3.1 %collective-permute-start = (bf16[72,2304]{1,0:T(8,128)(2,1)}, bf16[72,2304]{1,0:T(8,128)(2,1)S(1)}, u32[]{:S(2)}, u32[]{:S(2)}) collective-permute-start(bf16[72,2304]{1,0:T(8,128)(2,1)} %get-tuple-element.61), channel_id=1, source_target_pairs={{0,8},{8,16},{16,24},{24,0},{1,9},{9,17},{17,25},{25,1},{2,10},{10... | collective-permute-start | bytes 995336 | tf_op jit(solution)/shard_map/ppermute | solution.py:512
  6.1 1.5 %collective-permute-start.4 = (bf16[72,4608]{1,0:T(8,128)(2,1)}, bf16[72,4608]{1,0:T(8,128)(2,1)S(1)}, u32[]{:S(2)}, u32[]{:S(2)}) collective-permute-start(bf16[72,4608]{1,0:T(8,128)(2,1)} %get-tuple-element.63.refs_4_), channel_id=1, source_target_pairs={{0,2},{1,3},{2,0},{3,1},{4,6},{5,7},{6,4},{7,5},{8,10},{9,11},{10,... | collective-permute-start | bytes 1990664 | tf_op jit(solution)/shard_map/ppermute | solution.py:423
  7.6 1.5 %collective-permute-start.1 = (bf16[128,1152]{1,0:T(8,128)(2,1)}, bf16[128,1152]{1,0:T(8,128)(2,1)S(1)}, u32[]{:S(2)}, u32[]{:S(2)}) collective-permute-start(bf16[128,1152]{1,0:T(8,128)(2,1)} %bitcast.7), channel_id=1, source_target_pairs={{0,4},{4,0},{1,5},{5,1},{2,6},{6,2},{3,7},{7,3},{8,12},{12,8},{9,1... | collective-permute-start | bytes 884744 | tf_op jit(solution)/shard_map/ppermute | solution.py:423
  9.1 6.9 %collective-permute-done.1.refs_5_ = bf16[128,1152]{1,0:T(8,128)(2,1)S(1)} collective-permute-done((bf16[128,1152]{1,0:T(8,128)(2,1)}, bf16[128,1152]{1,0:T(8,128)(2,1)S(1)}, u32[]{:S(2)}, u32[]{:S(2)}) %collective-permute-start.1) | collective-permute-done | bytes 294944 | tf_op jit(solution)/shard_map/ppermute | solution.py:423
  16.2 1.5 %collective-permute-start.2 = (bf16[72,2304]{1,0:T(8,128)(2,1)S(1)}, bf16[72,2304]{1,0:T(8,128)(2,1)S(1)}, u32[]{:S(2)}, u32[]{:S(2)}) collective-permute-start(bf16[72,2304]{1,0:T(8,128)(2,1)S(1)} %collective-permute-done.refs_6_), channel_id=1, source_target_pairs={{0,2},{1,3},{2,0},{3,1},{4,6},{5,7},{6,4},{7,5},{8,10},{9,11},{10,... | collective-permute-start | bytes 995336 | tf_op jit(solution)/shard_map/ppermute | solution.py:423
  17.7 1.5 %collective-permute-start.3 = (bf16[72,2304]{1,0:T(8,128)(2,1)S(1)}, bf16[72,2304]{1,0:T(8,128)(2,1)S(1)}, u32[]{:S(2)}, u32[]{:S(2)}) collective-permute-start(bf16[72,2304]{1,0:T(8,128)(2,1)S(1)} %collective-permute-done.refs_6_), channel_id=1, source_target_pairs={{0,4},{4,0},{1,5},{5,1},{2,6},{6,2},{3,7},{7,3},{8,12},{12,8},{9,1... | collective-permute-start | bytes 995336 | tf_op jit(solution)/shard_map/ppermute | solution.py:423
  19.7 10.1 %collective-permute-done.2.refs_2_.refs_7_ = bf16[72,2304]{1,0:T(8,128)(2,1)S(1)} collective-permute-done((bf16[72,2304]{1,0:T(8,128)(2,1)S(1)}, bf16[72,2304]{1,0:T(8,128)(2,1)S(1)}, u32[]{:S(2)}, u32[]{:S(2)}) %collective-permute-start.2) | collective-permute-done | bytes 331808 | tf_op jit(solution)/shard_map/ppermute | solution.py:423
  29.8 1.5 %send.3 = (bf16[72,3456]{1,0:T(8,128)(2,1)}, bf16[72,3456]{1,0:T(8,128)(2,1)}) custom-call(s32[2]{0:T(128)S(1)} %pad_add_fusion.1.refs_0_, bf16[72,2304]{1,0:T(8,128)(2,1)S(1)} %collective-permute-done.5.refs_1_.refs_3_, bf16[72,2304]{1,0:T(8,128)(2,1)S(1)} %collective-permute-done.2.refs_2_.refs_7_, bf16[72,2304]{1,0:T(8,128)(2,1)S(1)} %collective-permute-done.3.refs_3_.refs_8_), custom_call_target="tpu_custom_call" | custom-call | tf_op jit(solution)/shard_map/send/pallas_call | solution.py:410
  31.4 1.5 %collective-permute-start.6 = (bf16[72,3456]{1,0:T(8,128)(2,1)}, bf16[72,3456]{1,0:T(8,128)(2,1)S(1)}, u32[]{:S(2)}, u32[]{:S(2)}) collective-permute-start(bf16[72,3456]{1,0:T(8,128)(2,1)} %get-tuple-element.69), channel_id=1, source_target_pairs={{0,2},{1,3},{2,0},{3,1},{4,6},{5,7},{6,4},{7,5},{8,10},{9,11},{10,... | collective-permute-start | bytes 1493000 | tf_op jit(solution)/shard_map/ppermute | solution.py:423
  32.9 1.5 %collective-permute-start.7 = (bf16[72,3456]{1,0:T(8,128)(2,1)}, bf16[72,3456]{1,0:T(8,128)(2,1)S(1)}, u32[]{:S(2)}, u32[]{:S(2)}) collective-permute-start(bf16[72,3456]{1,0:T(8,128)(2,1)} %get-tuple-element.70), channel_id=1, source_target_pairs={{0,4},{4,0},{1,5},{5,1},{2,6},{6,2},{3,7},{7,3},{8,12},{12,8},{9,1... | collective-permute-start | bytes 1493000 | tf_op jit(solution)/shard_map/ppermute | solution.py:423
  34.4 1.6 %collective-permute-start.8 = (bf16[72,2304]{1,0:T(8,128)(2,1)S(1)}, bf16[72,2304]{1,0:T(8,128)(2,1)S(1)}, u32[]{:S(2)}, u32[]{:S(2)}) collective-permute-start(bf16[72,2304]{1,0:T(8,128)(2,1)S(1)} %collective-permute-done.5.refs_1_.refs_3_), channel_id=1, source_target_pairs={{0,8},{8,16},{16,24},{24,0},{1,9},{9,17},{17,25},{25,1},{2,10},{10... | collective-permute-start | bytes 995336 | tf_op jit(solution)/shard_map/ppermute | solution.py:512
  36.6 6.9 %collective-permute-done.6.refs_2_.refs_9_.refs_4_ = bf16[72,3456]{1,0:T(8,128)(2,1)S(1)} collective-permute-done((bf16[72,3456]{1,0:T(8,128)(2,1)}, bf16[72,3456]{1,0:T(8,128)(2,1)S(1)}, u32[]{:S(2)}, u32[]{:S(2)}) %collective-permute-start.6) | collective-permute-done | bytes 497696 | tf_op jit(solution)/shard_map/ppermute | solution.py:423
  43.5 1.2 %collective-permute-done.7.refs_3_.refs_10_.refs_5_ = bf16[72,3456]{1,0:T(8,128)(2,1)S(1)} collective-permute-done((bf16[72,3456]{1,0:T(8,128)(2,1)}, bf16[72,3456]{1,0:T(8,128)(2,1)S(1)}, u32[]{:S(2)}, u32[]{:S(2)}) %collective-permute-start.7) | collective-permute-done | bytes 497696 | tf_op jit(solution)/shard_map/ppermute | solution.py:423
  44.7 1.1 send.4
  45.9 0.6 collective-permute-start.9
  46.5 1.5 %collective-permute-start.10 = (bf16[72,3456]{1,0:T(8,128)(2,1)S(1)}, bf16[72,3456]{1,0:T(8,128)(2,1)S(1)}, u32[]{:S(2)}, u32[]{:S(2)}) collective-permute-start(bf16[72,3456]{1,0:T(8,128)(2,1)S(1)} %get-tuple-element.79), channel_id=1, source_target_pairs={{0,4},{4,0},{1,5},{5,1},{2,6},{6,2},{3,7},{7,3},{8,12},{12,8},{9,1... | collective-permute-start | bytes 1493000 | tf_op jit(solution)/shard_map/ppermute | solution.py:423
  48.0 11.7 %collective-permute-done.9.refs_1_.refs_6_.refs_2_ = bf16[72,3456]{1,0:T(8,128)(2,1)S(1)} collective-permute-done((bf16[72,3456]{1,0:T(8,128)(2,1)S(1)}, bf16[72,3456]{1,0:T(8,128)(2,1)S(1)}, u32[]{:S(2)}, u32[]{:S(2)}) %collective-permute-start.9) | collective-permute-done | bytes 497696 | tf_op jit(solution)/shard_map/ppermute | solution.py:423
  60.0 0.9 send.5
  60.9 1.6 %collective-permute-start.12 = (bf16[72,1152]{1,0:T(8,128)(2,1)S(1)}, bf16[72,1152]{1,0:T(8,128)(2,1)S(1)}, u32[]{:S(2)}, u32[]{:S(2)}) collective-permute-start(bf16[72,1152]{1,0:T(8,128)(2,1)S(1)} %get-tuple-element.83), channel_id=1, source_target_pairs={{0,2},{1,3},{2,0},{3,1},{4,6},{5,7},{6,4},{7,5},{8,10},{9,11},{10,... | collective-permute-start | bytes 497672 | tf_op jit(solution)/shard_map/ppermute | solution.py:423
  62.5 1.5 %collective-permute-start.13 = (bf16[72,1152]{1,0:T(8,128)(2,1)S(1)}, bf16[72,1152]{1,0:T(8,128)(2,1)S(1)}, u32[]{:S(2)}, u32[]{:S(2)}) collective-permute-start(bf16[72,1152]{1,0:T(8,128)(2,1)S(1)} %get-tuple-element.84), channel_id=1, source_target_pairs={{0,4},{4,0},{1,5},{5,1},{2,6},{6,2},{3,7},{7,3},{8,12},{12,8},{9,1... | collective-permute-start | bytes 497672 | tf_op jit(solution)/shard_map/ppermute | solution.py:423
  64.0 1.8 %collective-permute-start.15 = (bf16[64,1152]{1,0:T(8,128)(2,1)S(1)}, bf16[64,1152]{1,0:T(8,128)(2,1)S(1)}, u32[]{:S(2)}, u32[]{:S(2)}) collective-permute-start(bf16[64,1152]{1,0:T(8,128)(2,1)S(1)} %get-tuple-element.123), channel_id=1, source_target_pairs={{0,1},{1,2},{2,3},{4,5},{5,6},{6,7},{8,9},{9,10},{10,11},{12,13},{... | collective-permute-start | bytes 442376 | tf_op jit(solution)/shard_map/ppermute | solution.py:489
  65.8 1.4 %collective-permute-start.16 = (bf16[64,1152]{1,0:T(8,128)(2,1)S(1)}, bf16[64,1152]{1,0:T(8,128)(2,1)S(1)}, u32[]{:S(2)}, u32[]{:S(2)}) collective-permute-start(bf16[64,1152]{1,0:T(8,128)(2,1)S(1)} %get-tuple-element.122), channel_id=1, source_target_pairs={{1,0},{2,1},{3,2},{5,4},{6,5},{7,6},{9,8},{10,9},{11,10},{13,12},{... | collective-permute-start | bytes 442376 | tf_op jit(solution)/shard_map/ppermute | solution.py:490
  67.6 1.2 %collective-permute-done.13.refs_5_ = bf16[72,1152]{1,0:T(8,128)(2,1)S(1)} collective-permute-done((bf16[72,1152]{1,0:T(8,128)(2,1)S(1)}, bf16[72,1152]{1,0:T(8,128)(2,1)S(1)}, u32[]{:S(2)}, u32[]{:S(2)}) %collective-permute-start.13) | collective-permute-done | bytes 165920 | tf_op jit(solution)/shard_map/ppermute | solution.py:423
  68.8 1.1 join.1.refs_6_.refs_7_.refs_5_.refs_11_.refs_4_.refs_10_
  69.9 3.3 %collective-permute-start.17 = (bf16[144,4736]{1,0:T(8,128)(2,1)S(1)}, bf16[144,4736]{1,0:T(8,128)(2,1)S(1)}, u32[]{:S(2)}, u32[]{:S(2)}) collective-permute-start(bf16[144,4736]{1,0:T(8,128)(2,1)S(1)} %join.1.refs_6_.refs_7_.refs_5_.refs_11_.refs_4_.refs_10_), channel_id=1, source_target_pairs={{0,1},{1,0},{2,3},{3,2},{4,5},{5,4},{6,7},{7,6},{8,9},{9,8},{10,11... | collective-permute-start | bytes 4091912 | tf_op jit(solution)/shard_map/ppermute | solution.py:423
  73.7 1.1 normed.1.refs_0_.refs_2_
  74.9 1.6 %space_early.1.refs_3_ = f32[256,1728]{1,0:T(8,128)S(1)} custom-call(bf16[256,1152]{1,0:T(8,128)(2,1)S(1)} %normed.1.refs_0_.refs_2_, bf16[288,4736]{1,0:T(8,128)(2,1)S(1)} %get-tuple-element.80.refs_1_.refs_4_.refs_5_.refs_3_.refs_9_.refs_2_.refs_8_, bf16[144,4736]{1,0:T(8,128)(2,1)S(1)} %get-tuple-element.86.refs_2_.refs_5_.refs_6_.refs_4_.refs_10_.refs_3_.refs_9_, ...), custom_call_target="tpu_custom_call" | custom-call | tf_op jit(solution)/shard_map/space_early/pallas_call | solution.py:410
  76.6 3.2 %forward.1 = (bf16[128,576]{1,0:T(8,128)(2,1)S(1)}, bf16[256,1152]{1,0:T(8,128)(2,1)S(1)}, bf16[128,576]{1,0:T(8,128)(2,1)S(1)}) custom-call(s32[2]{0:T(128)S(1)} %pad_add_fusion.1.refs_0_, s32[2,4]{1,0:T(2,128)S(1)} %copy-done.4, bf16[256,1152]{1,0:T(8,128)(2,1)S(1)} %normed.1.refs_0_.refs_2_, f32[256,1728]{1,0:T(8,128)S(1)} %space_early.1.refs_3_, ...), custom_call_target="tpu_custom_call" | custom-call | tf_op jit(solution)/shard_map/forward/pallas_call | solution.py:410
  79.8 2.3 %collective-permute-done.18.refs_2_.refs_3_ = bf16[128,1152]{1,0:T(8,128)(2,1)S(1)} collective-permute-done((bf16[128,1152]{1,0:T(8,128)(2,1)S(1)}, bf16[128,1152]{1,0:T(8,128)(2,1)S(1)}, u32[]{:S(2)}, u32[]{:S(2)}) %collective-permute-start.18) | collective-permute-done | bytes 294944 | tf_op jit(solution)/shard_map/ppermute | solution.py:423
  82.7 2.9 %middle.1 = (f32[128,1152]{1,0:T(8,128)S(1)}, bf16[128,1728]{1,0:T(8,128)(2,1)S(1)}) custom-call(s32[3,1152]{1,0:T(4,128)S(1)} %pad_add_fusion.refs_0_.refs_2_, bf16[1152,1152]{1,0:T(8,128)(2,1)S(1)} %order.1.refs_0_.refs_1_.refs_3_, bf16[128,1152]{1,0:T(8,128)(2,1)S(1)} %bitcast.10, f32[2,1152]{1,0:T(2,128)S(1)} %bitcast.17, ...), custom_call_target="tpu_custom_call" | custom-call | tf_op jit(solution)/shard_map/middle/pallas_call | solution.py:410
  85.6 1.6 %att_grad.1.refs_8_ = bf16[256,576]{1,0:T(8,128)(2,1)S(1)} custom-call(s32[3,1152]{1,0:T(4,128)S(1)} %pad_add_fusion.refs_0_.refs_2_, bf16[128,1152]{1,0:T(8,128)(2,1)S(1)} %bitcast.13, bf16[128,1152]{1,0:T(8,128)(2,1)S(1)} %collective-permute-done.18.refs_2_.refs_3_, ...), custom_call_target="tpu_custom_call" | custom-call | tf_op jit(solution)/shard_map/att_grad/pallas_call | solution.py:410
  87.4 4.7 %time_att.1 = (bf16[128,2304]{1,0:T(8,128)(2,1)S(1)}, bf16[256,576]{1,0:T(8,128)(2,1)S(1)}) custom-call(s32[2]{0:T(128)S(1)} %pad_add_fusion.1.refs_0_, s32[2,2]{1,0:T(2,128)S(1)} %copy-done.5, s32[3,1152]{1,0:T(4,128)S(1)} %pad_add_fusion.refs_0_.refs_2_, bf16[1152,1152]{1,0:T(8,128)(2,1)S(1)} %order.1.refs_0_.refs_1_.refs_3_, f32[2,1152]{1,0:T(2,128)S(1)} %bitcast.18, ...), custom_call_target="tpu_custom_call" | custom-call | tf_op jit(solution)/shard_map/time_att/pallas_call | solution.py:410
  92.1 1.3 %term.1 = (bf16[288,1152]{1,0:T(8,128)(2,1)S(1)}, bf16[288,1152]{1,0:T(8,128)(2,1)S(1)}) custom-call(s32[1,576]{1,0:T(1,128)S(1)} %reshape.29.refs_0_, bf16[256,576]{1,0:T(8,128)(2,1)S(1)} %get-tuple-element.111.refs_1_, bf16[128,1152]{1,0:T(8,128)(2,1)S(1)} %bitcast.14, bf16[128,1152]{1,0:T(8,128)(2,1)S(1)} %collective-permute-done.18.refs_2_.refs_3_), custom_call_target="tpu_custom_call" | custom-call | tf_op jit(solution)/shard_map/term/pallas_call | solution.py:410
  93.5 2.5 %middle_back.1.refs_1_.refs_3_ = f32[128,1152]{1,0:T(8,128)S(1)} custom-call(bf16[1152,1152]{1,0:T(8,128)(2,1)S(1)} %order.1.refs_0_.refs_1_.refs_3_, bf16[128,1152]{1,0:T(8,128)(2,1)S(1)} %bitcast.15, f32[2,1152]{1,0:T(2,128)S(1)} %bitcast.19, f32[128,1152]{1,0:T(8,128)S(1)} %get-tuple-element.97.refs_3_.refs_1_, ...), custom_call_target="tpu_custom_call" | custom-call | tf_op jit(solution)/shard_map/middle_back/pallas_call | solution.py:410
  96.2 0.8 collective-permute-start.23
  97.0 1.4 %space_grad.1.refs_4_ = bf16[128,576]{1,0:T(8,128)(2,1)S(1)} custom-call(s32[3,1152]{1,0:T(4,128)S(1)} %pad_add_fusion.refs_0_.refs_2_, f32[128,1152]{1,0:T(8,128)S(1)} %middle_back.1.refs_1_.refs_3_, bf16[288,4736]{1,0:T(8,128)(2,1)S(1)} %get-tuple-element.80.refs_1_.refs_4_.refs_5_.refs_3_.refs_9_.refs_2_.refs_8_, ...), custom_call_target="tpu_custom_call" | custom-call | tf_op jit(solution)/shard_map/space_grad/pallas_call | solution.py:410
  98.4 3.1 %space_back.1 = (bf16[128,576]{1,0:T(8,128)(2,1)S(1)}, f32[128,1152]{1,0:T(8,128)S(1)}, bf16[64,1152]{1,0:T(8,128)(2,1)S(1)}, bf16[64,1152]{1,0:T(8,128)(2,1)S(1)}) custom-call(s32[2]{0:T(128)S(1)} %pad_add_fusion.1.refs_0_, s32[2,4]{1,0:T(2,128)S(1)} %copy-done.4, bf16[128,576]{1,0:T(8,128)(2,1)S(1)} %get-tuple-element.104.refs_2_, ...), custom_call_target="tpu_custom_call" | custom-call | tf_op jit(solution)/shard_map/space_back/pallas_call | solution.py:410
  101.6 2.1 %collective-permute-start.20 = (bf16[64,1152]{1,0:T(8,128)(2,1)S(1)}, bf16[64,1152]{1,0:T(8,128)(2,1)S(1)}, u32[]{:S(2)}, u32[]{:S(2)}) collective-permute-start(bf16[64,1152]{1,0:T(8,128)(2,1)S(1)} %get-tuple-element.108), channel_id=1, source_target_pairs={{0,1},{1,2},{2,3},{4,5},{5,6},{6,7},{8,9},{9,10},{10,11},{12,13},{... | collective-permute-start | bytes 442376 | tf_op jit(solution)/shard_map/ppermute | solution.py:649
  103.7 1.3 %collective-permute-start.21 = (bf16[64,1152]{1,0:T(8,128)(2,1)S(1)}, bf16[64,1152]{1,0:T(8,128)(2,1)S(1)}, u32[]{:S(2)}, u32[]{:S(2)}) collective-permute-start(bf16[64,1152]{1,0:T(8,128)(2,1)S(1)} %get-tuple-element.109), channel_id=1, source_target_pairs={{1,0},{2,1},{3,2},{5,4},{6,5},{7,6},{9,8},{10,9},{11,10},{13,12},{... | collective-permute-start | bytes 442376 | tf_op jit(solution)/shard_map/ppermute | solution.py:650
  105.0 1.4 %collective-permute-done.23 = bf16[144,1152]{1,0:T(8,128)(2,1)S(1)} collective-permute-done((bf16[144,1152]{1,0:T(8,128)(2,1)S(1)}, bf16[144,1152]{1,0:T(8,128)(2,1)S(1)}, u32[]{:S(2)}, u32[]{:S(2)}) %collective-permute-start.23) | collective-permute-done | bytes 331808 | tf_op jit(solution)/shard_map/ppermute | solution.py:423
  106.6 1.7 %collective-permute-start.24 = (bf16[36,1152]{1,0:T(8,128)(2,1)S(1)}, bf16[36,1152]{1,0:T(8,128)(2,1)S(1)}, u32[]{:S(2)}, u32[]{:S(2)}) collective-permute-start(bf16[36,1152]{1,0:T(8,128)(2,1)S(1)} %get-tuple-element.121), channel_id=1, source_target_pairs={{0,8},{8,0},{16,24},{24,16},{1,9},{9,1},{17,25},{25,17},{2,10},{10... | collective-permute-start | bytes 248840 | tf_op jit(solution)/shard_map/ppermute | solution.py:423
  108.2 1.5 %collective-permute-start.25 = (bf16[36,1152]{1,0:T(8,128)(2,1)S(1)}, bf16[36,1152]{1,0:T(8,128)(2,1)S(1)}, u32[]{:S(2)}, u32[]{:S(2)}) collective-permute-start(bf16[36,1152]{1,0:T(8,128)(2,1)S(1)} %get-tuple-element.120), channel_id=1, source_target_pairs={{0,16},{8,24},{16,0},{24,8},{1,17},{9,25},{17,1},{25,9},{2,18},{10... | collective-permute-start | bytes 248840 | tf_op jit(solution)/shard_map/ppermute | solution.py:423
  109.8 1.3 %collective-permute-start.26 = (bf16[36,1152]{1,0:T(8,128)(2,1)S(1)}, bf16[36,1152]{1,0:T(8,128)(2,1)S(1)}, u32[]{:S(2)}, u32[]{:S(2)}) collective-permute-start(bf16[36,1152]{1,0:T(8,128)(2,1)S(1)} %get-tuple-element.119), channel_id=1, source_target_pairs={{0,24},{8,16},{16,8},{24,0},{1,25},{9,17},{17,9},{25,1},{2,26},{10... | collective-permute-start | bytes 248840 | tf_op jit(solution)/shard_map/ppermute | solution.py:423
  111.1 3.2 %start_back.1 = bf16[128,1152]{1,0:T(8,128)(2,1)} custom-call(bf16[1152,1152]{1,0:T(8,128)(2,1)S(1)} %order.1.refs_0_.refs_1_.refs_3_, bf16[128,1152]{1,0:T(8,128)(2,1)S(1)} %bitcast.11, f32[2,1152]{1,0:T(2,128)S(1)} %bitcast.20, f32[128,1152]{1,0:T(8,128)S(1)} %middle_back.1.refs_1_.refs_3_, bf16[128,576]{1,0:T(8,128)(2,1)S(1)} %get-tuple-element.106.refs_4_, ...), custom_call_target="tpu_custom_call" | custom-call | tf_op jit(solution)/shard_map/start_back/pallas_call | solution.py:410
  114.2 1.9 %result.1 = bf16[128,1152]{1,0:T(8,128)(2,1)} custom-call(s32[3,1152]{1,0:T(4,128)S(1)} %pad_add_fusion.refs_0_.refs_2_, f32[128,1152]{1,0:T(8,128)S(1)} %get-tuple-element.97.refs_3_.refs_1_, bf16[128,2304]{1,0:T(8,128)(2,1)S(1)} %get-tuple-element.110.refs_4_.refs_2_, ...), custom_call_target="tpu_custom_call" | custom-call | tf_op jit(solution)/shard_map/result/pallas_call | solution.py:410
  116.1 2.3 %collective-permute-done.25 = bf16[36,1152]{1,0:T(8,128)(2,1)S(1)} collective-permute-done((bf16[36,1152]{1,0:T(8,128)(2,1)S(1)}, bf16[36,1152]{1,0:T(8,128)(2,1)S(1)}, u32[]{:S(2)}, u32[]{:S(2)}) %collective-permute-start.25) | collective-permute-done | bytes 82976 | tf_op jit(solution)/shard_map/ppermute | solution.py:423
  118.4 0.7 convert_add_fusion
  (62 shorter events, 3.8 us)
Async XLA Ops:
  0.6 35.3 %copy-start.6 = (s32[1152]{0:T(1024)S(1)}, s32[1152]{0:T(1024)}, u32[]{:S(2)}) copy-start(s32[1152]{0:T(1024)} %constant.72.clone) | copy-start | bytes 13828
  0.6 35.3 %copy-start.7 = (s32[1152]{0:T(1024)S(1)}, s32[1152]{0:T(1024)}, u32[]{:S(2)}) copy-start(s32[1152]{0:T(1024)} %constant.70.clone) | copy-start | bytes 13828
  0.7 35.3 %copy-start.8 = (s32[1152]{0:T(1024)S(1)}, s32[1152]{0:T(1024)}, u32[]{:S(2)}) copy-start(s32[1152]{0:T(1024)} %constant.84) | copy-start | bytes 13828
  3.1 13.1 %collective-permute-start = (bf16[72,2304]{1,0:T(8,128)(2,1)}, bf16[72,2304]{1,0:T(8,128)(2,1)S(1)}, u32[]{:S(2)}, u32[]{:S(2)}) collective-permute-start(bf16[72,2304]{1,0:T(8,128)(2,1)} %get-tuple-element.61), channel_id=1, source_target_pairs={{0,8},{8,16},{16,24},{24,0},{1,9},{9,17},{17,25},{25,1},{2,10},{10... | collective-permute-start | bytes 995336 | tf_op jit(solution)/shard_map/ppermute | solution.py:512
  6.1 23.7 %collective-permute-start.4 = (bf16[72,4608]{1,0:T(8,128)(2,1)}, bf16[72,4608]{1,0:T(8,128)(2,1)S(1)}, u32[]{:S(2)}, u32[]{:S(2)}) collective-permute-start(bf16[72,4608]{1,0:T(8,128)(2,1)} %get-tuple-element.63.refs_4_), channel_id=1, source_target_pairs={{0,2},{1,3},{2,0},{3,1},{4,6},{5,7},{6,4},{7,5},{8,10},{9,11},{10,... | collective-permute-start | bytes 1990664 | tf_op jit(solution)/shard_map/ppermute | solution.py:423
  7.6 8.4 %collective-permute-start.1 = (bf16[128,1152]{1,0:T(8,128)(2,1)}, bf16[128,1152]{1,0:T(8,128)(2,1)S(1)}, u32[]{:S(2)}, u32[]{:S(2)}) collective-permute-start(bf16[128,1152]{1,0:T(8,128)(2,1)} %bitcast.7), channel_id=1, source_target_pairs={{0,4},{4,0},{1,5},{5,1},{2,6},{6,2},{3,7},{7,3},{8,12},{12,8},{9,1... | collective-permute-start | bytes 884744 | tf_op jit(solution)/shard_map/ppermute | solution.py:423
  16.2 13.7 %collective-permute-start.2 = (bf16[72,2304]{1,0:T(8,128)(2,1)S(1)}, bf16[72,2304]{1,0:T(8,128)(2,1)S(1)}, u32[]{:S(2)}, u32[]{:S(2)}) collective-permute-start(bf16[72,2304]{1,0:T(8,128)(2,1)S(1)} %collective-permute-done.refs_6_), channel_id=1, source_target_pairs={{0,2},{1,3},{2,0},{3,1},{4,6},{5,7},{6,4},{7,5},{8,10},{9,11},{10,... | collective-permute-start | bytes 995336 | tf_op jit(solution)/shard_map/ppermute | solution.py:423
  17.7 12.2 %collective-permute-start.3 = (bf16[72,2304]{1,0:T(8,128)(2,1)S(1)}, bf16[72,2304]{1,0:T(8,128)(2,1)S(1)}, u32[]{:S(2)}, u32[]{:S(2)}) collective-permute-start(bf16[72,2304]{1,0:T(8,128)(2,1)S(1)} %collective-permute-done.refs_6_), channel_id=1, source_target_pairs={{0,4},{4,0},{1,5},{5,1},{2,6},{6,2},{3,7},{7,3},{8,12},{12,8},{9,1... | collective-permute-start | bytes 995336 | tf_op jit(solution)/shard_map/ppermute | solution.py:423
  19.2 10.6 %collective-permute-start.5 = (bf16[72,2304]{1,0:T(8,128)(2,1)S(1)}, bf16[72,2304]{1,0:T(8,128)(2,1)S(1)}, u32[]{:S(2)}, u32[]{:S(2)}) collective-permute-start(bf16[72,2304]{1,0:T(8,128)(2,1)S(1)} %collective-permute-done.refs_6_), channel_id=1, source_target_pairs={{0,8},{8,16},{16,24},{24,0},{1,9},{9,17},{17,25},{25,1},{2,10},{10... | collective-permute-start | bytes 995336 | tf_op jit(solution)/shard_map/ppermute | solution.py:512
  31.4 12.1 %collective-permute-start.6 = (bf16[72,3456]{1,0:T(8,128)(2,1)}, bf16[72,3456]{1,0:T(8,128)(2,1)S(1)}, u32[]{:S(2)}, u32[]{:S(2)}) collective-permute-start(bf16[72,3456]{1,0:T(8,128)(2,1)} %get-tuple-element.69), channel_id=1, source_target_pairs={{0,2},{1,3},{2,0},{3,1},{4,6},{5,7},{6,4},{7,5},{8,10},{9,11},{10,... | collective-permute-start | bytes 1493000 | tf_op jit(solution)/shard_map/ppermute | solution.py:423
  32.9 11.8 %collective-permute-start.7 = (bf16[72,3456]{1,0:T(8,128)(2,1)}, bf16[72,3456]{1,0:T(8,128)(2,1)S(1)}, u32[]{:S(2)}, u32[]{:S(2)}) collective-permute-start(bf16[72,3456]{1,0:T(8,128)(2,1)} %get-tuple-element.70), channel_id=1, source_target_pairs={{0,4},{4,0},{1,5},{5,1},{2,6},{6,2},{3,7},{7,3},{8,12},{12,8},{9,1... | collective-permute-start | bytes 1493000 | tf_op jit(solution)/shard_map/ppermute | solution.py:423
  34.4 10.3 %collective-permute-start.8 = (bf16[72,2304]{1,0:T(8,128)(2,1)S(1)}, bf16[72,2304]{1,0:T(8,128)(2,1)S(1)}, u32[]{:S(2)}, u32[]{:S(2)}) collective-permute-start(bf16[72,2304]{1,0:T(8,128)(2,1)S(1)} %collective-permute-done.5.refs_1_.refs_3_), channel_id=1, source_target_pairs={{0,8},{8,16},{16,24},{24,0},{1,9},{9,17},{17,25},{25,1},{2,10},{10... | collective-permute-start | bytes 995336 | tf_op jit(solution)/shard_map/ppermute | solution.py:512
  36.0 8.7 %copy-start.2 = (bf16[72,4608]{1,0:T(8,128)(2,1)S(1)}, bf16[72,4608]{1,0:T(8,128)(2,1)}, u32[]{:S(2)}) copy-start(bf16[72,4608]{1,0:T(8,128)(2,1)} %get-tuple-element.63.refs_4_) | copy-start | bytes 1990660
  45.8 14.1 %collective-permute-start.11 = (bf16[288,4736]{1,0:T(8,128)(2,1)S(1)}, bf16[288,4736]{1,0:T(8,128)(2,1)S(1)}, u32[]{:S(2)}, u32[]{:S(2)}) collective-permute-start(bf16[288,4736]{1,0:T(8,128)(2,1)S(1)} %get-tuple-element.80.refs_1_.refs_4_.refs_5_.refs_3_.refs_9_.refs_2_.refs_8_), channel_id=1, source_target_pairs={{0,1},{1,0},{2,3},{3,2},{4,5},{5,4},{6,7},{7,6},{8,9},{9,8},{10,11... | collective-permute-start | bytes 8183816 | tf_op jit(solution)/shard_map/ppermute | solution.py:423
  45.9 13.8 %collective-permute-start.9 = (bf16[72,3456]{1,0:T(8,128)(2,1)S(1)}, bf16[72,3456]{1,0:T(8,128)(2,1)S(1)}, u32[]{:S(2)}, u32[]{:S(2)}) collective-permute-start(bf16[72,3456]{1,0:T(8,128)(2,1)S(1)} %get-tuple-element.78), channel_id=1, source_target_pairs={{0,2},{1,3},{2,0},{3,1},{4,6},{5,7},{6,4},{7,5},{8,10},{9,11},{10,... | collective-permute-start | bytes 1493000 | tf_op jit(solution)/shard_map/ppermute | solution.py:423
  46.5 17.5 %copy-start = (bf16[1,1,128,1152]{3,2,1,0:T(8,128)(2,1)S(1)}, bf16[1,1,128,1152]{3,2,1,0:T(8,128)(2,1)}, u32[]{:S(2)}) copy-start(bf16[1,1,128,1152]{3,2,1,0:T(8,128)(2,1)} %param.15) | copy-start | bytes 884740
  46.5 13.4 %collective-permute-start.10 = (bf16[72,3456]{1,0:T(8,128)(2,1)S(1)}, bf16[72,3456]{1,0:T(8,128)(2,1)S(1)}, u32[]{:S(2)}, u32[]{:S(2)}) collective-permute-start(bf16[72,3456]{1,0:T(8,128)(2,1)S(1)} %get-tuple-element.79), channel_id=1, source_target_pairs={{0,4},{4,0},{1,5},{5,1},{2,6},{6,2},{3,7},{7,3},{8,12},{12,8},{9,1... | collective-permute-start | bytes 1493000 | tf_op jit(solution)/shard_map/ppermute | solution.py:423
  60.9 8.0 %collective-permute-start.14 = (bf16[144,4736]{1,0:T(8,128)(2,1)S(1)}, bf16[144,4736]{1,0:T(8,128)(2,1)S(1)}, u32[]{:S(2)}, u32[]{:S(2)}) collective-permute-start(bf16[144,4736]{1,0:T(8,128)(2,1)S(1)} %get-tuple-element.86.refs_2_.refs_5_.refs_6_.refs_4_.refs_10_.refs_3_.refs_9_), channel_id=1, source_target_pairs={{0,1},{1,0},{2,3},{3,2},{4,5},{5,4},{6,7},{7,6},{8,9},{9,8},{10,11... | collective-permute-start | bytes 4091912 | tf_op jit(solution)/shard_map/ppermute | solution.py:423
  60.9 6.7 %collective-permute-start.12 = (bf16[72,1152]{1,0:T(8,128)(2,1)S(1)}, bf16[72,1152]{1,0:T(8,128)(2,1)S(1)}, u32[]{:S(2)}, u32[]{:S(2)}) collective-permute-start(bf16[72,1152]{1,0:T(8,128)(2,1)S(1)} %get-tuple-element.83), channel_id=1, source_target_pairs={{0,2},{1,3},{2,0},{3,1},{4,6},{5,7},{6,4},{7,5},{8,10},{9,11},{10,... | collective-permute-start | bytes 497672 | tf_op jit(solution)/shard_map/ppermute | solution.py:423
  62.5 6.3 %collective-permute-start.13 = (bf16[72,1152]{1,0:T(8,128)(2,1)S(1)}, bf16[72,1152]{1,0:T(8,128)(2,1)S(1)}, u32[]{:S(2)}, u32[]{:S(2)}) collective-permute-start(bf16[72,1152]{1,0:T(8,128)(2,1)S(1)} %get-tuple-element.84), channel_id=1, source_target_pairs={{0,4},{4,0},{1,5},{5,1},{2,6},{6,2},{3,7},{7,3},{8,12},{12,8},{9,1... | collective-permute-start | bytes 497672 | tf_op jit(solution)/shard_map/ppermute | solution.py:423
  64.0 5.9 %collective-permute-start.15 = (bf16[64,1152]{1,0:T(8,128)(2,1)S(1)}, bf16[64,1152]{1,0:T(8,128)(2,1)S(1)}, u32[]{:S(2)}, u32[]{:S(2)}) collective-permute-start(bf16[64,1152]{1,0:T(8,128)(2,1)S(1)} %get-tuple-element.123), channel_id=1, source_target_pairs={{0,1},{1,2},{2,3},{4,5},{5,6},{6,7},{8,9},{9,10},{10,11},{12,13},{... | collective-permute-start | bytes 442376 | tf_op jit(solution)/shard_map/ppermute | solution.py:489
  65.8 7.4 %copy-start.1 = (bf16[1,1,128,1152]{3,2,1,0:T(8,128)(2,1)S(1)}, bf16[1,1,128,1152]{3,2,1,0:T(8,128)(2,1)}, u32[]{:S(2)}) copy-start(bf16[1,1,128,1152]{3,2,1,0:T(8,128)(2,1)} %param.16) | copy-start | bytes 884740
  65.8 7.9 %copy-start.3 = (f32[1,2,1152]{2,1,0:T(2,128)S(1)}, f32[1,2,1152]{2,1,0:T(2,128)}, u32[]{:S(2)}) copy-start(f32[1,2,1152]{2,1,0:T(2,128)} %param.17) | copy-start | bytes 27652
  65.8 4.0 %collective-permute-start.16 = (bf16[64,1152]{1,0:T(8,128)(2,1)S(1)}, bf16[64,1152]{1,0:T(8,128)(2,1)S(1)}, u32[]{:S(2)}, u32[]{:S(2)}) collective-permute-start(bf16[64,1152]{1,0:T(8,128)(2,1)S(1)} %get-tuple-element.122), channel_id=1, source_target_pairs={{1,0},{2,1},{3,2},{5,4},{6,5},{7,6},{9,8},{10,9},{11,10},{13,12},{... | collective-permute-start | bytes 442376 | tf_op jit(solution)/shard_map/ppermute | solution.py:490
  69.9 6.6 %collective-permute-start.17 = (bf16[144,4736]{1,0:T(8,128)(2,1)S(1)}, bf16[144,4736]{1,0:T(8,128)(2,1)S(1)}, u32[]{:S(2)}, u32[]{:S(2)}) collective-permute-start(bf16[144,4736]{1,0:T(8,128)(2,1)S(1)} %join.1.refs_6_.refs_7_.refs_5_.refs_11_.refs_4_.refs_10_), channel_id=1, source_target_pairs={{0,1},{1,0},{2,3},{3,2},{4,5},{5,4},{6,7},{7,6},{8,9},{9,8},{10,11... | collective-permute-start | bytes 4091912 | tf_op jit(solution)/shard_map/ppermute | solution.py:423
  73.2 8.9 %collective-permute-start.18 = (bf16[128,1152]{1,0:T(8,128)(2,1)S(1)}, bf16[128,1152]{1,0:T(8,128)(2,1)S(1)}, u32[]{:S(2)}, u32[]{:S(2)}) collective-permute-start(bf16[128,1152]{1,0:T(8,128)(2,1)S(1)} %bitcast.12), channel_id=1, source_target_pairs={{0,4},{4,0},{1,5},{5,1},{2,6},{6,2},{3,7},{7,3},{8,12},{12,8},{9,1... | collective-permute-start | bytes 884744 | tf_op jit(solution)/shard_map/ppermute | solution.py:423
  74.9 1.7 %copy-start.4 = (s32[2,4]{1,0:T(2,128)S(1)}, s32[2,4]{1,0:T(2,128)}, u32[]{:S(2)}) copy-start(s32[2,4]{1,0:T(2,128)} %refs_1_.7) | copy-start | bytes 100
  76.5 6.2 %copy-start.9 = (s32[576]{0:T(1024)S(1)}, s32[576]{0:T(1024)}, u32[]{:S(2)}) copy-start(s32[576]{0:T(1024)} %constant.75.clone) | copy-start | bytes 6916
  76.5 6.1 %copy-start.10 = (s32[576]{0:T(1024)S(1)}, s32[576]{0:T(1024)}, u32[]{:S(2)}) copy-start(s32[576]{0:T(1024)} %constant.74.clone) | copy-start | bytes 6916
  76.5 6.1 %copy-start.11 = (s32[576]{0:T(1024)S(1)}, s32[576]{0:T(1024)}, u32[]{:S(2)}) copy-start(s32[576]{0:T(1024)} %constant.73.clone) | copy-start | bytes 6916
  82.1 5.3 %collective-permute-start.19 = (bf16[128,576]{1,0:T(8,128)(2,1)S(1)}, bf16[128,576]{1,0:T(8,128)(2,1)S(1)}, u32[]{:S(2)}, u32[]{:S(2)}) collective-permute-start(bf16[128,576]{1,0:T(8,128)(2,1)S(1)} %get-tuple-element.100.refs_4_), channel_id=1, source_target_pairs={{0,4},{4,0},{1,5},{5,1},{2,6},{6,2},{3,7},{7,3},{8,12},{12,8},{9,1... | collective-permute-start | bytes 442376 | tf_op jit(solution)/shard_map/ppermute | solution.py:423
  85.6 1.8 %copy-start.5 = (s32[2,2]{1,0:T(2,128)S(1)}, s32[2,2]{1,0:T(2,128)}, u32[]{:S(2)}) copy-start(s32[2,2]{1,0:T(2,128)} %refs_1_.6) | copy-start | bytes 52
  93.4 2.5 %collective-permute-start.22 = (bf16[288,1152]{1,0:T(8,128)(2,1)S(1)}, bf16[288,1152]{1,0:T(8,128)(2,1)S(1)}, u32[]{:S(2)}, u32[]{:S(2)}) collective-permute-start(bf16[288,1152]{1,0:T(8,128)(2,1)S(1)} %get-tuple-element.113), channel_id=1, source_target_pairs={{0,1},{1,0},{2,3},{3,2},{4,5},{5,4},{6,7},{7,6},{8,9},{9,8},{10,11... | collective-permute-start | bytes 1990664 | tf_op jit(solution)/shard_map/ppermute | solution.py:423
  96.2 10.3 %collective-permute-start.23 = (bf16[144,1152]{1,0:T(8,128)(2,1)S(1)}, bf16[144,1152]{1,0:T(8,128)(2,1)S(1)}, u32[]{:S(2)}, u32[]{:S(2)}) collective-permute-start(bf16[144,1152]{1,0:T(8,128)(2,1)S(1)} %slice.33), channel_id=1, source_target_pairs={{0,2},{1,3},{2,0},{3,1},{4,6},{5,7},{6,4},{7,5},{8,10},{9,11},{10,... | collective-permute-start | bytes 995336 | tf_op jit(solution)/shard_map/ppermute | solution.py:423
  101.6 9.5 %collective-permute-start.20 = (bf16[64,1152]{1,0:T(8,128)(2,1)S(1)}, bf16[64,1152]{1,0:T(8,128)(2,1)S(1)}, u32[]{:S(2)}, u32[]{:S(2)}) collective-permute-start(bf16[64,1152]{1,0:T(8,128)(2,1)S(1)} %get-tuple-element.108), channel_id=1, source_target_pairs={{0,1},{1,2},{2,3},{4,5},{5,6},{6,7},{8,9},{9,10},{10,11},{12,13},{... | collective-permute-start | bytes 442376 | tf_op jit(solution)/shard_map/ppermute | solution.py:649
  103.7 7.4 %collective-permute-start.21 = (bf16[64,1152]{1,0:T(8,128)(2,1)S(1)}, bf16[64,1152]{1,0:T(8,128)(2,1)S(1)}, u32[]{:S(2)}, u32[]{:S(2)}) collective-permute-start(bf16[64,1152]{1,0:T(8,128)(2,1)S(1)} %get-tuple-element.109), channel_id=1, source_target_pairs={{1,0},{2,1},{3,2},{5,4},{6,5},{7,6},{9,8},{10,9},{11,10},{13,12},{... | collective-permute-start | bytes 442376 | tf_op jit(solution)/shard_map/ppermute | solution.py:650
  106.6 9.6 %collective-permute-start.24 = (bf16[36,1152]{1,0:T(8,128)(2,1)S(1)}, bf16[36,1152]{1,0:T(8,128)(2,1)S(1)}, u32[]{:S(2)}, u32[]{:S(2)}) collective-permute-start(bf16[36,1152]{1,0:T(8,128)(2,1)S(1)} %get-tuple-element.121), channel_id=1, source_target_pairs={{0,8},{8,0},{16,24},{24,16},{1,9},{9,1},{17,25},{25,17},{2,10},{10... | collective-permute-start | bytes 248840 | tf_op jit(solution)/shard_map/ppermute | solution.py:423
  108.2 10.2 %collective-permute-start.25 = (bf16[36,1152]{1,0:T(8,128)(2,1)S(1)}, bf16[36,1152]{1,0:T(8,128)(2,1)S(1)}, u32[]{:S(2)}, u32[]{:S(2)}) collective-permute-start(bf16[36,1152]{1,0:T(8,128)(2,1)S(1)} %get-tuple-element.120), channel_id=1, source_target_pairs={{0,16},{8,24},{16,0},{24,8},{1,17},{9,25},{17,1},{25,9},{2,18},{10... | collective-permute-start | bytes 248840 | tf_op jit(solution)/shard_map/ppermute | solution.py:423
  109.8 8.7 %collective-permute-start.26 = (bf16[36,1152]{1,0:T(8,128)(2,1)S(1)}, bf16[36,1152]{1,0:T(8,128)(2,1)S(1)}, u32[]{:S(2)}, u32[]{:S(2)}) collective-permute-start(bf16[36,1152]{1,0:T(8,128)(2,1)S(1)} %get-tuple-element.119), channel_id=1, source_target_pairs={{0,24},{8,16},{16,8},{24,0},{1,25},{9,17},{17,9},{25,1},{2,26},{10... | collective-permute-start | bytes 248840 | tf_op jit(solution)/shard_map/ppermute | solution.py:423

commit v2 on v1

--- a/solution.py
+++ b/solution.py
@@ -18,6 +18,7 @@
 F32 = jnp.float32
 VMEM_LIMIT = 16 * 1024 * 1024
 PACK_LIMIT = 63 * 1024 * 1024
+SHORT = pl.CostEstimate(flops=1024, bytes_accessed=1024, transcendentals=0)
 
 
 def mm(a, b):
@@ -393,7 +394,7 @@
 HBM = pl.BlockSpec(memory_space=pltpu.HBM)
 
 
-def call(kernel, name, scalars, arrays, weight, outs, scratch=(), far=(), grant=VMEM_LIMIT):
+def call(kernel, name, scalars, arrays, weight, outs, scratch=(), far=(), grant=VMEM_LIMIT, cost=None):
     plain = len(scalars) + len(arrays) + len(far)
     weight, tree = jax.tree.flatten(list(weight))
 
@@ -415,6 +416,7 @@
         out_shape=outs,
         scratch_shapes=near + list(scratch),
         compiler_params=pltpu.CompilerParams(vmem_limit_bytes=grant),
+        cost_estimate=cost,
     )(*scalars, *arrays, *far, *weight)
 
 
@@ -549,9 +551,12 @@
                     others.append(swapped(groups[-1], "tile", 1))
             if step == 1:
                 moves, made = hold((moves, made))
+            if step == clips - 2:
+                early, *_ = hold((early, came[-1]))
+                moves, before, after = hold((moves, *rims(early)))
             if step == clips - 1:
-                early, *_ = hold((early, came[-1]))
-                before, after = rims(early)
+                normed = normed_of(made, before, x, after)
+                moves, normed = hold((moves, normed))
             moves, following, others = hold((moves, following, others))
             came.append(moves)
             if step < clips - 2:
@@ -559,12 +564,8 @@
         order = made
         late_up, _ = hold((up, came[-1]))
         other_up = swapped(late_up, "seq", 1)
-        last, before, after = hold(
-            (joined(0, [pieces[-1], *came[-2], *came[-1]]), before, after)
-        )
-        groups.append(last)
+        groups.append(joined(0, [pieces[-1], *came[-2], *came[-1]]))
         others.append(swapped(groups[-1], "tile", 1))
-        normed = normed_of(order, before, x, after)
         weight = groups + others
         late = [len(groups) - 1, len(weight) - 1]
     else:
@@ -580,20 +581,19 @@
     if first:
         partial = tuple(call(
             functools.partial(early_kernel, [slots[n] for n in first]), "space_early", (),
-            (normed,), [weight[n] for n in first], (((2 * own, 3 * WIDTH), F32),),
+            (normed,), [weight[n] for n in first], (((2 * own, 3 * WIDTH), F32),), cost=SHORT,
         ))
 
     query, window, att = call(
         functools.partial(forward_kernel, tiles, slots, late), "forward", (place, space_pattern),
         (normed,) + partial, weight,
-        (((own, WIDTH), BF16), ((2 * own, 2 * WIDTH), BF16), ((own, WIDTH), BF16)),
+        (((own, WIDTH), BF16), ((2 * own, 2 * WIDTH), BF16), ((own, WIDTH), BF16)), cost=SHORT,
     )
     middle, rows = call(
         functools.partial(middle_kernel, slots), "middle", (), (index, order, x, mod, att), weight,
         (((own, model), F32), ((own, 3 * WIDTH), BF16)),
     )
     if square:
-        att, other_up = hold((att, other_up))
         ups = (up, other_up)
         other_att = swapped(att, "seq", 1)
     else:

time: 119 us -> 115 us (0.966)
  waiting for transfers between devices: 45 us -> 41.9 us
    ppermute x20, waiting for transfers between devices: 44.8 us -> 38.5 us  [swapped(): return lax.ppermute(array, axis, [(i, i ^ bit) for i in range(count)])]
    ppermute x1, waiting for transfers between devices: 0.01 us -> 3.17 us  [rims(): return (before, lax.ppermute(rows[:span], 'tile', fall))]
where the time goes in v2:
time: 115 us
  waiting for transfers between devices  41.9 us (36%)
  Pallas kernels  36 us (31%)
  starting transfers between devices  34.8 us (30%)
    ppermute x20, waiting for transfers between devices, swapped(): return lax.ppermute(array, axis, [(i, i ^ bit) for i in range(count)])  38.5 us
    pallas_call x18, Pallas kernels, call(): pl.pallas_call(body, name=name, in_specs=specs, out_specs=[VMEM] * len(ou...  36 us
    ppermute x20, starting transfers between devices, swapped(): return lax.ppermute(array, axis, [(i, i ^ bit) for i in range(count)])  23.2 us
    ppermute x3, starting transfers between devices, onward(): lax.ppermute(piece, 'dp', [(i, (i + 1) % clips) for i in range(clips)])  5.13 us
    ppermute x1, waiting for transfers between devices, rims(): return (before, lax.ppermute(rows[:span], 'tile', fall))  3.17 us
  transfers between devices with their start and end apart: 27, of which 13 were waited for; matrix products, arithmetic and copies ran while one was open for 0% of the time, Pallas kernels for 20%

profile of v2, /device:TPU:0, one launch (start us, length us, event | category | flops | bytes accessed | tf_op | source)
XLA Modules:
  0.0 115.0 jit_solution(5741090348560145192)
XLA Ops:
  0.7 2.4 %pack.1 = (bf16[72,4608]{1,0:T(8,128)(2,1)}, bf16[72,2304]{1,0:T(8,128)(2,1)}) custom-call(bf16[72,1728]{1,0:T(8,128)(2,1)} %refs_0_.1, bf16[72,1728]{1,0:T(8,128)(2,1)} %refs_1_.4, bf16[36,1152]{1,0:T(8,128)(2,1)} %refs_2_.1, bf16[36,1152]{1,0:T(8,128)(2,1)} %refs_3_.1), custom_call_target="tpu_custom_call" | custom-call | tf_op jit(solution)/shard_map/pack/pallas_call | solution.py:411
  3.1 3.1 %collective-permute-start = (bf16[72,2304]{1,0:T(8,128)(2,1)}, bf16[72,2304]{1,0:T(8,128)(2,1)S(1)}, u32[]{:S(2)}, u32[]{:S(2)}) collective-permute-start(bf16[72,2304]{1,0:T(8,128)(2,1)} %get-tuple-element.63), channel_id=1, source_target_pairs={{0,8},{8,16},{16,24},{24,0},{1,9},{9,17},{17,25},{25,1},{2,10},{10... | collective-permute-start | bytes 995336 | tf_op jit(solution)/shard_map/ppermute | solution.py:514
  6.1 1.5 %collective-permute-start.4 = (bf16[72,4608]{1,0:T(8,128)(2,1)}, bf16[72,4608]{1,0:T(8,128)(2,1)S(1)}, u32[]{:S(2)}, u32[]{:S(2)}) collective-permute-start(bf16[72,4608]{1,0:T(8,128)(2,1)} %get-tuple-element.65.refs_4_), channel_id=1, source_target_pairs={{0,2},{1,3},{2,0},{3,1},{4,6},{5,7},{6,4},{7,5},{8,10},{9,11},{10,... | collective-permute-start | bytes 1990664 | tf_op jit(solution)/shard_map/ppermute | solution.py:425
  7.6 1.5 %collective-permute-start.1 = (bf16[128,1152]{1,0:T(8,128)(2,1)}, bf16[128,1152]{1,0:T(8,128)(2,1)S(1)}, u32[]{:S(2)}, u32[]{:S(2)}) collective-permute-start(bf16[128,1152]{1,0:T(8,128)(2,1)} %bitcast.7), channel_id=1, source_target_pairs={{0,4},{4,0},{1,5},{5,1},{2,6},{6,2},{3,7},{7,3},{8,12},{12,8},{9,1... | collective-permute-start | bytes 884744 | tf_op jit(solution)/shard_map/ppermute | solution.py:425
  9.1 6.9 %collective-permute-done.1.refs_5_ = bf16[128,1152]{1,0:T(8,128)(2,1)S(1)} collective-permute-done((bf16[128,1152]{1,0:T(8,128)(2,1)}, bf16[128,1152]{1,0:T(8,128)(2,1)S(1)}, u32[]{:S(2)}, u32[]{:S(2)}) %collective-permute-start.1) | collective-permute-done | bytes 294944 | tf_op jit(solution)/shard_map/ppermute | solution.py:425
  16.2 1.5 %collective-permute-start.2 = (bf16[72,2304]{1,0:T(8,128)(2,1)S(1)}, bf16[72,2304]{1,0:T(8,128)(2,1)S(1)}, u32[]{:S(2)}, u32[]{:S(2)}) collective-permute-start(bf16[72,2304]{1,0:T(8,128)(2,1)S(1)} %collective-permute-done.refs_6_), channel_id=1, source_target_pairs={{0,2},{1,3},{2,0},{3,1},{4,6},{5,7},{6,4},{7,5},{8,10},{9,11},{10,... | collective-permute-start | bytes 995336 | tf_op jit(solution)/shard_map/ppermute | solution.py:425
  17.7 1.5 %collective-permute-start.3 = (bf16[72,2304]{1,0:T(8,128)(2,1)S(1)}, bf16[72,2304]{1,0:T(8,128)(2,1)S(1)}, u32[]{:S(2)}, u32[]{:S(2)}) collective-permute-start(bf16[72,2304]{1,0:T(8,128)(2,1)S(1)} %collective-permute-done.refs_6_), channel_id=1, source_target_pairs={{0,4},{4,0},{1,5},{5,1},{2,6},{6,2},{3,7},{7,3},{8,12},{12,8},{9,1... | collective-permute-start | bytes 995336 | tf_op jit(solution)/shard_map/ppermute | solution.py:425
  19.7 10.1 %collective-permute-done.2.refs_2_.refs_7_ = bf16[72,2304]{1,0:T(8,128)(2,1)S(1)} collective-permute-done((bf16[72,2304]{1,0:T(8,128)(2,1)S(1)}, bf16[72,2304]{1,0:T(8,128)(2,1)S(1)}, u32[]{:S(2)}, u32[]{:S(2)}) %collective-permute-start.2) | collective-permute-done | bytes 331808 | tf_op jit(solution)/shard_map/ppermute | solution.py:425
  29.8 1.5 %send.3 = (bf16[72,3456]{1,0:T(8,128)(2,1)}, bf16[72,3456]{1,0:T(8,128)(2,1)}) custom-call(s32[2]{0:T(128)S(1)} %pad_add_fusion.1.refs_0_, bf16[72,2304]{1,0:T(8,128)(2,1)S(1)} %collective-permute-done.5.refs_1_.refs_3_, bf16[72,2304]{1,0:T(8,128)(2,1)S(1)} %collective-permute-done.2.refs_2_.refs_7_, bf16[72,2304]{1,0:T(8,128)(2,1)S(1)} %collective-permute-done.3.refs_3_.refs_8_), custom_call_target="tpu_custom_call" | custom-call | tf_op jit(solution)/shard_map/send/pallas_call | solution.py:411
  31.4 1.5 %collective-permute-start.6 = (bf16[72,3456]{1,0:T(8,128)(2,1)}, bf16[72,3456]{1,0:T(8,128)(2,1)S(1)}, u32[]{:S(2)}, u32[]{:S(2)}) collective-permute-start(bf16[72,3456]{1,0:T(8,128)(2,1)} %get-tuple-element.71), channel_id=1, source_target_pairs={{0,2},{1,3},{2,0},{3,1},{4,6},{5,7},{6,4},{7,5},{8,10},{9,11},{10,... | collective-permute-start | bytes 1493000 | tf_op jit(solution)/shard_map/ppermute | solution.py:425
  32.9 1.5 %collective-permute-start.7 = (bf16[72,3456]{1,0:T(8,128)(2,1)}, bf16[72,3456]{1,0:T(8,128)(2,1)S(1)}, u32[]{:S(2)}, u32[]{:S(2)}) collective-permute-start(bf16[72,3456]{1,0:T(8,128)(2,1)} %get-tuple-element.72), channel_id=1, source_target_pairs={{0,4},{4,0},{1,5},{5,1},{2,6},{6,2},{3,7},{7,3},{8,12},{12,8},{9,1... | collective-permute-start | bytes 1493000 | tf_op jit(solution)/shard_map/ppermute | solution.py:425
  34.4 1.6 %collective-permute-start.8 = (bf16[72,2304]{1,0:T(8,128)(2,1)S(1)}, bf16[72,2304]{1,0:T(8,128)(2,1)S(1)}, u32[]{:S(2)}, u32[]{:S(2)}) collective-permute-start(bf16[72,2304]{1,0:T(8,128)(2,1)S(1)} %collective-permute-done.5.refs_1_.refs_3_), channel_id=1, source_target_pairs={{0,8},{8,16},{16,24},{24,0},{1,9},{9,17},{17,25},{25,1},{2,10},{10... | collective-permute-start | bytes 995336 | tf_op jit(solution)/shard_map/ppermute | solution.py:514
  36.6 6.9 %collective-permute-done.6.refs_2_.refs_9_.refs_4_ = bf16[72,3456]{1,0:T(8,128)(2,1)S(1)} collective-permute-done((bf16[72,3456]{1,0:T(8,128)(2,1)}, bf16[72,3456]{1,0:T(8,128)(2,1)S(1)}, u32[]{:S(2)}, u32[]{:S(2)}) %collective-permute-start.6) | collective-permute-done | bytes 497696 | tf_op jit(solution)/shard_map/ppermute | solution.py:425
  43.5 1.2 %collective-permute-done.7.refs_3_.refs_10_.refs_5_ = bf16[72,3456]{1,0:T(8,128)(2,1)S(1)} collective-permute-done((bf16[72,3456]{1,0:T(8,128)(2,1)}, bf16[72,3456]{1,0:T(8,128)(2,1)S(1)}, u32[]{:S(2)}, u32[]{:S(2)}) %collective-permute-start.7) | collective-permute-done | bytes 497696 | tf_op jit(solution)/shard_map/ppermute | solution.py:425
  44.7 1.1 send.4
  46.5 1.5 %collective-permute-start.10 = (bf16[72,3456]{1,0:T(8,128)(2,1)S(1)}, bf16[72,3456]{1,0:T(8,128)(2,1)S(1)}, u32[]{:S(2)}, u32[]{:S(2)}) collective-permute-start(bf16[72,3456]{1,0:T(8,128)(2,1)S(1)} %get-tuple-element.81), channel_id=1, source_target_pairs={{0,4},{4,0},{1,5},{5,1},{2,6},{6,2},{3,7},{7,3},{8,12},{12,8},{9,1... | collective-permute-start | bytes 1493000 | tf_op jit(solution)/shard_map/ppermute | solution.py:425
  48.1 1.8 %collective-permute-start.11 = (bf16[64,1152]{1,0:T(8,128)(2,1)S(1)}, bf16[64,1152]{1,0:T(8,128)(2,1)S(1)}, u32[]{:S(2)}, u32[]{:S(2)}) collective-permute-start(bf16[64,1152]{1,0:T(8,128)(2,1)S(1)} %get-tuple-element.127), channel_id=1, source_target_pairs={{0,1},{1,2},{2,3},{4,5},{5,6},{6,7},{8,9},{9,10},{10,11},{12,13},{... | collective-permute-start | bytes 442376 | tf_op jit(solution)/shard_map/ppermute | solution.py:491
  49.9 1.3 %collective-permute-start.12 = (bf16[64,1152]{1,0:T(8,128)(2,1)S(1)}, bf16[64,1152]{1,0:T(8,128)(2,1)S(1)}, u32[]{:S(2)}, u32[]{:S(2)}) collective-permute-start(bf16[64,1152]{1,0:T(8,128)(2,1)S(1)} %get-tuple-element.126), channel_id=1, source_target_pairs={{1,0},{2,1},{3,2},{5,4},{6,5},{7,6},{9,8},{10,9},{11,10},{13,12},{... | collective-permute-start | bytes 442376 | tf_op jit(solution)/shard_map/ppermute | solution.py:492
  51.2 3.2 %collective-permute-done.12.refs_3_ = bf16[64,1152]{1,0:T(8,128)(2,1)S(1)} collective-permute-done((bf16[64,1152]{1,0:T(8,128)(2,1)S(1)}, bf16[64,1152]{1,0:T(8,128)(2,1)S(1)}, u32[]{:S(2)}, u32[]{:S(2)}) %collective-permute-start.12) | collective-permute-done | bytes 147488 | tf_op jit(solution)/shard_map/ppermute | solution.py:492
  54.4 5.3 %collective-permute-done.9.refs_1_.refs_6_.refs_2_ = bf16[72,3456]{1,0:T(8,128)(2,1)S(1)} collective-permute-done((bf16[72,3456]{1,0:T(8,128)(2,1)S(1)}, bf16[72,3456]{1,0:T(8,128)(2,1)S(1)}, u32[]{:S(2)}, u32[]{:S(2)}) %collective-permute-start.9) | collective-permute-done | bytes 497696 | tf_op jit(solution)/shard_map/ppermute | solution.py:425
  59.9 0.9 send.5
  60.9 1.2 %collective-permute-start.16 = (bf16[144,4736]{1,0:T(8,128)(2,1)S(1)}, bf16[144,4736]{1,0:T(8,128)(2,1)S(1)}, u32[]{:S(2)}, u32[]{:S(2)}) collective-permute-start(bf16[144,4736]{1,0:T(8,128)(2,1)S(1)} %get-tuple-element.94.refs_2_.refs_5_.refs_6_.refs_4_.refs_10_.refs_3_.refs_9_), channel_id=1, source_target_pairs={{0,1},{1,0},{2,3},{3,2},{4,5},{5,4},{6,7},{7,6},{8,9},{9,8},{10,11... | collective-permute-start | bytes 4091912 | tf_op jit(solution)/shard_map/ppermute | solution.py:425
  62.9 1.5 %collective-permute-start.15 = (bf16[72,1152]{1,0:T(8,128)(2,1)S(1)}, bf16[72,1152]{1,0:T(8,128)(2,1)S(1)}, u32[]{:S(2)}, u32[]{:S(2)}) collective-permute-start(bf16[72,1152]{1,0:T(8,128)(2,1)S(1)} %get-tuple-element.90), channel_id=1, source_target_pairs={{0,4},{4,0},{1,5},{5,1},{2,6},{6,2},{3,7},{7,3},{8,12},{12,8},{9,1... | collective-permute-start | bytes 497672 | tf_op jit(solution)/shard_map/ppermute | solution.py:425
  64.4 1.1 normed.1.refs_0_.refs_2_
  65.5 2.8 %collective-permute-done.14.refs_4_ = bf16[72,1152]{1,0:T(8,128)(2,1)S(1)} collective-permute-done((bf16[72,1152]{1,0:T(8,128)(2,1)S(1)}, bf16[72,1152]{1,0:T(8,128)(2,1)S(1)}, u32[]{:S(2)}, u32[]{:S(2)}) %collective-permute-start.14) | collective-permute-done | bytes 165920 | tf_op jit(solution)/shard_map/ppermute | solution.py:425
  68.3 0.9 collective-permute-done.15.refs_5_
  69.2 1.1 join.1.refs_6_.refs_7_.refs_5_.refs_11_.refs_4_.refs_10_
  70.4 1.5 %collective-permute-start.19 = (bf16[128,1152]{1,0:T(8,128)(2,1)S(1)}, bf16[128,1152]{1,0:T(8,128)(2,1)S(1)}, u32[]{:S(2)}, u32[]{:S(2)}) collective-permute-start(bf16[128,1152]{1,0:T(8,128)(2,1)S(1)} %bitcast.12), channel_id=1, source_target_pairs={{0,4},{4,0},{1,5},{5,1},{2,6},{6,2},{3,7},{7,3},{8,12},{12,8},{9,1... | collective-permute-start | bytes 884744 | tf_op jit(solution)/shard_map/ppermute | solution.py:425
  71.9 1.6 %space_early.1.refs_3_ = f32[256,1728]{1,0:T(8,128)S(1)} custom-call(bf16[256,1152]{1,0:T(8,128)(2,1)S(1)} %normed.1.refs_0_.refs_2_, bf16[288,4736]{1,0:T(8,128)(2,1)S(1)} %get-tuple-element.86.refs_1_.refs_4_.refs_5_.refs_3_.refs_9_.refs_2_.refs_8_, bf16[144,4736]{1,0:T(8,128)(2,1)S(1)} %get-tuple-element.94.refs_2_.refs_5_.refs_6_.refs_4_.refs_10_.refs_3_.refs_9_, ...), custom_call_target="tpu_custom_call" | custom-call | flops 1024 | bytes 1024 | tf_op jit(solution)/shard_map/space_early/pallas_call | solution.py:411
  73.6 3.2 %forward.1 = (bf16[128,576]{1,0:T(8,128)(2,1)S(1)}, bf16[256,1152]{1,0:T(8,128)(2,1)S(1)}, bf16[128,576]{1,0:T(8,128)(2,1)S(1)}) custom-call(s32[2]{0:T(128)S(1)} %pad_add_fusion.1.refs_0_, s32[2,4]{1,0:T(2,128)S(1)} %copy-done.4, bf16[256,1152]{1,0:T(8,128)(2,1)S(1)} %normed.1.refs_0_.refs_2_, f32[256,1728]{1,0:T(8,128)S(1)} %space_early.1.refs_3_, ...), custom_call_target="tpu_custom_call" | custom-call | flops 1024 | bytes 1024 | tf_op jit(solution)/shard_map/forward/pallas_call | solution.py:411
  76.8 1.4 %collective-permute-start.18 = (bf16[128,576]{1,0:T(8,128)(2,1)S(1)}, bf16[128,576]{1,0:T(8,128)(2,1)S(1)}, u32[]{:S(2)}, u32[]{:S(2)}) collective-permute-start(bf16[128,576]{1,0:T(8,128)(2,1)S(1)} %get-tuple-element.102.refs_4_), channel_id=1, source_target_pairs={{0,4},{4,0},{1,5},{5,1},{2,6},{6,2},{3,7},{7,3},{8,12},{12,8},{9,1... | collective-permute-start | bytes 442376 | tf_op jit(solution)/shard_map/ppermute | solution.py:425
  78.2 2.9 %middle.1 = (f32[128,1152]{1,0:T(8,128)S(1)}, bf16[128,1728]{1,0:T(8,128)(2,1)S(1)}) custom-call(s32[3,1152]{1,0:T(4,128)S(1)} %pad_add_fusion.refs_0_.refs_2_, bf16[1152,1152]{1,0:T(8,128)(2,1)S(1)} %order.1.refs_0_.refs_1_.refs_3_, bf16[128,1152]{1,0:T(8,128)(2,1)S(1)} %bitcast.10, f32[2,1152]{1,0:T(2,128)S(1)} %bitcast.17, ...), custom_call_target="tpu_custom_call" | custom-call | tf_op jit(solution)/shard_map/middle/pallas_call | solution.py:411
  81.2 1.6 %att_grad.1.refs_8_ = bf16[256,576]{1,0:T(8,128)(2,1)S(1)} custom-call(s32[3,1152]{1,0:T(4,128)S(1)} %pad_add_fusion.refs_0_.refs_2_, bf16[128,1152]{1,0:T(8,128)(2,1)S(1)} %bitcast.13, bf16[128,1152]{1,0:T(8,128)(2,1)S(1)} %collective-permute-done.19.refs_2_.refs_3_, ...), custom_call_target="tpu_custom_call" | custom-call | tf_op jit(solution)/shard_map/att_grad/pallas_call | solution.py:411
  83.3 4.7 %time_att.1 = (bf16[128,2304]{1,0:T(8,128)(2,1)S(1)}, bf16[256,576]{1,0:T(8,128)(2,1)S(1)}) custom-call(s32[2]{0:T(128)S(1)} %pad_add_fusion.1.refs_0_, s32[2,2]{1,0:T(2,128)S(1)} %copy-done.5, s32[3,1152]{1,0:T(4,128)S(1)} %pad_add_fusion.refs_0_.refs_2_, bf16[1152,1152]{1,0:T(8,128)(2,1)S(1)} %order.1.refs_0_.refs_1_.refs_3_, f32[2,1152]{1,0:T(2,128)S(1)} %bitcast.18, ...), custom_call_target="tpu_custom_call" | custom-call | tf_op jit(solution)/shard_map/time_att/pallas_call | solution.py:411
  88.0 1.1 term.1
  89.1 2.7 %middle_back.1.refs_1_.refs_3_ = f32[128,1152]{1,0:T(8,128)S(1)} custom-call(bf16[1152,1152]{1,0:T(8,128)(2,1)S(1)} %order.1.refs_0_.refs_1_.refs_3_, bf16[128,1152]{1,0:T(8,128)(2,1)S(1)} %bitcast.15, f32[2,1152]{1,0:T(2,128)S(1)} %bitcast.19, f32[128,1152]{1,0:T(8,128)S(1)} %get-tuple-element.103.refs_3_.refs_1_, ...), custom_call_target="tpu_custom_call" | custom-call | tf_op jit(solution)/shard_map/middle_back/pallas_call | solution.py:411
  92.0 0.9 collective-permute-start.23
  92.9 1.4 %space_grad.1.refs_4_ = bf16[128,576]{1,0:T(8,128)(2,1)S(1)} custom-call(s32[3,1152]{1,0:T(4,128)S(1)} %pad_add_fusion.refs_0_.refs_2_, f32[128,1152]{1,0:T(8,128)S(1)} %middle_back.1.refs_1_.refs_3_, bf16[288,4736]{1,0:T(8,128)(2,1)S(1)} %get-tuple-element.86.refs_1_.refs_4_.refs_5_.refs_3_.refs_9_.refs_2_.refs_8_, ...), custom_call_target="tpu_custom_call" | custom-call | tf_op jit(solution)/shard_map/space_grad/pallas_call | solution.py:411
  94.4 3.1 %space_back.1 = (bf16[128,576]{1,0:T(8,128)(2,1)S(1)}, f32[128,1152]{1,0:T(8,128)S(1)}, bf16[64,1152]{1,0:T(8,128)(2,1)S(1)}, bf16[64,1152]{1,0:T(8,128)(2,1)S(1)}) custom-call(s32[2]{0:T(128)S(1)} %pad_add_fusion.1.refs_0_, s32[2,4]{1,0:T(2,128)S(1)} %copy-done.4, bf16[128,576]{1,0:T(8,128)(2,1)S(1)} %get-tuple-element.108.refs_2_, ...), custom_call_target="tpu_custom_call" | custom-call | tf_op jit(solution)/shard_map/space_back/pallas_call | solution.py:411
  97.5 2.1 %collective-permute-start.20 = (bf16[64,1152]{1,0:T(8,128)(2,1)S(1)}, bf16[64,1152]{1,0:T(8,128)(2,1)S(1)}, u32[]{:S(2)}, u32[]{:S(2)}) collective-permute-start(bf16[64,1152]{1,0:T(8,128)(2,1)S(1)} %get-tuple-element.112), channel_id=1, source_target_pairs={{0,1},{1,2},{2,3},{4,5},{5,6},{6,7},{8,9},{9,10},{10,11},{12,13},{... | collective-permute-start | bytes 442376 | tf_op jit(solution)/shard_map/ppermute | solution.py:649
  99.6 1.3 %collective-permute-start.21 = (bf16[64,1152]{1,0:T(8,128)(2,1)S(1)}, bf16[64,1152]{1,0:T(8,128)(2,1)S(1)}, u32[]{:S(2)}, u32[]{:S(2)}) collective-permute-start(bf16[64,1152]{1,0:T(8,128)(2,1)S(1)} %get-tuple-element.113), channel_id=1, source_target_pairs={{1,0},{2,1},{3,2},{5,4},{6,5},{7,6},{9,8},{10,9},{11,10},{13,12},{... | collective-permute-start | bytes 442376 | tf_op jit(solution)/shard_map/ppermute | solution.py:650
  100.9 1.4 %collective-permute-done.23 = bf16[144,1152]{1,0:T(8,128)(2,1)S(1)} collective-permute-done((bf16[144,1152]{1,0:T(8,128)(2,1)S(1)}, bf16[144,1152]{1,0:T(8,128)(2,1)S(1)}, u32[]{:S(2)}, u32[]{:S(2)}) %collective-permute-start.23) | collective-permute-done | bytes 331808 | tf_op jit(solution)/shard_map/ppermute | solution.py:425
  102.5 1.7 %collective-permute-start.24 = (bf16[36,1152]{1,0:T(8,128)(2,1)S(1)}, bf16[36,1152]{1,0:T(8,128)(2,1)S(1)}, u32[]{:S(2)}, u32[]{:S(2)}) collective-permute-start(bf16[36,1152]{1,0:T(8,128)(2,1)S(1)} %get-tuple-element.125), channel_id=1, source_target_pairs={{0,8},{8,0},{16,24},{24,16},{1,9},{9,1},{17,25},{25,17},{2,10},{10... | collective-permute-start | bytes 248840 | tf_op jit(solution)/shard_map/ppermute | solution.py:425
  104.1 1.7 %collective-permute-start.25 = (bf16[36,1152]{1,0:T(8,128)(2,1)S(1)}, bf16[36,1152]{1,0:T(8,128)(2,1)S(1)}, u32[]{:S(2)}, u32[]{:S(2)}) collective-permute-start(bf16[36,1152]{1,0:T(8,128)(2,1)S(1)} %get-tuple-element.124), channel_id=1, source_target_pairs={{0,16},{8,24},{16,0},{24,8},{1,17},{9,25},{17,1},{25,9},{2,18},{10... | collective-permute-start | bytes 248840 | tf_op jit(solution)/shard_map/ppermute | solution.py:425
  105.8 1.1 collective-permute-start.26
  106.9 3.2 %start_back.1 = bf16[128,1152]{1,0:T(8,128)(2,1)} custom-call(bf16[1152,1152]{1,0:T(8,128)(2,1)S(1)} %order.1.refs_0_.refs_1_.refs_3_, bf16[128,1152]{1,0:T(8,128)(2,1)S(1)} %bitcast.11, f32[2,1152]{1,0:T(2,128)S(1)} %bitcast.20, f32[128,1152]{1,0:T(8,128)S(1)} %middle_back.1.refs_1_.refs_3_, bf16[128,576]{1,0:T(8,128)(2,1)S(1)} %get-tuple-element.110.refs_4_, ...), custom_call_target="tpu_custom_call" | custom-call | tf_op jit(solution)/shard_map/start_back/pallas_call | solution.py:411
  110.1 1.9 %result.1 = bf16[128,1152]{1,0:T(8,128)(2,1)} custom-call(s32[3,1152]{1,0:T(4,128)S(1)} %pad_add_fusion.refs_0_.refs_2_, f32[128,1152]{1,0:T(8,128)S(1)} %get-tuple-element.103.refs_3_.refs_1_, bf16[128,2304]{1,0:T(8,128)(2,1)S(1)} %get-tuple-element.114.refs_4_.refs_2_, ...), custom_call_target="tpu_custom_call" | custom-call | tf_op jit(solution)/shard_map/result/pallas_call | solution.py:411
  112.0 2.3 %collective-permute-done.25 = bf16[36,1152]{1,0:T(8,128)(2,1)S(1)} collective-permute-done((bf16[36,1152]{1,0:T(8,128)(2,1)S(1)}, bf16[36,1152]{1,0:T(8,128)(2,1)S(1)}, u32[]{:S(2)}, u32[]{:S(2)}) %collective-permute-start.25) | collective-permute-done | bytes 82976 | tf_op jit(solution)/shard_map/ppermute | solution.py:425
  (62 shorter events, 4.8 us)
Async XLA Ops:
  0.6 35.3 %copy-start.6 = (s32[1152]{0:T(1024)S(1)}, s32[1152]{0:T(1024)}, u32[]{:S(2)}) copy-start(s32[1152]{0:T(1024)} %constant.72.clone) | copy-start | bytes 13828
  0.6 35.3 %copy-start.7 = (s32[1152]{0:T(1024)S(1)}, s32[1152]{0:T(1024)}, u32[]{:S(2)}) copy-start(s32[1152]{0:T(1024)} %constant.70.clone) | copy-start | bytes 13828
  0.7 35.3 %copy-start.8 = (s32[1152]{0:T(1024)S(1)}, s32[1152]{0:T(1024)}, u32[]{:S(2)}) copy-start(s32[1152]{0:T(1024)} %constant.84) | copy-start | bytes 13828
  3.1 13.1 %collective-permute-start = (bf16[72,2304]{1,0:T(8,128)(2,1)}, bf16[72,2304]{1,0:T(8,128)(2,1)S(1)}, u32[]{:S(2)}, u32[]{:S(2)}) collective-permute-start(bf16[72,2304]{1,0:T(8,128)(2,1)} %get-tuple-element.63), channel_id=1, source_target_pairs={{0,8},{8,16},{16,24},{24,0},{1,9},{9,17},{17,25},{25,1},{2,10},{10... | collective-permute-start | bytes 995336 | tf_op jit(solution)/shard_map/ppermute | solution.py:514
  6.1 23.7 %collective-permute-start.4 = (bf16[72,4608]{1,0:T(8,128)(2,1)}, bf16[72,4608]{1,0:T(8,128)(2,1)S(1)}, u32[]{:S(2)}, u32[]{:S(2)}) collective-permute-start(bf16[72,4608]{1,0:T(8,128)(2,1)} %get-tuple-element.65.refs_4_), channel_id=1, source_target_pairs={{0,2},{1,3},{2,0},{3,1},{4,6},{5,7},{6,4},{7,5},{8,10},{9,11},{10,... | collective-permute-start | bytes 1990664 | tf_op jit(solution)/shard_map/ppermute | solution.py:425
  7.6 8.4 %collective-permute-start.1 = (bf16[128,1152]{1,0:T(8,128)(2,1)}, bf16[128,1152]{1,0:T(8,128)(2,1)S(1)}, u32[]{:S(2)}, u32[]{:S(2)}) collective-permute-start(bf16[128,1152]{1,0:T(8,128)(2,1)} %bitcast.7), channel_id=1, source_target_pairs={{0,4},{4,0},{1,5},{5,1},{2,6},{6,2},{3,7},{7,3},{8,12},{12,8},{9,1... | collective-permute-start | bytes 884744 | tf_op jit(solution)/shard_map/ppermute | solution.py:425
  16.2 13.7 %collective-permute-start.2 = (bf16[72,2304]{1,0:T(8,128)(2,1)S(1)}, bf16[72,2304]{1,0:T(8,128)(2,1)S(1)}, u32[]{:S(2)}, u32[]{:S(2)}) collective-permute-start(bf16[72,2304]{1,0:T(8,128)(2,1)S(1)} %collective-permute-done.refs_6_), channel_id=1, source_target_pairs={{0,2},{1,3},{2,0},{3,1},{4,6},{5,7},{6,4},{7,5},{8,10},{9,11},{10,... | collective-permute-start | bytes 995336 | tf_op jit(solution)/shard_map/ppermute | solution.py:425
  17.7 12.2 %collective-permute-start.3 = (bf16[72,2304]{1,0:T(8,128)(2,1)S(1)}, bf16[72,2304]{1,0:T(8,128)(2,1)S(1)}, u32[]{:S(2)}, u32[]{:S(2)}) collective-permute-start(bf16[72,2304]{1,0:T(8,128)(2,1)S(1)} %collective-permute-done.refs_6_), channel_id=1, source_target_pairs={{0,4},{4,0},{1,5},{5,1},{2,6},{6,2},{3,7},{7,3},{8,12},{12,8},{9,1... | collective-permute-start | bytes 995336 | tf_op jit(solution)/shard_map/ppermute | solution.py:425
  19.2 10.6 %collective-permute-start.5 = (bf16[72,2304]{1,0:T(8,128)(2,1)S(1)}, bf16[72,2304]{1,0:T(8,128)(2,1)S(1)}, u32[]{:S(2)}, u32[]{:S(2)}) collective-permute-start(bf16[72,2304]{1,0:T(8,128)(2,1)S(1)} %collective-permute-done.refs_6_), channel_id=1, source_target_pairs={{0,8},{8,16},{16,24},{24,0},{1,9},{9,17},{17,25},{25,1},{2,10},{10... | collective-permute-start | bytes 995336 | tf_op jit(solution)/shard_map/ppermute | solution.py:514
  31.4 12.1 %collective-permute-start.6 = (bf16[72,3456]{1,0:T(8,128)(2,1)}, bf16[72,3456]{1,0:T(8,128)(2,1)S(1)}, u32[]{:S(2)}, u32[]{:S(2)}) collective-permute-start(bf16[72,3456]{1,0:T(8,128)(2,1)} %get-tuple-element.71), channel_id=1, source_target_pairs={{0,2},{1,3},{2,0},{3,1},{4,6},{5,7},{6,4},{7,5},{8,10},{9,11},{10,... | collective-permute-start | bytes 1493000 | tf_op jit(solution)/shard_map/ppermute | solution.py:425
  32.9 11.8 %collective-permute-start.7 = (bf16[72,3456]{1,0:T(8,128)(2,1)}, bf16[72,3456]{1,0:T(8,128)(2,1)S(1)}, u32[]{:S(2)}, u32[]{:S(2)}) collective-permute-start(bf16[72,3456]{1,0:T(8,128)(2,1)} %get-tuple-element.72), channel_id=1, source_target_pairs={{0,4},{4,0},{1,5},{5,1},{2,6},{6,2},{3,7},{7,3},{8,12},{12,8},{9,1... | collective-permute-start | bytes 1493000 | tf_op jit(solution)/shard_map/ppermute | solution.py:425
  34.4 10.3 %collective-permute-start.8 = (bf16[72,2304]{1,0:T(8,128)(2,1)S(1)}, bf16[72,2304]{1,0:T(8,128)(2,1)S(1)}, u32[]{:S(2)}, u32[]{:S(2)}) collective-permute-start(bf16[72,2304]{1,0:T(8,128)(2,1)S(1)} %collective-permute-done.5.refs_1_.refs_3_), channel_id=1, source_target_pairs={{0,8},{8,16},{16,24},{24,0},{1,9},{9,17},{17,25},{25,1},{2,10},{10... | collective-permute-start | bytes 995336 | tf_op jit(solution)/shard_map/ppermute | solution.py:514
  36.0 8.7 %copy-start.2 = (bf16[72,4608]{1,0:T(8,128)(2,1)S(1)}, bf16[72,4608]{1,0:T(8,128)(2,1)}, u32[]{:S(2)}) copy-start(bf16[72,4608]{1,0:T(8,128)(2,1)} %get-tuple-element.65.refs_4_) | copy-start | bytes 1990660
  36.6 11.5 %copy-start = (bf16[1,1,128,1152]{3,2,1,0:T(8,128)(2,1)S(1)}, bf16[1,1,128,1152]{3,2,1,0:T(8,128)(2,1)}, u32[]{:S(2)}) copy-start(bf16[1,1,128,1152]{3,2,1,0:T(8,128)(2,1)} %param.15) | copy-start | bytes 884740
  45.8 14.1 %collective-permute-start.13 = (bf16[288,4736]{1,0:T(8,128)(2,1)S(1)}, bf16[288,4736]{1,0:T(8,128)(2,1)S(1)}, u32[]{:S(2)}, u32[]{:S(2)}) collective-permute-start(bf16[288,4736]{1,0:T(8,128)(2,1)S(1)} %get-tuple-element.86.refs_1_.refs_4_.refs_5_.refs_3_.refs_9_.refs_2_.refs_8_), channel_id=1, source_target_pairs={{0,1},{1,0},{2,3},{3,2},{4,5},{5,4},{6,7},{7,6},{8,9},{9,8},{10,11... | collective-permute-start | bytes 8183816 | tf_op jit(solution)/shard_map/ppermute | solution.py:425
  45.9 13.8 %collective-permute-start.9 = (bf16[72,3456]{1,0:T(8,128)(2,1)S(1)}, bf16[72,3456]{1,0:T(8,128)(2,1)S(1)}, u32[]{:S(2)}, u32[]{:S(2)}) collective-permute-start(bf16[72,3456]{1,0:T(8,128)(2,1)S(1)} %get-tuple-element.80), channel_id=1, source_target_pairs={{0,2},{1,3},{2,0},{3,1},{4,6},{5,7},{6,4},{7,5},{8,10},{9,11},{10,... | collective-permute-start | bytes 1493000 | tf_op jit(solution)/shard_map/ppermute | solution.py:425
  46.5 13.4 %collective-permute-start.10 = (bf16[72,3456]{1,0:T(8,128)(2,1)S(1)}, bf16[72,3456]{1,0:T(8,128)(2,1)S(1)}, u32[]{:S(2)}, u32[]{:S(2)}) collective-permute-start(bf16[72,3456]{1,0:T(8,128)(2,1)S(1)} %get-tuple-element.81), channel_id=1, source_target_pairs={{0,4},{4,0},{1,5},{5,1},{2,6},{6,2},{3,7},{7,3},{8,12},{12,8},{9,1... | collective-permute-start | bytes 1493000 | tf_op jit(solution)/shard_map/ppermute | solution.py:425
  48.1 3.1 %collective-permute-start.11 = (bf16[64,1152]{1,0:T(8,128)(2,1)S(1)}, bf16[64,1152]{1,0:T(8,128)(2,1)S(1)}, u32[]{:S(2)}, u32[]{:S(2)}) collective-permute-start(bf16[64,1152]{1,0:T(8,128)(2,1)S(1)} %get-tuple-element.127), channel_id=1, source_target_pairs={{0,1},{1,2},{2,3},{4,5},{5,6},{6,7},{8,9},{9,10},{10,11},{12,13},{... | collective-permute-start | bytes 442376 | tf_op jit(solution)/shard_map/ppermute | solution.py:491
  49.9 14.5 %copy-start.3 = (f32[1,2,1152]{2,1,0:T(2,128)S(1)}, f32[1,2,1152]{2,1,0:T(2,128)}, u32[]{:S(2)}) copy-start(f32[1,2,1152]{2,1,0:T(2,128)} %param.17) | copy-start | bytes 27652
  49.9 4.5 %collective-permute-start.12 = (bf16[64,1152]{1,0:T(8,128)(2,1)S(1)}, bf16[64,1152]{1,0:T(8,128)(2,1)S(1)}, u32[]{:S(2)}, u32[]{:S(2)}) collective-permute-start(bf16[64,1152]{1,0:T(8,128)(2,1)S(1)} %get-tuple-element.126), channel_id=1, source_target_pairs={{1,0},{2,1},{3,2},{5,4},{6,5},{7,6},{9,8},{10,9},{11,10},{13,12},{... | collective-permute-start | bytes 442376 | tf_op jit(solution)/shard_map/ppermute | solution.py:492
  60.9 8.3 %collective-permute-start.16 = (bf16[144,4736]{1,0:T(8,128)(2,1)S(1)}, bf16[144,4736]{1,0:T(8,128)(2,1)S(1)}, u32[]{:S(2)}, u32[]{:S(2)}) collective-permute-start(bf16[144,4736]{1,0:T(8,128)(2,1)S(1)} %get-tuple-element.94.refs_2_.refs_5_.refs_6_.refs_4_.refs_10_.refs_3_.refs_9_), channel_id=1, source_target_pairs={{0,1},{1,0},{2,3},{3,2},{4,5},{5,4},{6,7},{7,6},{8,9},{9,8},{10,11... | collective-permute-start | bytes 4091912 | tf_op jit(solution)/shard_map/ppermute | solution.py:425
  62.1 6.2 %collective-permute-start.14 = (bf16[72,1152]{1,0:T(8,128)(2,1)S(1)}, bf16[72,1152]{1,0:T(8,128)(2,1)S(1)}, u32[]{:S(2)}, u32[]{:S(2)}) collective-permute-start(bf16[72,1152]{1,0:T(8,128)(2,1)S(1)} %get-tuple-element.89), channel_id=1, source_target_pairs={{0,2},{1,3},{2,0},{3,1},{4,6},{5,7},{6,4},{7,5},{8,10},{9,11},{10,... | collective-permute-start | bytes 497672 | tf_op jit(solution)/shard_map/ppermute | solution.py:425
  62.9 6.3 %collective-permute-start.15 = (bf16[72,1152]{1,0:T(8,128)(2,1)S(1)}, bf16[72,1152]{1,0:T(8,128)(2,1)S(1)}, u32[]{:S(2)}, u32[]{:S(2)}) collective-permute-start(bf16[72,1152]{1,0:T(8,128)(2,1)S(1)} %get-tuple-element.90), channel_id=1, source_target_pairs={{0,4},{4,0},{1,5},{5,1},{2,6},{6,2},{3,7},{7,3},{8,12},{12,8},{9,1... | collective-permute-start | bytes 497672 | tf_op jit(solution)/shard_map/ppermute | solution.py:425
  65.5 4.9 %copy-start.1 = (bf16[1,1,128,1152]{3,2,1,0:T(8,128)(2,1)S(1)}, bf16[1,1,128,1152]{3,2,1,0:T(8,128)(2,1)}, u32[]{:S(2)}) copy-start(bf16[1,1,128,1152]{3,2,1,0:T(8,128)(2,1)} %param.16) | copy-start | bytes 884740
  70.3 3.3 %collective-permute-start.17 = (bf16[144,4736]{1,0:T(8,128)(2,1)S(1)}, bf16[144,4736]{1,0:T(8,128)(2,1)S(1)}, u32[]{:S(2)}, u32[]{:S(2)}) collective-permute-start(bf16[144,4736]{1,0:T(8,128)(2,1)S(1)} %join.1.refs_6_.refs_7_.refs_5_.refs_11_.refs_4_.refs_10_), channel_id=1, source_target_pairs={{0,1},{1,0},{2,3},{3,2},{4,5},{5,4},{6,7},{7,6},{8,9},{9,8},{10,11... | collective-permute-start | bytes 4091912 | tf_op jit(solution)/shard_map/ppermute | solution.py:425
  70.4 3.2 %copy-start.4 = (s32[2,4]{1,0:T(2,128)S(1)}, s32[2,4]{1,0:T(2,128)}, u32[]{:S(2)}) copy-start(s32[2,4]{1,0:T(2,128)} %refs_1_.7) | copy-start | bytes 100
  70.4 10.8 %collective-permute-start.19 = (bf16[128,1152]{1,0:T(8,128)(2,1)S(1)}, bf16[128,1152]{1,0:T(8,128)(2,1)S(1)}, u32[]{:S(2)}, u32[]{:S(2)}) collective-permute-start(bf16[128,1152]{1,0:T(8,128)(2,1)S(1)} %bitcast.12), channel_id=1, source_target_pairs={{0,4},{4,0},{1,5},{5,1},{2,6},{6,2},{3,7},{7,3},{8,12},{12,8},{9,1... | collective-permute-start | bytes 884744 | tf_op jit(solution)/shard_map/ppermute | solution.py:425
  73.6 4.6 %copy-start.9 = (s32[576]{0:T(1024)S(1)}, s32[576]{0:T(1024)}, u32[]{:S(2)}) copy-start(s32[576]{0:T(1024)} %constant.75.clone) | copy-start | bytes 6916
  73.6 4.6 %copy-start.10 = (s32[576]{0:T(1024)S(1)}, s32[576]{0:T(1024)}, u32[]{:S(2)}) copy-start(s32[576]{0:T(1024)} %constant.74.clone) | copy-start | bytes 6916
  73.6 4.6 %copy-start.11 = (s32[576]{0:T(1024)S(1)}, s32[576]{0:T(1024)}, u32[]{:S(2)}) copy-start(s32[576]{0:T(1024)} %constant.73.clone) | copy-start | bytes 6916
  76.8 6.5 %collective-permute-start.18 = (bf16[128,576]{1,0:T(8,128)(2,1)S(1)}, bf16[128,576]{1,0:T(8,128)(2,1)S(1)}, u32[]{:S(2)}, u32[]{:S(2)}) collective-permute-start(bf16[128,576]{1,0:T(8,128)(2,1)S(1)} %get-tuple-element.102.refs_4_), channel_id=1, source_target_pairs={{0,4},{4,0},{1,5},{5,1},{2,6},{6,2},{3,7},{7,3},{8,12},{12,8},{9,1... | collective-permute-start | bytes 442376 | tf_op jit(solution)/shard_map/ppermute | solution.py:425
  81.2 2.1 %copy-start.5 = (s32[2,2]{1,0:T(2,128)S(1)}, s32[2,2]{1,0:T(2,128)}, u32[]{:S(2)}) copy-start(s32[2,2]{1,0:T(2,128)} %refs_1_.6) | copy-start | bytes 52
  89.0 2.8 %collective-permute-start.22 = (bf16[288,1152]{1,0:T(8,128)(2,1)S(1)}, bf16[288,1152]{1,0:T(8,128)(2,1)S(1)}, u32[]{:S(2)}, u32[]{:S(2)}) collective-permute-start(bf16[288,1152]{1,0:T(8,128)(2,1)S(1)} %get-tuple-element.117), channel_id=1, source_target_pairs={{0,1},{1,0},{2,3},{3,2},{4,5},{5,4},{6,7},{7,6},{8,9},{9,8},{10,11... | collective-permute-start | bytes 1990664 | tf_op jit(solution)/shard_map/ppermute | solution.py:425
  92.0 10.3 %collective-permute-start.23 = (bf16[144,1152]{1,0:T(8,128)(2,1)S(1)}, bf16[144,1152]{1,0:T(8,128)(2,1)S(1)}, u32[]{:S(2)}, u32[]{:S(2)}) collective-permute-start(bf16[144,1152]{1,0:T(8,128)(2,1)S(1)} %slice.33), channel_id=1, source_target_pairs={{0,2},{1,3},{2,0},{3,1},{4,6},{5,7},{6,4},{7,5},{8,10},{9,11},{10,... | collective-permute-start | bytes 995336 | tf_op jit(solution)/shard_map/ppermute | solution.py:425
  97.5 9.4 %collective-permute-start.20 = (bf16[64,1152]{1,0:T(8,128)(2,1)S(1)}, bf16[64,1152]{1,0:T(8,128)(2,1)S(1)}, u32[]{:S(2)}, u32[]{:S(2)}) collective-permute-start(bf16[64,1152]{1,0:T(8,128)(2,1)S(1)} %get-tuple-element.112), channel_id=1, source_target_pairs={{0,1},{1,2},{2,3},{4,5},{5,6},{6,7},{8,9},{9,10},{10,11},{12,13},{... | collective-permute-start | bytes 442376 | tf_op jit(solution)/shard_map/ppermute | solution.py:649
  99.6 7.3 %collective-permute-start.21 = (bf16[64,1152]{1,0:T(8,128)(2,1)S(1)}, bf16[64,1152]{1,0:T(8,128)(2,1)S(1)}, u32[]{:S(2)}, u32[]{:S(2)}) collective-permute-start(bf16[64,1152]{1,0:T(8,128)(2,1)S(1)} %get-tuple-element.113), channel_id=1, source_target_pairs={{1,0},{2,1},{3,2},{5,4},{6,5},{7,6},{9,8},{10,9},{11,10},{13,12},{... | collective-permute-start | bytes 442376 | tf_op jit(solution)/shard_map/ppermute | solution.py:650
  102.5 9.6 %collective-permute-start.24 = (bf16[36,1152]{1,0:T(8,128)(2,1)S(1)}, bf16[36,1152]{1,0:T(8,128)(2,1)S(1)}, u32[]{:S(2)}, u32[]{:S(2)}) collective-permute-start(bf16[36,1152]{1,0:T(8,128)(2,1)S(1)} %get-tuple-element.125), channel_id=1, source_target_pairs={{0,8},{8,0},{16,24},{24,16},{1,9},{9,1},{17,25},{25,17},{2,10},{10... | collective-permute-start | bytes 248840 | tf_op jit(solution)/shard_map/ppermute | solution.py:425
  104.1 10.2 %collective-permute-start.25 = (bf16[36,1152]{1,0:T(8,128)(2,1)S(1)}, bf16[36,1152]{1,0:T(8,128)(2,1)S(1)}, u32[]{:S(2)}, u32[]{:S(2)}) collective-permute-start(bf16[36,1152]{1,0:T(8,128)(2,1)S(1)} %get-tuple-element.124), channel_id=1, source_target_pairs={{0,16},{8,24},{16,0},{24,8},{1,17},{9,25},{17,1},{25,9},{2,18},{10... | collective-permute-start | bytes 248840 | tf_op jit(solution)/shard_map/ppermute | solution.py:425
  105.8 8.5 %collective-permute-start.26 = (bf16[36,1152]{1,0:T(8,128)(2,1)S(1)}, bf16[36,1152]{1,0:T(8,128)(2,1)S(1)}, u32[]{:S(2)}, u32[]{:S(2)}) collective-permute-start(bf16[36,1152]{1,0:T(8,128)(2,1)S(1)} %get-tuple-element.123), channel_id=1, source_target_pairs={{0,24},{8,16},{16,8},{24,0},{1,25},{9,17},{17,9},{25,1},{2,26},{10... | collective-permute-start | bytes 248840 | tf_op jit(solution)/shard_map/ppermute | solution.py:425

commit v3 on v2

--- a/solution.py
+++ b/solution.py
@@ -96,17 +96,10 @@
     return total
 
 
-def behind(grad, weight, start, stop, select, rounded=False):
-    count = grad.shape[0]
+def behind(grad, weight, start, stop, select):
     turned = grad.astype(F32).T.astype(BF16)
-    parts = [mm(ref[:, start:stop], turned) for ref in weight]
-    part = jnp.concatenate(parts, axis=0)
-    high = part.astype(BF16)
-    if rounded:
-        return mm(select[...], high).T.astype(BF16)
-    low = (part - high.astype(F32)).astype(BF16)
-    both = mm(select[...], jnp.concatenate([high, low], axis=1))
-    return (both[:, :count] + both[:, count:]).T
+    parts = [mm(ref[:, start:stop], turned).astype(BF16) for ref in weight]
+    return mm(select[...], jnp.concatenate(parts, axis=0)).T
 
 
 def space_allowed(place, pattern, span, tiles):
@@ -186,34 +179,24 @@
     out_ref[rows, out:stop] = full[:, 6 * WIDTH :].astype(BF16)
 
 
-def join_kernel(owned, place, *refs):
-    whole, parts, out_ref = refs[:owned], refs[owned:-1], refs[-1]
-    top = 0
-    if whole:
-        rows = [ref[...].astype(F32) for ref in whole]
+def join_kernel(layout, place, *refs):
+    *refs, out_ref = refs
+    blocks, at = [], 0
+    for ranges in layout:
+        taken = refs[at : at + len(ranges)]
+        parts = [ref[:, start:stop].astype(F32) for ref, (start, stop) in zip(taken, ranges)]
+        blocks.append((parts[0], parts[1:]))
+        at += len(ranges)
+
+    def write(first):
+        rows = []
+        for mine, other in blocks:
+            sides = [mine, *other] if first else [*other, mine]
+            rows.append(jnp.concatenate(sides, axis=1) if other else mine)
         place_columns(out_ref, 0, jnp.concatenate(rows, axis=0))
-        top = sum(ref.shape[0] for ref in whole)
-    if not parts:
-        return
-    near, by_tile, by_seq, corner_low, corner_high = parts
-    lanes = near.shape[1]
-    mine = [near[...].astype(F32), by_tile[:, :lanes].astype(F32)]
-    mine = jnp.concatenate(mine, axis=0)
-    low, high = corner_low.shape[1] % lanes, corner_high.shape[1] % lanes
-    corner = [
-        corner_low[:, corner_low.shape[1] - low :].astype(F32),
-        corner_high[:, corner_high.shape[1] - high :].astype(F32),
-    ]
-    corner = jnp.concatenate(corner, axis=1)
-    other = jnp.concatenate([by_seq[:, :lanes].astype(F32), corner], axis=0)
-
-    @pl.when(place[1] == 0)
-    def _():
-        place_columns(out_ref, top, jnp.concatenate([mine, other], axis=1))
-
-    @pl.when(place[1] != 0)
-    def _():
-        place_columns(out_ref, top, jnp.concatenate([other, mine], axis=1))
+
+    pl.when(place[1] == 0)(lambda: write(True))
+    pl.when(place[1] != 0)(lambda: write(False))
 
 
 def order_kernel(index_ref, order_ref):
@@ -231,7 +214,7 @@
 
 
 def forward_kernel(tiles, slots, late, place, pattern, normed_ref, *refs):
-    *partial, weight, q_ref, kv_ref, att_ref = refs
+    *partial, weight, q_ref, kv_ref, att_ref, probs_ref = refs
     own = q_ref.shape[0]
     span = own // 2
     rows = ahead(
@@ -246,6 +229,7 @@
     kv_ref[...] = kv
     allowed = space_allowed(place, pattern, span, tiles)
     probs = softmax_of(spread(query), keys, allowed)
+    probs_ref[...] = probs
     att_ref[...] = collect(mm(probs.astype(BF16), values)).astype(BF16)
 
 
@@ -268,9 +252,8 @@
     upstream = jnp.concatenate([ref[...] for ref in refs[:parts]], axis=0).astype(BF16)
     weight, grad_ref = refs[parts:]
     *_, out, stop = columns(upstream.shape[1])
-    grad_ref[...] = behind(
-        upstream, weight, out, stop, expander(index_ref[row : row + 1, :]), rounded=True
-    )
+    select = expander(index_ref[row : row + 1, :])
+    grad_ref[...] = behind(upstream, weight, out, stop, select).astype(BF16)
 
 
 def time_att_kernel(allowed_ref, rows_ref, grad_ref, out_ref):
@@ -332,11 +315,15 @@
 
 
 def term_kernel(parts, index_ref, att_ref, *refs):
-    upstream = jnp.concatenate([ref[...] for ref in refs[:parts]], axis=0)
-    mine_ref, theirs_ref = refs[parts:]
+    ups, (mine_ref, theirs_ref) = refs[:parts], refs[parts:]
     att = mm(att_ref[...], expander(index_ref[...])).astype(BF16)
+    count = ups[0].shape[0]
+    term = mm_tn(att[:count], ups[0][...])
+    if parts > 1:
+        other = jnp.concatenate([ref[...] for ref in ups[1:]], axis=0)
+        term = term + mm_tn(att[count:], other)
     half = mine_ref.shape[0]
-    term = mm_tn(att, upstream).astype(BF16)
+    term = term.astype(BF16)
     mine_ref[...] = term[:half]
     theirs_ref[...] = term[half:]
 
@@ -360,14 +347,13 @@
 
 
 def space_back_kernel(
-    tiles, place, pattern, q_ref, kv_ref, att_grad_ref, dq_ref, own_ref, low_ref, high_ref
+    q_ref, kv_ref, probs_ref, att_grad_ref, dq_ref, own_ref, low_ref, high_ref
 ):
     span = low_ref.shape[0]
     keys, values = kv_ref[:, :WIDTH], kv_ref[:, WIDTH:]
-    allowed = space_allowed(place, pattern, span, tiles)
-    spread_q = spread(q_ref[...])
-    probs = softmax_of(spread_q, keys, allowed)
-    dquery, dkeys, dvalues = attention_back(spread_q, keys, values, probs, att_grad_ref[...])
+    dquery, dkeys, dvalues = attention_back(
+        spread(q_ref[...]), keys, values, probs_ref[...], att_grad_ref[...]
+    )
     dq_ref[...] = dquery.astype(BF16)
     both = jnp.concatenate([dkeys, dvalues], axis=1)
     low_ref[...] = both[:span].astype(BF16)
@@ -460,7 +446,6 @@
 
     square = seq == 2 and tiles == 4
     hold = lax.optimization_barrier
-    apart = range(1, clips)
     width = 6 * WIDTH + model
     own_w, half_w = call(
         pack_kernel, "pack", (), (), (),
@@ -491,12 +476,14 @@
         before = lax.ppermute(rows[span:], "tile", rise)
         return before, lax.ppermute(rows[:span], "tile", fall)
 
-    def joined(owned, pieces):
-        rows = owned * 2 * shard + (4 * shard if len(pieces) > owned else 0)
-        return call(
-            functools.partial(join_kernel, owned), "join", (place,), pieces, (),
-            (((rows, columns(model)[-1]), BF16),),
-        )[0]
+    def joined(blocks):
+        layout = [[(start, stop) for _, start, stop in block] for block in blocks]
+        arrays = [array for block in blocks for array, _, _ in block]
+        shape = (len(blocks) * 2 * shard, columns(model)[-1])
+        return functools.partial(join_kernel, layout), arrays, (shape, BF16)
+
+    def whole(array):
+        return (array, 0, array.shape[1])
 
     (made,) = call(order_kernel, "order", (), (index,), (), (((model, model), BF16),))
 
@@ -513,23 +500,34 @@
         def onward(piece):
             return lax.ppermute(piece, "dp", [(i, (i + 1) % clips) for i in range(clips)])
 
-        def sends(piece, by_tile, by_seq, owned=(), parts=()):
+        def near_rows(piece, sides):
+            return [(piece, 0, lanes), (sides[1], 0, lanes)]
+
+        def far_rows(sides, later):
+            low, high = (part.shape[1] for part in later)
+            return [
+                (sides[0], 0, lanes),
+                (later[0], low - cut, low), (later[1], high - (lanes - cut), high),
+            ]
+
+        def sends(piece, by_tile, by_seq, blocks=()):
             arrays = [by_tile, by_seq] if piece is None else [piece, by_tile, by_seq]
-            at, count, joins = (0 if piece is None else lanes), len(arrays), len(owned) + len(parts)
+            at, count = (0 if piece is None else lanes), len(arrays)
+            join, parts, shape = joined(blocks)
 
             def kernel(place_ref, *refs):
-                sides, earlier, outs = refs[:count], refs[count : count + joins], refs[count + joins :]
+                sides, earlier = refs[:count], refs[count : count + len(parts)]
+                outs = refs[count + len(parts) :]
                 sides = sides if piece is not None else (None,) + sides
                 send_kernel((cut, lanes), *sides, *outs[:2])
-                if joins:
-                    join_kernel(len(owned), place_ref, *earlier, outs[2])
+                if parts:
+                    join(place_ref, *earlier, outs[2])
 
             outs = [((2 * shard, at + cut), BF16), ((2 * shard, at + lanes - cut), BF16)]
-            if joins:
-                rows = len(owned) * 2 * shard + 4 * shard
-                outs.append(((rows, columns(model)[-1]), BF16))
+            if parts:
+                outs.append(shape)
             over_tile, over_seq, *group = call(
-                kernel, "send", (place,), (*arrays, *owned, *parts), (), outs
+                kernel, "send", (place,), (*arrays, *parts), (), outs
             )
             return group, (swapped(over_tile, "tile", 2), swapped(over_seq, "seq", 1))
 
@@ -541,11 +539,16 @@
             following = onward(piece) if step < clips - 2 else ()
             if step == 0:
                 moves = swapped(piece, "tile", 2), swapped(piece, "seq", 1)
-                moves, across = hold((moves, across))
+                later_up, _ = hold((up, piece))
+                moves, across, other_up = hold((moves, across, swapped(later_up[:half], "seq", 1)))
             else:
-                owned = [own_w, across] if step == 2 else []
-                parts = [pieces[step - 2], *came[step - 2], *came[step - 1]] if step > 1 else []
-                group, moves = sends(piece, *came[-1], owned, parts)
+                blocks = [[whole(own_w)], [whole(across)]] if step == 2 else []
+                if step > 1:
+                    blocks.append(near_rows(pieces[step - 2], came[step - 2]))
+                    blocks.append(far_rows(came[step - 2], came[step - 1]))
+                if step == clips - 1:
+                    blocks.append(near_rows(pieces[step - 1], came[step - 1]))
+                group, moves = sends(piece, *came[-1], blocks)
                 if group:
                     groups += group
                     others.append(swapped(groups[-1], "tile", 1))
@@ -556,45 +559,52 @@
                 moves, before, after = hold((moves, *rims(early)))
             if step == clips - 1:
                 normed = normed_of(made, before, x, after)
-                moves, normed = hold((moves, normed))
+                at = groups[0].shape[0]
+                (partial,) = call(
+                    functools.partial(early_kernel, [(0, at), (at, groups[1].shape[0]), (model // 2, at)]),
+                    "space_early", (), (normed,), [*groups[:2], others[0]],
+                    (((2 * own, 3 * WIDTH), F32),), cost=SHORT,
+                )
+                late = normed
+                moves, normed, partial = hold((moves, normed, partial))
             moves, following, others = hold((moves, following, others))
             came.append(moves)
             if step < clips - 2:
                 pieces.append(following)
         order = made
-        late_up, _ = hold((up, came[-1]))
-        other_up = swapped(late_up, "seq", 1)
-        groups.append(joined(0, [pieces[-1], *came[-2], *came[-1]]))
+        late_up, _ = hold((up, late))
+        other_up = other_up, swapped(late_up[half:], "seq", 1)
+        join, parts, shape = joined([far_rows(came[-2], came[-1])])
+        groups += call(join, "join", (place,), parts, (), (shape,))
         others.append(swapped(groups[-1], "tile", 1))
         weight = groups + others
-        late = [len(groups) - 1, len(weight) - 1]
+        late, partial = [2, 4, 5], (partial,)
     else:
         before, after = rims(x)
         order = made
         normed = normed_of(order, before, x, after)
-        weight = [lax.all_gather(joined(1, [own_w]), ("dp", "tile"), axis=0, tiled=True)]
-        late = [0]
+        join, parts, shape = joined([[whole(own_w)]])
+        (laid,) = call(join, "join", (place,), parts, (), (shape,))
+        weight = [lax.all_gather(laid, ("dp", "tile"), axis=0, tiled=True)]
+        late, partial = [0], ()
     ends = np.cumsum([0] + [part.shape[0] for part in weight]).tolist()
     slots = [(at, part.shape[0]) for at, part in zip(ends, weight)]
-    first = [n for n in range(len(weight)) if n not in late]
-    partial = ()
-    if first:
-        partial = tuple(call(
-            functools.partial(early_kernel, [slots[n] for n in first]), "space_early", (),
-            (normed,), [weight[n] for n in first], (((2 * own, 3 * WIDTH), F32),), cost=SHORT,
-        ))
-
-    query, window, att = call(
+
+    query, window, att, probs = call(
         functools.partial(forward_kernel, tiles, slots, late), "forward", (place, space_pattern),
         (normed,) + partial, weight,
-        (((own, WIDTH), BF16), ((2 * own, 2 * WIDTH), BF16), ((own, WIDTH), BF16)), cost=SHORT,
+        (
+            ((own, WIDTH), BF16), ((2 * own, 2 * WIDTH), BF16), ((own, WIDTH), BF16),
+            ((HEADS * own, 2 * own), F32),
+        ),
+        cost=SHORT,
     )
     middle, rows = call(
         functools.partial(middle_kernel, slots), "middle", (), (index, order, x, mod, att), weight,
-        (((own, model), F32), ((own, 3 * WIDTH), BF16)),
+        (((own, model), F32), ((own, 3 * WIDTH), BF16)), cost=SHORT,
     )
     if square:
-        ups = (up, other_up)
+        ups = (up,) + other_up
         other_att = swapped(att, "seq", 1)
     else:
         def turned(array):
@@ -605,7 +615,7 @@
         ups = (turned(up),)
     (time_att_grad,) = call(
         functools.partial(att_grad_kernel, len(ups), 2), "att_grad", (), (index,) + ups, weight,
-        (((len(ups) * own, WIDTH), BF16),),
+        ((((2 if square else 1) * own, WIDTH), BF16),),
     )
     if square:
         rows, att = call(
@@ -639,8 +649,7 @@
         (((own, WIDTH), BF16),),
     )
     dq, own_grads, to_left, to_right = call(
-        functools.partial(space_back_kernel, tiles), "space_back", (place, space_pattern),
-        (query, window, att_grad), (),
+        space_back_kernel, "space_back", (), (query, window, probs, att_grad), (),
         (
             ((own, WIDTH), BF16), ((own, 2 * WIDTH), F32),
             ((span, 2 * WIDTH), BF16), ((span, 2 * WIDTH), BF16),
@@ -670,8 +679,8 @@
         if bit < tiles:
             rows = mine.shape[0] // 2
             mine, theirs = mine[:rows], mine[rows:]
-    came = [swapped(mine[by * shard : (by + 1) * shard], "dp", by) for by in apart]
-    came = ended(came, result)
+    came = [swapped(mine[by * shard : (by + 1) * shard], "dp", by) for by in range(1, clips)]
+    came = [ended(came[0], result)] + ended(came[1:], start_grad)
     total = mine[:shard].astype(F32)
     for part in came:
         total = total + part.astype(F32)

time: 115 us -> 113 us (0.983)
  waiting for transfers between devices: 41.9 us -> 38 us
    ppermute x20 -> x21, waiting for transfers between devices: 38.5 us -> 34.7 us  [swapped(): return lax.ppermute(array, axis, [(i, i ^ bit) for i in range(count)])]
    ppermute x20 -> x21, starting transfers between devices: 23.2 us -> 23.5 us  [swapped(): return lax.ppermute(array, axis, [(i, i ^ bit) for i in range(count)])]
  transfers between devices with their start and end apart: 27 -> 28, of which waited for: 13 -> 16; matrix products, arithmetic and copies ran while one was open for 0% -> 2% of each run, Pallas kernels for 20% -> 20%
where the time goes in v3:
time: 113 us
  waiting for transfers between devices  38 us (34%)
  Pallas kernels  35.8 us (32%)
  starting transfers between devices  35.2 us (31%)
  other arithmetic  1.82 us (2%)
  local copies, waits for them, and re-layouts  1.19 us (1%)
    pallas_call x18, Pallas kernels, call(): pl.pallas_call(body, name=name, in_specs=specs, out_specs=[VMEM] * len(ou...  35.8 us
    ppermute x21, waiting for transfers between devices, swapped(): return lax.ppermute(array, axis, [(i, i ^ bit) for i in range(count)])  34.7 us
    ppermute x21, starting transfers between devices, swapped(): return lax.ppermute(array, axis, [(i, i ^ bit) for i in range(count)])  23.5 us
    ppermute x3, starting transfers between devices, onward(): lax.ppermute(piece, 'dp', [(i, (i + 1) % clips) for i in range(clips)])  5.2 us
    ppermute x1, waiting for transfers between devices, rims(): return (before, lax.ppermute(rows[:span], 'tile', fall))  3.17 us
  transfers between devices with their start and end apart: 28, of which 16 were waited for; matrix products, arithmetic and copies ran while one was open for 2% of the time, Pallas kernels for 20%

profile of v3, /device:TPU:0, one launch (start us, length us, event | category | flops | bytes accessed | tf_op | source)
XLA Modules:
  0.0 113.1 jit_solution(14368094621185082270)
XLA Ops:
  0.6 2.4 %pack.1 = (bf16[72,4608]{1,0:T(8,128)(2,1)}, bf16[72,2304]{1,0:T(8,128)(2,1)}) custom-call(bf16[72,1728]{1,0:T(8,128)(2,1)} %refs_0_.1, bf16[72,1728]{1,0:T(8,128)(2,1)} %refs_1_.3, bf16[36,1152]{1,0:T(8,128)(2,1)} %refs_2_.1, bf16[36,1152]{1,0:T(8,128)(2,1)} %refs_3_.1), custom_call_target="tpu_custom_call" | custom-call | tf_op jit(solution)/shard_map/pack/pallas_call | solution.py:397
  3.0 3.1 %collective-permute-start = (bf16[72,2304]{1,0:T(8,128)(2,1)}, bf16[72,2304]{1,0:T(8,128)(2,1)S(1)}, u32[]{:S(2)}, u32[]{:S(2)}) collective-permute-start(bf16[72,2304]{1,0:T(8,128)(2,1)} %get-tuple-element.67), channel_id=1, source_target_pairs={{0,8},{8,16},{16,24},{24,0},{1,9},{9,17},{17,25},{25,1},{2,10},{10... | collective-permute-start | bytes 995336 | tf_op jit(solution)/shard_map/ppermute | solution.py:501
  6.1 1.5 %collective-permute-start.4 = (bf16[72,4608]{1,0:T(8,128)(2,1)}, bf16[72,4608]{1,0:T(8,128)(2,1)S(1)}, u32[]{:S(2)}, u32[]{:S(2)}) collective-permute-start(bf16[72,4608]{1,0:T(8,128)(2,1)} %get-tuple-element.69.refs_4_), channel_id=1, source_target_pairs={{0,2},{1,3},{2,0},{3,1},{4,6},{5,7},{6,4},{7,5},{8,10},{9,11},{10,... | collective-permute-start | bytes 1990664 | tf_op jit(solution)/shard_map/ppermute | solution.py:411
  7.6 1.5 %collective-permute-start.1 = (bf16[128,1152]{1,0:T(8,128)(2,1)}, bf16[128,1152]{1,0:T(8,128)(2,1)S(1)}, u32[]{:S(2)}, u32[]{:S(2)}) collective-permute-start(bf16[128,1152]{1,0:T(8,128)(2,1)} %bitcast.7), channel_id=1, source_target_pairs={{0,4},{4,0},{1,5},{5,1},{2,6},{6,2},{3,7},{7,3},{8,12},{12,8},{9,1... | collective-permute-start | bytes 884744 | tf_op jit(solution)/shard_map/ppermute | solution.py:411
  9.1 6.9 %collective-permute-done.1.refs_5_ = bf16[128,1152]{1,0:T(8,128)(2,1)S(1)} collective-permute-done((bf16[128,1152]{1,0:T(8,128)(2,1)}, bf16[128,1152]{1,0:T(8,128)(2,1)S(1)}, u32[]{:S(2)}, u32[]{:S(2)}) %collective-permute-start.1) | collective-permute-done | bytes 294944 | tf_op jit(solution)/shard_map/ppermute | solution.py:411
  16.1 1.5 %collective-permute-start.2 = (bf16[72,2304]{1,0:T(8,128)(2,1)S(1)}, bf16[72,2304]{1,0:T(8,128)(2,1)S(1)}, u32[]{:S(2)}, u32[]{:S(2)}) collective-permute-start(bf16[72,2304]{1,0:T(8,128)(2,1)S(1)} %collective-permute-done.refs_6_), channel_id=1, source_target_pairs={{0,2},{1,3},{2,0},{3,1},{4,6},{5,7},{6,4},{7,5},{8,10},{9,11},{10,... | collective-permute-start | bytes 995336 | tf_op jit(solution)/shard_map/ppermute | solution.py:411
  17.6 1.5 %collective-permute-start.3 = (bf16[72,2304]{1,0:T(8,128)(2,1)S(1)}, bf16[72,2304]{1,0:T(8,128)(2,1)S(1)}, u32[]{:S(2)}, u32[]{:S(2)}) collective-permute-start(bf16[72,2304]{1,0:T(8,128)(2,1)S(1)} %collective-permute-done.refs_6_), channel_id=1, source_target_pairs={{0,4},{4,0},{1,5},{5,1},{2,6},{6,2},{3,7},{7,3},{8,12},{12,8},{9,1... | collective-permute-start | bytes 995336 | tf_op jit(solution)/shard_map/ppermute | solution.py:411
  19.7 1.0 slice.30
  21.3 7.9 %collective-permute-done.5.refs_2_.refs_3_ = bf16[64,1152]{1,0:T(8,128)(2,1)S(1)} collective-permute-done((bf16[64,1152]{1,0:T(8,128)(2,1)S(1)}, bf16[64,1152]{1,0:T(8,128)(2,1)S(1)}, u32[]{:S(2)}, u32[]{:S(2)}) %collective-permute-start.5) | collective-permute-done | bytes 147488 | tf_op jit(solution)/shard_map/ppermute | solution.py:411
  29.8 1.5 %send.3 = (bf16[72,3456]{1,0:T(8,128)(2,1)}, bf16[72,3456]{1,0:T(8,128)(2,1)}) custom-call(s32[2]{0:T(128)S(1)} %pad_add_fusion.1.refs_0_, bf16[72,2304]{1,0:T(8,128)(2,1)S(1)} %collective-permute-done.6.refs_1_.refs_3_, bf16[72,2304]{1,0:T(8,128)(2,1)S(1)} %collective-permute-done.2.refs_2_.refs_8_, bf16[72,2304]{1,0:T(8,128)(2,1)S(1)} %collective-permute-done.3.refs_3_.refs_7_), custom_call_target="tpu_custom_call" | custom-call | tf_op jit(solution)/shard_map/send/pallas_call | solution.py:397
  31.3 1.5 %collective-permute-start.7 = (bf16[72,3456]{1,0:T(8,128)(2,1)}, bf16[72,3456]{1,0:T(8,128)(2,1)S(1)}, u32[]{:S(2)}, u32[]{:S(2)}) collective-permute-start(bf16[72,3456]{1,0:T(8,128)(2,1)} %get-tuple-element.76), channel_id=1, source_target_pairs={{0,2},{1,3},{2,0},{3,1},{4,6},{5,7},{6,4},{7,5},{8,10},{9,11},{10,... | collective-permute-start | bytes 1493000 | tf_op jit(solution)/shard_map/ppermute | solution.py:411
  32.8 1.5 %collective-permute-start.8 = (bf16[72,3456]{1,0:T(8,128)(2,1)}, bf16[72,3456]{1,0:T(8,128)(2,1)S(1)}, u32[]{:S(2)}, u32[]{:S(2)}) collective-permute-start(bf16[72,3456]{1,0:T(8,128)(2,1)} %get-tuple-element.77), channel_id=1, source_target_pairs={{0,4},{4,0},{1,5},{5,1},{2,6},{6,2},{3,7},{7,3},{8,12},{12,8},{9,1... | collective-permute-start | bytes 1493000 | tf_op jit(solution)/shard_map/ppermute | solution.py:411
  34.4 1.6 %collective-permute-start.9 = (bf16[72,2304]{1,0:T(8,128)(2,1)S(1)}, bf16[72,2304]{1,0:T(8,128)(2,1)S(1)}, u32[]{:S(2)}, u32[]{:S(2)}) collective-permute-start(bf16[72,2304]{1,0:T(8,128)(2,1)S(1)} %collective-permute-done.6.refs_1_.refs_3_), channel_id=1, source_target_pairs={{0,8},{8,16},{16,24},{24,0},{1,9},{9,17},{17,25},{25,1},{2,10},{10... | collective-permute-start | bytes 995336 | tf_op jit(solution)/shard_map/ppermute | solution.py:501
  37.2 6.2 %collective-permute-done.7.refs_2_.refs_9_.refs_5_ = bf16[72,3456]{1,0:T(8,128)(2,1)S(1)} collective-permute-done((bf16[72,3456]{1,0:T(8,128)(2,1)}, bf16[72,3456]{1,0:T(8,128)(2,1)S(1)}, u32[]{:S(2)}, u32[]{:S(2)}) %collective-permute-start.7) | collective-permute-done | bytes 497696 | tf_op jit(solution)/shard_map/ppermute | solution.py:411
  43.4 1.2 %collective-permute-done.8.refs_3_.refs_10_.refs_4_ = bf16[72,3456]{1,0:T(8,128)(2,1)S(1)} collective-permute-done((bf16[72,3456]{1,0:T(8,128)(2,1)}, bf16[72,3456]{1,0:T(8,128)(2,1)S(1)}, u32[]{:S(2)}, u32[]{:S(2)}) %collective-permute-start.8) | collective-permute-done | bytes 497696 | tf_op jit(solution)/shard_map/ppermute | solution.py:411
  44.7 1.2 %send.4 = (bf16[72,3456]{1,0:T(8,128)(2,1)S(1)}, bf16[72,3456]{1,0:T(8,128)(2,1)S(1)}, bf16[288,4736]{1,0:T(8,128)(2,1)S(1)}) custom-call(s32[2]{0:T(128)S(1)} %pad_add_fusion.1.refs_0_, bf16[72,2304]{1,0:T(8,128)(2,1)S(1)} %collective-permute-done.9.refs_1_.refs_8_, bf16[72,3456]{1,0:T(8,128)(2,1)S(1)} %collective-permute-done.7.refs_2_.refs_9_.refs_5_, ...), custom_call_target="tpu_custom_call" | custom-call | tf_op jit(solution)/shard_map/send/pallas_call | solution.py:397
  46.6 1.5 %collective-permute-start.11 = (bf16[72,3456]{1,0:T(8,128)(2,1)S(1)}, bf16[72,3456]{1,0:T(8,128)(2,1)S(1)}, u32[]{:S(2)}, u32[]{:S(2)}) collective-permute-start(bf16[72,3456]{1,0:T(8,128)(2,1)S(1)} %get-tuple-element.86), channel_id=1, source_target_pairs={{0,4},{4,0},{1,5},{5,1},{2,6},{6,2},{3,7},{7,3},{8,12},{12,8},{9,1... | collective-permute-start | bytes 1493000 | tf_op jit(solution)/shard_map/ppermute | solution.py:411
  48.1 1.8 %collective-permute-start.12 = (bf16[64,1152]{1,0:T(8,128)(2,1)S(1)}, bf16[64,1152]{1,0:T(8,128)(2,1)S(1)}, u32[]{:S(2)}, u32[]{:S(2)}) collective-permute-start(bf16[64,1152]{1,0:T(8,128)(2,1)S(1)} %get-tuple-element.135), channel_id=1, source_target_pairs={{0,1},{1,2},{2,3},{4,5},{5,6},{6,7},{8,9},{9,10},{10,11},{12,13},{... | collective-permute-start | bytes 442376 | tf_op jit(solution)/shard_map/ppermute | solution.py:476
  49.9 1.3 %collective-permute-start.13 = (bf16[64,1152]{1,0:T(8,128)(2,1)S(1)}, bf16[64,1152]{1,0:T(8,128)(2,1)S(1)}, u32[]{:S(2)}, u32[]{:S(2)}) collective-permute-start(bf16[64,1152]{1,0:T(8,128)(2,1)S(1)} %get-tuple-element.134), channel_id=1, source_target_pairs={{1,0},{2,1},{3,2},{5,4},{6,5},{7,6},{9,8},{10,9},{11,10},{13,12},{... | collective-permute-start | bytes 442376 | tf_op jit(solution)/shard_map/ppermute | solution.py:477
  51.2 3.2 %collective-permute-done.13.refs_3_ = bf16[64,1152]{1,0:T(8,128)(2,1)S(1)} collective-permute-done((bf16[64,1152]{1,0:T(8,128)(2,1)S(1)}, bf16[64,1152]{1,0:T(8,128)(2,1)S(1)}, u32[]{:S(2)}, u32[]{:S(2)}) %collective-permute-start.13) | collective-permute-done | bytes 147488 | tf_op jit(solution)/shard_map/ppermute | solution.py:477
  54.4 5.3 %collective-permute-done.10.refs_1_.refs_6_ = bf16[72,3456]{1,0:T(8,128)(2,1)S(1)} collective-permute-done((bf16[72,3456]{1,0:T(8,128)(2,1)S(1)}, bf16[72,3456]{1,0:T(8,128)(2,1)S(1)}, u32[]{:S(2)}, u32[]{:S(2)}) %collective-permute-start.10) | collective-permute-done | bytes 497696 | tf_op jit(solution)/shard_map/ppermute | solution.py:411
  60.0 1.0 send.5
  61.0 1.2 %collective-permute-start.17 = (bf16[216,4736]{1,0:T(8,128)(2,1)S(1)}, bf16[216,4736]{1,0:T(8,128)(2,1)S(1)}, u32[]{:S(2)}, u32[]{:S(2)}) collective-permute-start(bf16[216,4736]{1,0:T(8,128)(2,1)S(1)} %get-tuple-element.98.refs_2_.refs_5_.refs_6_.refs_10_.refs_3_.refs_9_.refs_4_), channel_id=1, source_target_pairs={{0,1},{1,0},{2,3},{3,2},{4,5},{5,4},{6,7},{7,6},{8,9},{9,8},{10,11... | collective-permute-start | bytes 6137864 | tf_op jit(solution)/shard_map/ppermute | solution.py:411
  63.1 1.5 %collective-permute-start.16 = (bf16[72,1152]{1,0:T(8,128)(2,1)S(1)}, bf16[72,1152]{1,0:T(8,128)(2,1)S(1)}, u32[]{:S(2)}, u32[]{:S(2)}) collective-permute-start(bf16[72,1152]{1,0:T(8,128)(2,1)S(1)} %get-tuple-element.95), channel_id=1, source_target_pairs={{0,4},{4,0},{1,5},{5,1},{2,6},{6,2},{3,7},{7,3},{8,12},{12,8},{9,1... | collective-permute-start | bytes 497672 | tf_op jit(solution)/shard_map/ppermute | solution.py:411
  64.6 1.1 normed.1.refs_0_.refs_2_
  65.7 1.4 %space_early.1.refs_3_ = f32[256,1728]{1,0:T(8,128)S(1)} custom-call(bf16[256,1152]{1,0:T(8,128)(2,1)S(1)} %normed.1.refs_0_.refs_2_, bf16[288,4736]{1,0:T(8,128)(2,1)S(1)} %get-tuple-element.91.refs_1_.refs_4_.refs_5_.refs_9_.refs_2_.refs_8_.refs_3_, bf16[216,4736]{1,0:T(8,128)(2,1)S(1)} %get-tuple-element.98.refs_2_.refs_5_.refs_6_.refs_10_.refs_3_.refs_9_.refs_4_, ...), custom_call_target="tpu_custom_call" | custom-call | flops 1024 | bytes 1024 | tf_op jit(solution)/shard_map/space_early/pallas_call | solution.py:397
  67.1 1.4 %collective-permute-done.15.refs_2_ = bf16[72,1152]{1,0:T(8,128)(2,1)S(1)} collective-permute-done((bf16[72,1152]{1,0:T(8,128)(2,1)S(1)}, bf16[72,1152]{1,0:T(8,128)(2,1)S(1)}, u32[]{:S(2)}, u32[]{:S(2)}) %collective-permute-start.15) | collective-permute-done | bytes 165920 | tf_op jit(solution)/shard_map/ppermute | solution.py:411
  68.5 0.9 collective-permute-done.16.refs_3_
  69.4 0.9 join.1.refs_6_.refs_7_.refs_11_.refs_4_.refs_10_.refs_5_
  70.5 1.6 %collective-permute-start.20 = (bf16[64,1152]{1,0:T(8,128)(2,1)S(1)}, bf16[64,1152]{1,0:T(8,128)(2,1)S(1)}, u32[]{:S(2)}, u32[]{:S(2)}) collective-permute-start(bf16[64,1152]{1,0:T(8,128)(2,1)S(1)} %slice.33), channel_id=1, source_target_pairs={{0,4},{4,0},{1,5},{5,1},{2,6},{6,2},{3,7},{7,3},{8,12},{12,8},{9,1... | collective-permute-start | bytes 442376 | tf_op jit(solution)/shard_map/ppermute | solution.py:411
  72.5 3.3 %forward.1 = (bf16[128,576]{1,0:T(8,128)(2,1)S(1)}, bf16[256,1152]{1,0:T(8,128)(2,1)S(1)}, bf16[128,576]{1,0:T(8,128)(2,1)S(1)}, f32[1024,256]{1,0:T(8,128)S(1)}) custom-call(s32[2]{0:T(128)S(1)} %pad_add_fusion.1.refs_0_, s32[2,4]{1,0:T(2,128)S(1)} %copy-done.8, bf16[256,1152]{1,0:T(8,128)(2,1)S(1)} %normed.1.refs_0_.refs_2_, ...), custom_call_target="tpu_custom_call" | custom-call | flops 1024 | bytes 1024 | tf_op jit(solution)/shard_map/forward/pallas_call | solution.py:397
  75.8 1.6 %collective-permute-start.19 = (bf16[128,576]{1,0:T(8,128)(2,1)S(1)}, bf16[128,576]{1,0:T(8,128)(2,1)S(1)}, u32[]{:S(2)}, u32[]{:S(2)}) collective-permute-start(bf16[128,576]{1,0:T(8,128)(2,1)S(1)} %get-tuple-element.108.refs_4_), channel_id=1, source_target_pairs={{0,4},{4,0},{1,5},{5,1},{2,6},{6,2},{3,7},{7,3},{8,12},{12,8},{9,1... | collective-permute-start | bytes 442376 | tf_op jit(solution)/shard_map/ppermute | solution.py:411
  77.4 2.9 %middle.1 = (f32[128,1152]{1,0:T(8,128)S(1)}, bf16[128,1728]{1,0:T(8,128)(2,1)S(1)}) custom-call(s32[3,1152]{1,0:T(4,128)S(1)} %pad_add_fusion.refs_0_.refs_2_, bf16[1152,1152]{1,0:T(8,128)(2,1)S(1)} %order.1.refs_0_.refs_1_.refs_3_, bf16[128,1152]{1,0:T(8,128)(2,1)S(1)} %bitcast.10, f32[2,1152]{1,0:T(2,128)S(1)} %bitcast.18, ...), custom_call_target="tpu_custom_call" | custom-call | flops 1024 | bytes 1024 | tf_op jit(solution)/shard_map/middle/pallas_call | solution.py:397
  80.4 1.7 %att_grad.1.refs_8_ = bf16[256,576]{1,0:T(8,128)(2,1)S(1)} custom-call(s32[3,1152]{1,0:T(4,128)S(1)} %pad_add_fusion.refs_0_.refs_2_, bf16[128,1152]{1,0:T(8,128)(2,1)S(1)} %bitcast.14, bf16[64,1152]{1,0:T(8,128)(2,1)S(1)} %collective-permute-done.5.refs_2_.refs_3_, bf16[64,1152]{1,0:T(8,128)(2,1)S(1)} %collective-permute-done.20.refs_3_.refs_4_, ...), custom_call_target="tpu_custom_call" | custom-call | tf_op jit(solution)/shard_map/att_grad/pallas_call | solution.py:397
  82.1 4.7 %time_att.1 = (bf16[128,2304]{1,0:T(8,128)(2,1)S(1)}, bf16[256,576]{1,0:T(8,128)(2,1)S(1)}) custom-call(s32[2]{0:T(128)S(1)} %pad_add_fusion.1.refs_0_, s32[2,2]{1,0:T(2,128)S(1)} %copy-done.9, s32[3,1152]{1,0:T(4,128)S(1)} %pad_add_fusion.refs_0_.refs_2_, bf16[1152,1152]{1,0:T(8,128)(2,1)S(1)} %order.1.refs_0_.refs_1_.refs_3_, f32[2,1152]{1,0:T(2,128)S(1)} %bitcast.19, ...), custom_call_target="tpu_custom_call" | custom-call | tf_op jit(solution)/shard_map/time_att/pallas_call | solution.py:397
  86.8 1.3 %term.1 = (bf16[288,1152]{1,0:T(8,128)(2,1)S(1)}, bf16[288,1152]{1,0:T(8,128)(2,1)S(1)}) custom-call(s32[1,576]{1,0:T(1,128)S(1)} %reshape.29.refs_0_, bf16[256,576]{1,0:T(8,128)(2,1)S(1)} %get-tuple-element.123.refs_1_, bf16[128,1152]{1,0:T(8,128)(2,1)S(1)} %bitcast.15, bf16[64,1152]{1,0:T(8,128)(2,1)S(1)} %collective-permute-done.5.refs_2_.refs_3_, ...), custom_call_target="tpu_custom_call" | custom-call | tf_op jit(solution)/shard_map/term/pallas_call | solution.py:397
  88.2 2.6 %middle_back.1.refs_1_.refs_3_ = f32[128,1152]{1,0:T(8,128)S(1)} custom-call(bf16[1152,1152]{1,0:T(8,128)(2,1)S(1)} %order.1.refs_0_.refs_1_.refs_3_, bf16[128,1152]{1,0:T(8,128)(2,1)S(1)} %bitcast.16, f32[2,1152]{1,0:T(2,128)S(1)} %bitcast.20, f32[128,1152]{1,0:T(8,128)S(1)} %get-tuple-element.109.refs_3_.refs_1_, ...), custom_call_target="tpu_custom_call" | custom-call | tf_op jit(solution)/shard_map/middle_back/pallas_call | solution.py:397
  91.1 0.9 collective-permute-start.24
  92.0 1.4 %space_grad.1.refs_3_ = bf16[128,576]{1,0:T(8,128)(2,1)S(1)} custom-call(s32[3,1152]{1,0:T(4,128)S(1)} %pad_add_fusion.refs_0_.refs_2_, f32[128,1152]{1,0:T(8,128)S(1)} %middle_back.1.refs_1_.refs_3_, bf16[288,4736]{1,0:T(8,128)(2,1)S(1)} %get-tuple-element.91.refs_1_.refs_4_.refs_5_.refs_9_.refs_2_.refs_8_.refs_3_, ...), custom_call_target="tpu_custom_call" | custom-call | tf_op jit(solution)/shard_map/space_grad/pallas_call | solution.py:397
  93.4 2.8 %space_back.1 = (bf16[128,576]{1,0:T(8,128)(2,1)S(1)}, f32[128,1152]{1,0:T(8,128)S(1)}, bf16[64,1152]{1,0:T(8,128)(2,1)S(1)}, bf16[64,1152]{1,0:T(8,128)(2,1)S(1)}) custom-call(bf16[128,576]{1,0:T(8,128)(2,1)S(1)} %get-tuple-element.115.refs_0_, bf16[256,1152]{1,0:T(8,128)(2,1)S(1)} %get-tuple-element.116.refs_1_, ...), custom_call_target="tpu_custom_call" | custom-call | tf_op jit(solution)/shard_map/space_back/pallas_call | solution.py:397
  96.2 2.1 %collective-permute-start.21 = (bf16[64,1152]{1,0:T(8,128)(2,1)S(1)}, bf16[64,1152]{1,0:T(8,128)(2,1)S(1)}, u32[]{:S(2)}, u32[]{:S(2)}) collective-permute-start(bf16[64,1152]{1,0:T(8,128)(2,1)S(1)} %get-tuple-element.120), channel_id=1, source_target_pairs={{0,1},{1,2},{2,3},{4,5},{5,6},{6,7},{8,9},{9,10},{10,11},{12,13},{... | collective-permute-start | bytes 442376 | tf_op jit(solution)/shard_map/ppermute | solution.py:658
  98.3 1.3 %collective-permute-start.22 = (bf16[64,1152]{1,0:T(8,128)(2,1)S(1)}, bf16[64,1152]{1,0:T(8,128)(2,1)S(1)}, u32[]{:S(2)}, u32[]{:S(2)}) collective-permute-start(bf16[64,1152]{1,0:T(8,128)(2,1)S(1)} %get-tuple-element.121), channel_id=1, source_target_pairs={{1,0},{2,1},{3,2},{5,4},{6,5},{7,6},{9,8},{10,9},{11,10},{13,12},{... | collective-permute-start | bytes 442376 | tf_op jit(solution)/shard_map/ppermute | solution.py:659
  99.6 1.7 %collective-permute-done.24 = bf16[144,1152]{1,0:T(8,128)(2,1)S(1)} collective-permute-done((bf16[144,1152]{1,0:T(8,128)(2,1)S(1)}, bf16[144,1152]{1,0:T(8,128)(2,1)S(1)}, u32[]{:S(2)}, u32[]{:S(2)}) %collective-permute-start.24) | collective-permute-done | bytes 331808 | tf_op jit(solution)/shard_map/ppermute | solution.py:411
  101.5 2.7 %collective-permute-start.26 = (bf16[36,1152]{1,0:T(8,128)(2,1)S(1)}, bf16[36,1152]{1,0:T(8,128)(2,1)S(1)}, u32[]{:S(2)}, u32[]{:S(2)}) collective-permute-start(bf16[36,1152]{1,0:T(8,128)(2,1)S(1)} %get-tuple-element.133), channel_id=1, source_target_pairs={{0,16},{8,24},{16,0},{24,8},{1,17},{9,25},{17,1},{25,9},{2,18},{10... | collective-permute-start | bytes 248840 | tf_op jit(solution)/shard_map/ppermute | solution.py:411
  104.1 1.3 %collective-permute-start.27 = (bf16[36,1152]{1,0:T(8,128)(2,1)S(1)}, bf16[36,1152]{1,0:T(8,128)(2,1)S(1)}, u32[]{:S(2)}, u32[]{:S(2)}) collective-permute-start(bf16[36,1152]{1,0:T(8,128)(2,1)S(1)} %get-tuple-element.132), channel_id=1, source_target_pairs={{0,24},{8,16},{16,8},{24,0},{1,25},{9,17},{17,9},{25,1},{2,26},{10... | collective-permute-start | bytes 248840 | tf_op jit(solution)/shard_map/ppermute | solution.py:411
  105.5 3.1 %start_back.1 = bf16[128,1152]{1,0:T(8,128)(2,1)} custom-call(bf16[1152,1152]{1,0:T(8,128)(2,1)S(1)} %order.1.refs_0_.refs_1_.refs_3_, bf16[128,1152]{1,0:T(8,128)(2,1)S(1)} %bitcast.11, f32[2,1152]{1,0:T(2,128)S(1)} %bitcast.21, f32[128,1152]{1,0:T(8,128)S(1)} %middle_back.1.refs_1_.refs_3_, bf16[128,576]{1,0:T(8,128)(2,1)S(1)} %get-tuple-element.118.refs_4_, ...), custom_call_target="tpu_custom_call" | custom-call | tf_op jit(solution)/shard_map/start_back/pallas_call | solution.py:397
  108.6 2.0 %result.1 = bf16[128,1152]{1,0:T(8,128)(2,1)} custom-call(s32[3,1152]{1,0:T(4,128)S(1)} %pad_add_fusion.refs_0_.refs_2_, f32[128,1152]{1,0:T(8,128)S(1)} %get-tuple-element.109.refs_3_.refs_1_, bf16[128,2304]{1,0:T(8,128)(2,1)S(1)} %get-tuple-element.122.refs_4_.refs_2_, ...), custom_call_target="tpu_custom_call" | custom-call | tf_op jit(solution)/shard_map/result/pallas_call | solution.py:397
  110.5 1.3 %collective-permute-done.26 = bf16[36,1152]{1,0:T(8,128)(2,1)S(1)} collective-permute-done((bf16[36,1152]{1,0:T(8,128)(2,1)S(1)}, bf16[36,1152]{1,0:T(8,128)(2,1)S(1)}, u32[]{:S(2)}, u32[]{:S(2)}) %collective-permute-start.26) | collective-permute-done | bytes 82976 | tf_op jit(solution)/shard_map/ppermute | solution.py:411
  (68 shorter events, 7.2 us)
Async XLA Ops:
  3.0 13.1 %collective-permute-start = (bf16[72,2304]{1,0:T(8,128)(2,1)}, bf16[72,2304]{1,0:T(8,128)(2,1)S(1)}, u32[]{:S(2)}, u32[]{:S(2)}) collective-permute-start(bf16[72,2304]{1,0:T(8,128)(2,1)} %get-tuple-element.67), channel_id=1, source_target_pairs={{0,8},{8,16},{16,24},{24,0},{1,9},{9,17},{17,25},{25,1},{2,10},{10... | collective-permute-start | bytes 995336 | tf_op jit(solution)/shard_map/ppermute | solution.py:501
  6.1 23.7 %collective-permute-start.4 = (bf16[72,4608]{1,0:T(8,128)(2,1)}, bf16[72,4608]{1,0:T(8,128)(2,1)S(1)}, u32[]{:S(2)}, u32[]{:S(2)}) collective-permute-start(bf16[72,4608]{1,0:T(8,128)(2,1)} %get-tuple-element.69.refs_4_), channel_id=1, source_target_pairs={{0,2},{1,3},{2,0},{3,1},{4,6},{5,7},{6,4},{7,5},{8,10},{9,11},{10,... | collective-permute-start | bytes 1990664 | tf_op jit(solution)/shard_map/ppermute | solution.py:411
  7.6 8.4 %collective-permute-start.1 = (bf16[128,1152]{1,0:T(8,128)(2,1)}, bf16[128,1152]{1,0:T(8,128)(2,1)S(1)}, u32[]{:S(2)}, u32[]{:S(2)}) collective-permute-start(bf16[128,1152]{1,0:T(8,128)(2,1)} %bitcast.7), channel_id=1, source_target_pairs={{0,4},{4,0},{1,5},{5,1},{2,6},{6,2},{3,7},{7,3},{8,12},{12,8},{9,1... | collective-permute-start | bytes 884744 | tf_op jit(solution)/shard_map/ppermute | solution.py:411
  16.0 15.3 %copy-start.5 = (bf16[128,1152]{1,0:T(8,128)(2,1)}, bf16[128,1152]{1,0:T(8,128)(2,1)S(1)}, u32[]{:S(2)}) copy-start(bf16[128,1152]{1,0:T(8,128)(2,1)S(1)} %collective-permute-done.1.refs_5_) | copy-start | bytes 884740
  16.1 15.2 %copy-start.3 = (bf16[72,2304]{1,0:T(8,128)(2,1)}, bf16[72,2304]{1,0:T(8,128)(2,1)S(1)}, u32[]{:S(2)}) copy-start(bf16[72,2304]{1,0:T(8,128)(2,1)S(1)} %collective-permute-done.refs_6_) | copy-start | bytes 995332
  16.1 13.7 %collective-permute-start.2 = (bf16[72,2304]{1,0:T(8,128)(2,1)S(1)}, bf16[72,2304]{1,0:T(8,128)(2,1)S(1)}, u32[]{:S(2)}, u32[]{:S(2)}) collective-permute-start(bf16[72,2304]{1,0:T(8,128)(2,1)S(1)} %collective-permute-done.refs_6_), channel_id=1, source_target_pairs={{0,2},{1,3},{2,0},{3,1},{4,6},{5,7},{6,4},{7,5},{8,10},{9,11},{10,... | collective-permute-start | bytes 995336 | tf_op jit(solution)/shard_map/ppermute | solution.py:411
  17.6 12.2 %collective-permute-start.3 = (bf16[72,2304]{1,0:T(8,128)(2,1)S(1)}, bf16[72,2304]{1,0:T(8,128)(2,1)S(1)}, u32[]{:S(2)}, u32[]{:S(2)}) collective-permute-start(bf16[72,2304]{1,0:T(8,128)(2,1)S(1)} %collective-permute-done.refs_6_), channel_id=1, source_target_pairs={{0,4},{4,0},{1,5},{5,1},{2,6},{6,2},{3,7},{7,3},{8,12},{12,8},{9,1... | collective-permute-start | bytes 995336 | tf_op jit(solution)/shard_map/ppermute | solution.py:411
  19.1 10.6 %collective-permute-start.6 = (bf16[72,2304]{1,0:T(8,128)(2,1)S(1)}, bf16[72,2304]{1,0:T(8,128)(2,1)S(1)}, u32[]{:S(2)}, u32[]{:S(2)}) collective-permute-start(bf16[72,2304]{1,0:T(8,128)(2,1)S(1)} %collective-permute-done.refs_6_), channel_id=1, source_target_pairs={{0,8},{8,16},{16,24},{24,0},{1,9},{9,17},{17,25},{25,1},{2,10},{10... | collective-permute-start | bytes 995336 | tf_op jit(solution)/shard_map/ppermute | solution.py:501
  19.7 25.0 %copy-start.2 = (bf16[72,4608]{1,0:T(8,128)(2,1)S(1)}, bf16[72,4608]{1,0:T(8,128)(2,1)}, u32[]{:S(2)}) copy-start(bf16[72,4608]{1,0:T(8,128)(2,1)} %get-tuple-element.69.refs_4_) | copy-start | bytes 1990660
  20.7 8.6 %collective-permute-start.5 = (bf16[64,1152]{1,0:T(8,128)(2,1)S(1)}, bf16[64,1152]{1,0:T(8,128)(2,1)S(1)}, u32[]{:S(2)}, u32[]{:S(2)}) collective-permute-start(bf16[64,1152]{1,0:T(8,128)(2,1)S(1)} %slice.30), channel_id=1, source_target_pairs={{0,4},{4,0},{1,5},{5,1},{2,6},{6,2},{3,7},{7,3},{8,12},{12,8},{9,1... | collective-permute-start | bytes 442376 | tf_op jit(solution)/shard_map/ppermute | solution.py:411
  31.3 12.1 %collective-permute-start.7 = (bf16[72,3456]{1,0:T(8,128)(2,1)}, bf16[72,3456]{1,0:T(8,128)(2,1)S(1)}, u32[]{:S(2)}, u32[]{:S(2)}) collective-permute-start(bf16[72,3456]{1,0:T(8,128)(2,1)} %get-tuple-element.76), channel_id=1, source_target_pairs={{0,2},{1,3},{2,0},{3,1},{4,6},{5,7},{6,4},{7,5},{8,10},{9,11},{10,... | collective-permute-start | bytes 1493000 | tf_op jit(solution)/shard_map/ppermute | solution.py:411
  32.8 11.8 %collective-permute-start.8 = (bf16[72,3456]{1,0:T(8,128)(2,1)}, bf16[72,3456]{1,0:T(8,128)(2,1)S(1)}, u32[]{:S(2)}, u32[]{:S(2)}) collective-permute-start(bf16[72,3456]{1,0:T(8,128)(2,1)} %get-tuple-element.77), channel_id=1, source_target_pairs={{0,4},{4,0},{1,5},{5,1},{2,6},{6,2},{3,7},{7,3},{8,12},{12,8},{9,1... | collective-permute-start | bytes 1493000 | tf_op jit(solution)/shard_map/ppermute | solution.py:411
  34.3 10.3 %copy-start.4 = (bf16[72,2304]{1,0:T(8,128)(2,1)S(1)}, bf16[72,2304]{1,0:T(8,128)(2,1)}, u32[]{:S(2)}) copy-start(bf16[72,2304]{1,0:T(8,128)(2,1)} %copy-done.3) | copy-start | bytes 995332
  34.4 10.3 %collective-permute-start.9 = (bf16[72,2304]{1,0:T(8,128)(2,1)S(1)}, bf16[72,2304]{1,0:T(8,128)(2,1)S(1)}, u32[]{:S(2)}, u32[]{:S(2)}) collective-permute-start(bf16[72,2304]{1,0:T(8,128)(2,1)S(1)} %collective-permute-done.6.refs_1_.refs_3_), channel_id=1, source_target_pairs={{0,8},{8,16},{16,24},{24,0},{1,9},{9,17},{17,25},{25,1},{2,10},{10... | collective-permute-start | bytes 995336 | tf_op jit(solution)/shard_map/ppermute | solution.py:501
  37.2 10.9 %copy-start = (bf16[1,1,128,1152]{3,2,1,0:T(8,128)(2,1)S(1)}, bf16[1,1,128,1152]{3,2,1,0:T(8,128)(2,1)}, u32[]{:S(2)}) copy-start(bf16[1,1,128,1152]{3,2,1,0:T(8,128)(2,1)} %param.15) | copy-start | bytes 884740
  45.9 14.1 %collective-permute-start.14 = (bf16[288,4736]{1,0:T(8,128)(2,1)S(1)}, bf16[288,4736]{1,0:T(8,128)(2,1)S(1)}, u32[]{:S(2)}, u32[]{:S(2)}) collective-permute-start(bf16[288,4736]{1,0:T(8,128)(2,1)S(1)} %get-tuple-element.91.refs_1_.refs_4_.refs_5_.refs_9_.refs_2_.refs_8_.refs_3_), channel_id=1, source_target_pairs={{0,1},{1,0},{2,3},{3,2},{4,5},{5,4},{6,7},{7,6},{8,9},{9,8},{10,11... | collective-permute-start | bytes 8183816 | tf_op jit(solution)/shard_map/ppermute | solution.py:411
  46.0 13.8 %collective-permute-start.10 = (bf16[72,3456]{1,0:T(8,128)(2,1)S(1)}, bf16[72,3456]{1,0:T(8,128)(2,1)S(1)}, u32[]{:S(2)}, u32[]{:S(2)}) collective-permute-start(bf16[72,3456]{1,0:T(8,128)(2,1)S(1)} %get-tuple-element.85), channel_id=1, source_target_pairs={{0,2},{1,3},{2,0},{3,1},{4,6},{5,7},{6,4},{7,5},{8,10},{9,11},{10,... | collective-permute-start | bytes 1493000 | tf_op jit(solution)/shard_map/ppermute | solution.py:411
  46.6 13.4 %collective-permute-start.11 = (bf16[72,3456]{1,0:T(8,128)(2,1)S(1)}, bf16[72,3456]{1,0:T(8,128)(2,1)S(1)}, u32[]{:S(2)}, u32[]{:S(2)}) collective-permute-start(bf16[72,3456]{1,0:T(8,128)(2,1)S(1)} %get-tuple-element.86), channel_id=1, source_target_pairs={{0,4},{4,0},{1,5},{5,1},{2,6},{6,2},{3,7},{7,3},{8,12},{12,8},{9,1... | collective-permute-start | bytes 1493000 | tf_op jit(solution)/shard_map/ppermute | solution.py:411
  48.1 3.1 %collective-permute-start.12 = (bf16[64,1152]{1,0:T(8,128)(2,1)S(1)}, bf16[64,1152]{1,0:T(8,128)(2,1)S(1)}, u32[]{:S(2)}, u32[]{:S(2)}) collective-permute-start(bf16[64,1152]{1,0:T(8,128)(2,1)S(1)} %get-tuple-element.135), channel_id=1, source_target_pairs={{0,1},{1,2},{2,3},{4,5},{5,6},{6,7},{8,9},{9,10},{10,11},{12,13},{... | collective-permute-start | bytes 442376 | tf_op jit(solution)/shard_map/ppermute | solution.py:476
  49.9 14.6 %copy-start.7 = (f32[1,2,1152]{2,1,0:T(2,128)S(1)}, f32[1,2,1152]{2,1,0:T(2,128)}, u32[]{:S(2)}) copy-start(f32[1,2,1152]{2,1,0:T(2,128)} %param.17) | copy-start | bytes 27652
  49.9 4.5 %collective-permute-start.13 = (bf16[64,1152]{1,0:T(8,128)(2,1)S(1)}, bf16[64,1152]{1,0:T(8,128)(2,1)S(1)}, u32[]{:S(2)}, u32[]{:S(2)}) collective-permute-start(bf16[64,1152]{1,0:T(8,128)(2,1)S(1)} %get-tuple-element.134), channel_id=1, source_target_pairs={{1,0},{2,1},{3,2},{5,4},{6,5},{7,6},{9,8},{10,9},{11,10},{13,12},{... | collective-permute-start | bytes 442376 | tf_op jit(solution)/shard_map/ppermute | solution.py:477
  61.0 8.3 %collective-permute-start.17 = (bf16[216,4736]{1,0:T(8,128)(2,1)S(1)}, bf16[216,4736]{1,0:T(8,128)(2,1)S(1)}, u32[]{:S(2)}, u32[]{:S(2)}) collective-permute-start(bf16[216,4736]{1,0:T(8,128)(2,1)S(1)} %get-tuple-element.98.refs_2_.refs_5_.refs_6_.refs_10_.refs_3_.refs_9_.refs_4_), channel_id=1, source_target_pairs={{0,1},{1,0},{2,3},{3,2},{4,5},{5,4},{6,7},{7,6},{8,9},{9,8},{10,11... | collective-permute-start | bytes 6137864 | tf_op jit(solution)/shard_map/ppermute | solution.py:411
  62.3 6.2 %collective-permute-start.15 = (bf16[72,1152]{1,0:T(8,128)(2,1)S(1)}, bf16[72,1152]{1,0:T(8,128)(2,1)S(1)}, u32[]{:S(2)}, u32[]{:S(2)}) collective-permute-start(bf16[72,1152]{1,0:T(8,128)(2,1)S(1)} %get-tuple-element.94), channel_id=1, source_target_pairs={{0,2},{1,3},{2,0},{3,1},{4,6},{5,7},{6,4},{7,5},{8,10},{9,11},{10,... | collective-permute-start | bytes 497672 | tf_op jit(solution)/shard_map/ppermute | solution.py:411
  63.1 6.3 %collective-permute-start.16 = (bf16[72,1152]{1,0:T(8,128)(2,1)S(1)}, bf16[72,1152]{1,0:T(8,128)(2,1)S(1)}, u32[]{:S(2)}, u32[]{:S(2)}) collective-permute-start(bf16[72,1152]{1,0:T(8,128)(2,1)S(1)} %get-tuple-element.95), channel_id=1, source_target_pairs={{0,4},{4,0},{1,5},{5,1},{2,6},{6,2},{3,7},{7,3},{8,12},{12,8},{9,1... | collective-permute-start | bytes 497672 | tf_op jit(solution)/shard_map/ppermute | solution.py:411
  65.7 4.7 %copy-start.1 = (bf16[1,1,128,1152]{3,2,1,0:T(8,128)(2,1)S(1)}, bf16[1,1,128,1152]{3,2,1,0:T(8,128)(2,1)}, u32[]{:S(2)}) copy-start(bf16[1,1,128,1152]{3,2,1,0:T(8,128)(2,1)} %param.16) | copy-start | bytes 884740
  65.7 6.8 %copy-start.8 = (s32[2,4]{1,0:T(2,128)S(1)}, s32[2,4]{1,0:T(2,128)}, u32[]{:S(2)}) copy-start(s32[2,4]{1,0:T(2,128)} %refs_1_.4) | copy-start | bytes 100
  70.3 2.2 %collective-permute-start.18 = (bf16[72,4736]{1,0:T(8,128)(2,1)S(1)}, bf16[72,4736]{1,0:T(8,128)(2,1)S(1)}, u32[]{:S(2)}, u32[]{:S(2)}) collective-permute-start(bf16[72,4736]{1,0:T(8,128)(2,1)S(1)} %join.1.refs_6_.refs_7_.refs_11_.refs_4_.refs_10_.refs_5_), channel_id=1, source_target_pairs={{0,1},{1,0},{2,3},{3,2},{4,5},{5,4},{6,7},{7,6},{8,9},{9,8},{10,11... | collective-permute-start | bytes 2045960 | tf_op jit(solution)/shard_map/ppermute | solution.py:411
  70.4 7.0 %copy-start.10 = (s32[576]{0:T(1024)S(1)}, s32[576]{0:T(1024)}, u32[]{:S(2)}) copy-start(s32[576]{0:T(1024)} %constant.75.clone) | copy-start | bytes 6916
  70.4 7.0 %copy-start.11 = (s32[576]{0:T(1024)S(1)}, s32[576]{0:T(1024)}, u32[]{:S(2)}) copy-start(s32[576]{0:T(1024)} %constant.74.clone) | copy-start | bytes 6916
  70.4 6.9 %copy-start.12 = (s32[576]{0:T(1024)S(1)}, s32[576]{0:T(1024)}, u32[]{:S(2)}) copy-start(s32[576]{0:T(1024)} %constant.73.clone) | copy-start | bytes 6916
  70.5 9.9 %collective-permute-start.20 = (bf16[64,1152]{1,0:T(8,128)(2,1)S(1)}, bf16[64,1152]{1,0:T(8,128)(2,1)S(1)}, u32[]{:S(2)}, u32[]{:S(2)}) collective-permute-start(bf16[64,1152]{1,0:T(8,128)(2,1)S(1)} %slice.33), channel_id=1, source_target_pairs={{0,4},{4,0},{1,5},{5,1},{2,6},{6,2},{3,7},{7,3},{8,12},{12,8},{9,1... | collective-permute-start | bytes 442376 | tf_op jit(solution)/shard_map/ppermute | solution.py:411
  75.8 6.3 %collective-permute-start.19 = (bf16[128,576]{1,0:T(8,128)(2,1)S(1)}, bf16[128,576]{1,0:T(8,128)(2,1)S(1)}, u32[]{:S(2)}, u32[]{:S(2)}) collective-permute-start(bf16[128,576]{1,0:T(8,128)(2,1)S(1)} %get-tuple-element.108.refs_4_), channel_id=1, source_target_pairs={{0,4},{4,0},{1,5},{5,1},{2,6},{6,2},{3,7},{7,3},{8,12},{12,8},{9,1... | collective-permute-start | bytes 442376 | tf_op jit(solution)/shard_map/ppermute | solution.py:411
  80.3 1.8 %copy-start.6 = (bf16[128,1152]{1,0:T(8,128)(2,1)S(1)}, bf16[128,1152]{1,0:T(8,128)(2,1)}, u32[]{:S(2)}) copy-start(bf16[128,1152]{1,0:T(8,128)(2,1)} %copy-done.5) | copy-start | bytes 884740
  80.4 1.8 %copy-start.9 = (s32[2,2]{1,0:T(2,128)S(1)}, s32[2,2]{1,0:T(2,128)}, u32[]{:S(2)}) copy-start(s32[2,2]{1,0:T(2,128)} %refs_1_.5) | copy-start | bytes 52
  88.2 2.7 %collective-permute-start.23 = (bf16[288,1152]{1,0:T(8,128)(2,1)S(1)}, bf16[288,1152]{1,0:T(8,128)(2,1)S(1)}, u32[]{:S(2)}, u32[]{:S(2)}) collective-permute-start(bf16[288,1152]{1,0:T(8,128)(2,1)S(1)} %get-tuple-element.125), channel_id=1, source_target_pairs={{0,1},{1,0},{2,3},{3,2},{4,5},{5,4},{6,7},{7,6},{8,9},{9,8},{10,11... | collective-permute-start | bytes 1990664 | tf_op jit(solution)/shard_map/ppermute | solution.py:411
  91.1 10.3 %collective-permute-start.24 = (bf16[144,1152]{1,0:T(8,128)(2,1)S(1)}, bf16[144,1152]{1,0:T(8,128)(2,1)S(1)}, u32[]{:S(2)}, u32[]{:S(2)}) collective-permute-start(bf16[144,1152]{1,0:T(8,128)(2,1)S(1)} %slice.41), channel_id=1, source_target_pairs={{0,2},{1,3},{2,0},{3,1},{4,6},{5,7},{6,4},{7,5},{8,10},{9,11},{10,... | collective-permute-start | bytes 995336 | tf_op jit(solution)/shard_map/ppermute | solution.py:411
  96.2 9.3 %collective-permute-start.21 = (bf16[64,1152]{1,0:T(8,128)(2,1)S(1)}, bf16[64,1152]{1,0:T(8,128)(2,1)S(1)}, u32[]{:S(2)}, u32[]{:S(2)}) collective-permute-start(bf16[64,1152]{1,0:T(8,128)(2,1)S(1)} %get-tuple-element.120), channel_id=1, source_target_pairs={{0,1},{1,2},{2,3},{4,5},{5,6},{6,7},{8,9},{9,10},{10,11},{12,13},{... | collective-permute-start | bytes 442376 | tf_op jit(solution)/shard_map/ppermute | solution.py:658
  98.3 7.2 %collective-permute-start.22 = (bf16[64,1152]{1,0:T(8,128)(2,1)S(1)}, bf16[64,1152]{1,0:T(8,128)(2,1)S(1)}, u32[]{:S(2)}, u32[]{:S(2)}) collective-permute-start(bf16[64,1152]{1,0:T(8,128)(2,1)S(1)} %get-tuple-element.121), channel_id=1, source_target_pairs={{1,0},{2,1},{3,2},{5,4},{6,5},{7,6},{9,8},{10,9},{11,10},{13,12},{... | collective-permute-start | bytes 442376 | tf_op jit(solution)/shard_map/ppermute | solution.py:659
  101.5 10.4 %collective-permute-start.26 = (bf16[36,1152]{1,0:T(8,128)(2,1)S(1)}, bf16[36,1152]{1,0:T(8,128)(2,1)S(1)}, u32[]{:S(2)}, u32[]{:S(2)}) collective-permute-start(bf16[36,1152]{1,0:T(8,128)(2,1)S(1)} %get-tuple-element.133), channel_id=1, source_target_pairs={{0,16},{8,24},{16,0},{24,8},{1,17},{9,25},{17,1},{25,9},{2,18},{10... | collective-permute-start | bytes 248840 | tf_op jit(solution)/shard_map/ppermute | solution.py:411
  104.1 7.7 %collective-permute-start.27 = (bf16[36,1152]{1,0:T(8,128)(2,1)S(1)}, bf16[36,1152]{1,0:T(8,128)(2,1)S(1)}, u32[]{:S(2)}, u32[]{:S(2)}) collective-permute-start(bf16[36,1152]{1,0:T(8,128)(2,1)S(1)} %get-tuple-element.132), channel_id=1, source_target_pairs={{0,24},{8,16},{16,8},{24,0},{1,25},{9,17},{17,9},{25,1},{2,26},{10... | collective-permute-start | bytes 248840 | tf_op jit(solution)/shard_map/ppermute | solution.py:411
  105.5 6.9 %collective-permute-start.25 = (bf16[36,1152]{1,0:T(8,128)(2,1)S(1)}, bf16[36,1152]{1,0:T(8,128)(2,1)S(1)}, u32[]{:S(2)}, u32[]{:S(2)}) collective-permute-start(bf16[36,1152]{1,0:T(8,128)(2,1)S(1)} %get-tuple-element.131), channel_id=1, source_target_pairs={{0,8},{8,0},{16,24},{24,16},{1,9},{9,1},{17,25},{25,17},{2,10},{10... | collective-permute-start | bytes 248840 | tf_op jit(solution)/shard_map/ppermute | solution.py:411

commit v4 on v3

--- a/solution.py
+++ b/solution.py
@@ -96,10 +96,17 @@
     return total
 
 
-def behind(grad, weight, start, stop, select):
+def behind(grad, weight, start, stop, select, rounded=False):
+    count = grad.shape[0]
     turned = grad.astype(F32).T.astype(BF16)
-    parts = [mm(ref[:, start:stop], turned).astype(BF16) for ref in weight]
-    return mm(select[...], jnp.concatenate(parts, axis=0)).T
+    parts = [mm(ref[:, start:stop], turned) for ref in weight]
+    part = jnp.concatenate(parts, axis=0)
+    high = part.astype(BF16)
+    if rounded:
+        return mm(select[...], high).T.astype(BF16)
+    low = (part - high.astype(F32)).astype(BF16)
+    both = mm(select[...], jnp.concatenate([high, low], axis=1))
+    return (both[:, :count] + both[:, count:]).T
 
 
 def space_allowed(place, pattern, span, tiles):
@@ -144,8 +151,9 @@
         (space_qkv, time_qkv, space_out, time_out), ready,
     )
     outs = jnp.concatenate([space_out[...].astype(F32), time_out[...].astype(F32)], axis=0)
-    parts = [space_qkv[...].astype(F32), time_qkv[...].astype(F32), outs]
-    packed[...] = jnp.concatenate(parts, axis=1).astype(BF16)
+    packed[:, : 3 * WIDTH] = space_qkv[...]
+    packed[:, 3 * WIDTH : 6 * WIDTH] = time_qkv[...]
+    packed[:, 6 * WIDTH :] = outs.astype(BF16)
     lanes = half_ref.shape[1]
     first = lax.axis_index("seq") == 0
 
@@ -252,8 +260,9 @@
     upstream = jnp.concatenate([ref[...] for ref in refs[:parts]], axis=0).astype(BF16)
     weight, grad_ref = refs[parts:]
     *_, out, stop = columns(upstream.shape[1])
-    select = expander(index_ref[row : row + 1, :])
-    grad_ref[...] = behind(upstream, weight, out, stop, select).astype(BF16)
+    grad_ref[...] = behind(
+        upstream, weight, out, stop, expander(index_ref[row : row + 1, :]), rounded=True
+    )
 
 
 def time_att_kernel(allowed_ref, rows_ref, grad_ref, out_ref):

time: 113 us -> 113 us (level)
  no operation moved by 1% of the time
where the time goes in v4:
time: 113 us
  waiting for transfers between devices  37.9 us (34%)
  Pallas kernels  35.9 us (32%)
  starting transfers between devices  35.3 us (31%)
  other arithmetic  1.82 us (2%)
  local copies, waits for them, and re-layouts  1.19 us (1%)
    pallas_call x18, Pallas kernels, call(): pl.pallas_call(body, name=name, in_specs=specs, out_specs=[VMEM] * len(ou...  35.9 us
    ppermute x21, waiting for transfers between devices, swapped(): return lax.ppermute(array, axis, [(i, i ^ bit) for i in range(count)])  34.6 us
    ppermute x21, starting transfers between devices, swapped(): return lax.ppermute(array, axis, [(i, i ^ bit) for i in range(count)])  23.6 us
    ppermute x3, starting transfers between devices, onward(): lax.ppermute(piece, 'dp', [(i, (i + 1) % clips) for i in range(clips)])  5.2 us
    ppermute x1, waiting for transfers between devices, rims(): return (before, lax.ppermute(rows[:span], 'tile', fall))  3.17 us
  transfers between devices with their start and end apart: 28, of which 16 were waited for; matrix products, arithmetic and copies ran while one was open for 2% of the time, Pallas kernels for 20%

profile of v4, /device:TPU:0, one launch (start us, length us, event | category | flops | bytes accessed | tf_op | source)
XLA Modules:
  0.0 113.1 jit_solution(18411300148354778255)
XLA Ops:
  0.6 2.4 %pack.1 = (bf16[72,4608]{1,0:T(8,128)(2,1)}, bf16[72,2304]{1,0:T(8,128)(2,1)}) custom-call(bf16[72,1728]{1,0:T(8,128)(2,1)} %refs_0_.1, bf16[72,1728]{1,0:T(8,128)(2,1)} %refs_1_.3, bf16[36,1152]{1,0:T(8,128)(2,1)} %refs_2_.1, bf16[36,1152]{1,0:T(8,128)(2,1)} %refs_3_.1), custom_call_target="tpu_custom_call" | custom-call | tf_op jit(solution)/shard_map/pack/pallas_call | solution.py:406
  3.0 3.1 %collective-permute-start = (bf16[72,2304]{1,0:T(8,128)(2,1)}, bf16[72,2304]{1,0:T(8,128)(2,1)S(1)}, u32[]{:S(2)}, u32[]{:S(2)}) collective-permute-start(bf16[72,2304]{1,0:T(8,128)(2,1)} %get-tuple-element.67), channel_id=1, source_target_pairs={{0,8},{8,16},{16,24},{24,0},{1,9},{9,17},{17,25},{25,1},{2,10},{10... | collective-permute-start | bytes 995336 | tf_op jit(solution)/shard_map/ppermute | solution.py:510
  6.1 1.5 %collective-permute-start.4 = (bf16[72,4608]{1,0:T(8,128)(2,1)}, bf16[72,4608]{1,0:T(8,128)(2,1)S(1)}, u32[]{:S(2)}, u32[]{:S(2)}) collective-permute-start(bf16[72,4608]{1,0:T(8,128)(2,1)} %get-tuple-element.69.refs_4_), channel_id=1, source_target_pairs={{0,2},{1,3},{2,0},{3,1},{4,6},{5,7},{6,4},{7,5},{8,10},{9,11},{10,... | collective-permute-start | bytes 1990664 | tf_op jit(solution)/shard_map/ppermute | solution.py:420
  7.6 1.5 %collective-permute-start.1 = (bf16[128,1152]{1,0:T(8,128)(2,1)}, bf16[128,1152]{1,0:T(8,128)(2,1)S(1)}, u32[]{:S(2)}, u32[]{:S(2)}) collective-permute-start(bf16[128,1152]{1,0:T(8,128)(2,1)} %bitcast.7), channel_id=1, source_target_pairs={{0,4},{4,0},{1,5},{5,1},{2,6},{6,2},{3,7},{7,3},{8,12},{12,8},{9,1... | collective-permute-start | bytes 884744 | tf_op jit(solution)/shard_map/ppermute | solution.py:420
  9.1 6.9 %collective-permute-done.1.refs_5_ = bf16[128,1152]{1,0:T(8,128)(2,1)S(1)} collective-permute-done((bf16[128,1152]{1,0:T(8,128)(2,1)}, bf16[128,1152]{1,0:T(8,128)(2,1)S(1)}, u32[]{:S(2)}, u32[]{:S(2)}) %collective-permute-start.1) | collective-permute-done | bytes 294944 | tf_op jit(solution)/shard_map/ppermute | solution.py:420
  16.1 1.5 %collective-permute-start.2 = (bf16[72,2304]{1,0:T(8,128)(2,1)S(1)}, bf16[72,2304]{1,0:T(8,128)(2,1)S(1)}, u32[]{:S(2)}, u32[]{:S(2)}) collective-permute-start(bf16[72,2304]{1,0:T(8,128)(2,1)S(1)} %collective-permute-done.refs_6_), channel_id=1, source_target_pairs={{0,2},{1,3},{2,0},{3,1},{4,6},{5,7},{6,4},{7,5},{8,10},{9,11},{10,... | collective-permute-start | bytes 995336 | tf_op jit(solution)/shard_map/ppermute | solution.py:420
  17.6 1.5 %collective-permute-start.3 = (bf16[72,2304]{1,0:T(8,128)(2,1)S(1)}, bf16[72,2304]{1,0:T(8,128)(2,1)S(1)}, u32[]{:S(2)}, u32[]{:S(2)}) collective-permute-start(bf16[72,2304]{1,0:T(8,128)(2,1)S(1)} %collective-permute-done.refs_6_), channel_id=1, source_target_pairs={{0,4},{4,0},{1,5},{5,1},{2,6},{6,2},{3,7},{7,3},{8,12},{12,8},{9,1... | collective-permute-start | bytes 995336 | tf_op jit(solution)/shard_map/ppermute | solution.py:420
  19.7 1.0 slice.30
  21.3 7.9 %collective-permute-done.5.refs_2_.refs_3_ = bf16[64,1152]{1,0:T(8,128)(2,1)S(1)} collective-permute-done((bf16[64,1152]{1,0:T(8,128)(2,1)S(1)}, bf16[64,1152]{1,0:T(8,128)(2,1)S(1)}, u32[]{:S(2)}, u32[]{:S(2)}) %collective-permute-start.5) | collective-permute-done | bytes 147488 | tf_op jit(solution)/shard_map/ppermute | solution.py:420
  29.8 1.5 %send.3 = (bf16[72,3456]{1,0:T(8,128)(2,1)}, bf16[72,3456]{1,0:T(8,128)(2,1)}) custom-call(s32[2]{0:T(128)S(1)} %pad_add_fusion.1.refs_0_, bf16[72,2304]{1,0:T(8,128)(2,1)S(1)} %collective-permute-done.6.refs_1_.refs_3_, bf16[72,2304]{1,0:T(8,128)(2,1)S(1)} %collective-permute-done.2.refs_2_.refs_8_, bf16[72,2304]{1,0:T(8,128)(2,1)S(1)} %collective-permute-done.3.refs_3_.refs_7_), custom_call_target="tpu_custom_call" | custom-call | tf_op jit(solution)/shard_map/send/pallas_call | solution.py:406
  31.3 1.5 %collective-permute-start.7 = (bf16[72,3456]{1,0:T(8,128)(2,1)}, bf16[72,3456]{1,0:T(8,128)(2,1)S(1)}, u32[]{:S(2)}, u32[]{:S(2)}) collective-permute-start(bf16[72,3456]{1,0:T(8,128)(2,1)} %get-tuple-element.76), channel_id=1, source_target_pairs={{0,2},{1,3},{2,0},{3,1},{4,6},{5,7},{6,4},{7,5},{8,10},{9,11},{10,... | collective-permute-start | bytes 1493000 | tf_op jit(solution)/shard_map/ppermute | solution.py:420
  32.8 1.5 %collective-permute-start.8 = (bf16[72,3456]{1,0:T(8,128)(2,1)}, bf16[72,3456]{1,0:T(8,128)(2,1)S(1)}, u32[]{:S(2)}, u32[]{:S(2)}) collective-permute-start(bf16[72,3456]{1,0:T(8,128)(2,1)} %get-tuple-element.77), channel_id=1, source_target_pairs={{0,4},{4,0},{1,5},{5,1},{2,6},{6,2},{3,7},{7,3},{8,12},{12,8},{9,1... | collective-permute-start | bytes 1493000 | tf_op jit(solution)/shard_map/ppermute | solution.py:420
  34.4 1.6 %collective-permute-start.9 = (bf16[72,2304]{1,0:T(8,128)(2,1)S(1)}, bf16[72,2304]{1,0:T(8,128)(2,1)S(1)}, u32[]{:S(2)}, u32[]{:S(2)}) collective-permute-start(bf16[72,2304]{1,0:T(8,128)(2,1)S(1)} %collective-permute-done.6.refs_1_.refs_3_), channel_id=1, source_target_pairs={{0,8},{8,16},{16,24},{24,0},{1,9},{9,17},{17,25},{25,1},{2,10},{10... | collective-permute-start | bytes 995336 | tf_op jit(solution)/shard_map/ppermute | solution.py:510
  37.2 6.2 %collective-permute-done.7.refs_2_.refs_9_.refs_5_ = bf16[72,3456]{1,0:T(8,128)(2,1)S(1)} collective-permute-done((bf16[72,3456]{1,0:T(8,128)(2,1)}, bf16[72,3456]{1,0:T(8,128)(2,1)S(1)}, u32[]{:S(2)}, u32[]{:S(2)}) %collective-permute-start.7) | collective-permute-done | bytes 497696 | tf_op jit(solution)/shard_map/ppermute | solution.py:420
  43.5 1.2 %collective-permute-done.8.refs_3_.refs_10_.refs_4_ = bf16[72,3456]{1,0:T(8,128)(2,1)S(1)} collective-permute-done((bf16[72,3456]{1,0:T(8,128)(2,1)}, bf16[72,3456]{1,0:T(8,128)(2,1)S(1)}, u32[]{:S(2)}, u32[]{:S(2)}) %collective-permute-start.8) | collective-permute-done | bytes 497696 | tf_op jit(solution)/shard_map/ppermute | solution.py:420
  44.7 1.2 %send.4 = (bf16[72,3456]{1,0:T(8,128)(2,1)S(1)}, bf16[72,3456]{1,0:T(8,128)(2,1)S(1)}, bf16[288,4736]{1,0:T(8,128)(2,1)S(1)}) custom-call(s32[2]{0:T(128)S(1)} %pad_add_fusion.1.refs_0_, bf16[72,2304]{1,0:T(8,128)(2,1)S(1)} %collective-permute-done.9.refs_1_.refs_8_, bf16[72,3456]{1,0:T(8,128)(2,1)S(1)} %collective-permute-done.7.refs_2_.refs_9_.refs_5_, ...), custom_call_target="tpu_custom_call" | custom-call | tf_op jit(solution)/shard_map/send/pallas_call | solution.py:406
  46.6 1.5 %collective-permute-start.11 = (bf16[72,3456]{1,0:T(8,128)(2,1)S(1)}, bf16[72,3456]{1,0:T(8,128)(2,1)S(1)}, u32[]{:S(2)}, u32[]{:S(2)}) collective-permute-start(bf16[72,3456]{1,0:T(8,128)(2,1)S(1)} %get-tuple-element.86), channel_id=1, source_target_pairs={{0,4},{4,0},{1,5},{5,1},{2,6},{6,2},{3,7},{7,3},{8,12},{12,8},{9,1... | collective-permute-start | bytes 1493000 | tf_op jit(solution)/shard_map/ppermute | solution.py:420
  48.1 1.8 %collective-permute-start.12 = (bf16[64,1152]{1,0:T(8,128)(2,1)S(1)}, bf16[64,1152]{1,0:T(8,128)(2,1)S(1)}, u32[]{:S(2)}, u32[]{:S(2)}) collective-permute-start(bf16[64,1152]{1,0:T(8,128)(2,1)S(1)} %get-tuple-element.135), channel_id=1, source_target_pairs={{0,1},{1,2},{2,3},{4,5},{5,6},{6,7},{8,9},{9,10},{10,11},{12,13},{... | collective-permute-start | bytes 442376 | tf_op jit(solution)/shard_map/ppermute | solution.py:485
  49.9 1.3 %collective-permute-start.13 = (bf16[64,1152]{1,0:T(8,128)(2,1)S(1)}, bf16[64,1152]{1,0:T(8,128)(2,1)S(1)}, u32[]{:S(2)}, u32[]{:S(2)}) collective-permute-start(bf16[64,1152]{1,0:T(8,128)(2,1)S(1)} %get-tuple-element.134), channel_id=1, source_target_pairs={{1,0},{2,1},{3,2},{5,4},{6,5},{7,6},{9,8},{10,9},{11,10},{13,12},{... | collective-permute-start | bytes 442376 | tf_op jit(solution)/shard_map/ppermute | solution.py:486
  51.3 3.2 %collective-permute-done.13.refs_3_ = bf16[64,1152]{1,0:T(8,128)(2,1)S(1)} collective-permute-done((bf16[64,1152]{1,0:T(8,128)(2,1)S(1)}, bf16[64,1152]{1,0:T(8,128)(2,1)S(1)}, u32[]{:S(2)}, u32[]{:S(2)}) %collective-permute-start.13) | collective-permute-done | bytes 147488 | tf_op jit(solution)/shard_map/ppermute | solution.py:486
  54.4 5.3 %collective-permute-done.10.refs_1_.refs_6_ = bf16[72,3456]{1,0:T(8,128)(2,1)S(1)} collective-permute-done((bf16[72,3456]{1,0:T(8,128)(2,1)S(1)}, bf16[72,3456]{1,0:T(8,128)(2,1)S(1)}, u32[]{:S(2)}, u32[]{:S(2)}) %collective-permute-start.10) | collective-permute-done | bytes 497696 | tf_op jit(solution)/shard_map/ppermute | solution.py:420
  60.0 1.0 send.5
  61.0 1.2 %collective-permute-start.17 = (bf16[216,4736]{1,0:T(8,128)(2,1)S(1)}, bf16[216,4736]{1,0:T(8,128)(2,1)S(1)}, u32[]{:S(2)}, u32[]{:S(2)}) collective-permute-start(bf16[216,4736]{1,0:T(8,128)(2,1)S(1)} %get-tuple-element.98.refs_2_.refs_5_.refs_6_.refs_10_.refs_3_.refs_9_.refs_4_), channel_id=1, source_target_pairs={{0,1},{1,0},{2,3},{3,2},{4,5},{5,4},{6,7},{7,6},{8,9},{9,8},{10,11... | collective-permute-start | bytes 6137864 | tf_op jit(solution)/shard_map/ppermute | solution.py:420
  63.1 1.5 %collective-permute-start.16 = (bf16[72,1152]{1,0:T(8,128)(2,1)S(1)}, bf16[72,1152]{1,0:T(8,128)(2,1)S(1)}, u32[]{:S(2)}, u32[]{:S(2)}) collective-permute-start(bf16[72,1152]{1,0:T(8,128)(2,1)S(1)} %get-tuple-element.95), channel_id=1, source_target_pairs={{0,4},{4,0},{1,5},{5,1},{2,6},{6,2},{3,7},{7,3},{8,12},{12,8},{9,1... | collective-permute-start | bytes 497672 | tf_op jit(solution)/shard_map/ppermute | solution.py:420
  64.6 1.1 normed.1.refs_0_.refs_2_
  65.7 1.4 %space_early.1.refs_3_ = f32[256,1728]{1,0:T(8,128)S(1)} custom-call(bf16[256,1152]{1,0:T(8,128)(2,1)S(1)} %normed.1.refs_0_.refs_2_, bf16[288,4736]{1,0:T(8,128)(2,1)S(1)} %get-tuple-element.91.refs_1_.refs_4_.refs_5_.refs_9_.refs_2_.refs_8_.refs_3_, bf16[216,4736]{1,0:T(8,128)(2,1)S(1)} %get-tuple-element.98.refs_2_.refs_5_.refs_6_.refs_10_.refs_3_.refs_9_.refs_4_, ...), custom_call_target="tpu_custom_call" | custom-call | flops 1024 | bytes 1024 | tf_op jit(solution)/shard_map/space_early/pallas_call | solution.py:406
  67.1 1.4 %collective-permute-done.15.refs_2_ = bf16[72,1152]{1,0:T(8,128)(2,1)S(1)} collective-permute-done((bf16[72,1152]{1,0:T(8,128)(2,1)S(1)}, bf16[72,1152]{1,0:T(8,128)(2,1)S(1)}, u32[]{:S(2)}, u32[]{:S(2)}) %collective-permute-start.15) | collective-permute-done | bytes 165920 | tf_op jit(solution)/shard_map/ppermute | solution.py:420
  68.5 0.9 collective-permute-done.16.refs_3_
  69.4 0.9 join.1.refs_6_.refs_7_.refs_11_.refs_4_.refs_10_.refs_5_
  70.5 1.6 %collective-permute-start.20 = (bf16[64,1152]{1,0:T(8,128)(2,1)S(1)}, bf16[64,1152]{1,0:T(8,128)(2,1)S(1)}, u32[]{:S(2)}, u32[]{:S(2)}) collective-permute-start(bf16[64,1152]{1,0:T(8,128)(2,1)S(1)} %slice.33), channel_id=1, source_target_pairs={{0,4},{4,0},{1,5},{5,1},{2,6},{6,2},{3,7},{7,3},{8,12},{12,8},{9,1... | collective-permute-start | bytes 442376 | tf_op jit(solution)/shard_map/ppermute | solution.py:420
  72.5 3.3 %forward.1 = (bf16[128,576]{1,0:T(8,128)(2,1)S(1)}, bf16[256,1152]{1,0:T(8,128)(2,1)S(1)}, bf16[128,576]{1,0:T(8,128)(2,1)S(1)}, f32[1024,256]{1,0:T(8,128)S(1)}) custom-call(s32[2]{0:T(128)S(1)} %pad_add_fusion.1.refs_0_, s32[2,4]{1,0:T(2,128)S(1)} %copy-done.8, bf16[256,1152]{1,0:T(8,128)(2,1)S(1)} %normed.1.refs_0_.refs_2_, ...), custom_call_target="tpu_custom_call" | custom-call | flops 1024 | bytes 1024 | tf_op jit(solution)/shard_map/forward/pallas_call | solution.py:406
  75.8 1.6 %collective-permute-start.19 = (bf16[128,576]{1,0:T(8,128)(2,1)S(1)}, bf16[128,576]{1,0:T(8,128)(2,1)S(1)}, u32[]{:S(2)}, u32[]{:S(2)}) collective-permute-start(bf16[128,576]{1,0:T(8,128)(2,1)S(1)} %get-tuple-element.108.refs_4_), channel_id=1, source_target_pairs={{0,4},{4,0},{1,5},{5,1},{2,6},{6,2},{3,7},{7,3},{8,12},{12,8},{9,1... | collective-permute-start | bytes 442376 | tf_op jit(solution)/shard_map/ppermute | solution.py:420
  77.4 2.9 %middle.1 = (f32[128,1152]{1,0:T(8,128)S(1)}, bf16[128,1728]{1,0:T(8,128)(2,1)S(1)}) custom-call(s32[3,1152]{1,0:T(4,128)S(1)} %pad_add_fusion.refs_0_.refs_2_, bf16[1152,1152]{1,0:T(8,128)(2,1)S(1)} %order.1.refs_0_.refs_1_.refs_3_, bf16[128,1152]{1,0:T(8,128)(2,1)S(1)} %bitcast.10, f32[2,1152]{1,0:T(2,128)S(1)} %bitcast.18, ...), custom_call_target="tpu_custom_call" | custom-call | flops 1024 | bytes 1024 | tf_op jit(solution)/shard_map/middle/pallas_call | solution.py:406
  80.4 1.7 %att_grad.1.refs_8_ = bf16[256,576]{1,0:T(8,128)(2,1)S(1)} custom-call(s32[3,1152]{1,0:T(4,128)S(1)} %pad_add_fusion.refs_0_.refs_2_, bf16[128,1152]{1,0:T(8,128)(2,1)S(1)} %bitcast.14, bf16[64,1152]{1,0:T(8,128)(2,1)S(1)} %collective-permute-done.5.refs_2_.refs_3_, bf16[64,1152]{1,0:T(8,128)(2,1)S(1)} %collective-permute-done.20.refs_3_.refs_4_, ...), custom_call_target="tpu_custom_call" | custom-call | tf_op jit(solution)/shard_map/att_grad/pallas_call | solution.py:406
  82.1 4.7 %time_att.1 = (bf16[128,2304]{1,0:T(8,128)(2,1)S(1)}, bf16[256,576]{1,0:T(8,128)(2,1)S(1)}) custom-call(s32[2]{0:T(128)S(1)} %pad_add_fusion.1.refs_0_, s32[2,2]{1,0:T(2,128)S(1)} %copy-done.9, s32[3,1152]{1,0:T(4,128)S(1)} %pad_add_fusion.refs_0_.refs_2_, bf16[1152,1152]{1,0:T(8,128)(2,1)S(1)} %order.1.refs_0_.refs_1_.refs_3_, f32[2,1152]{1,0:T(2,128)S(1)} %bitcast.19, ...), custom_call_target="tpu_custom_call" | custom-call | tf_op jit(solution)/shard_map/time_att/pallas_call | solution.py:406
  86.8 1.3 %term.1 = (bf16[288,1152]{1,0:T(8,128)(2,1)S(1)}, bf16[288,1152]{1,0:T(8,128)(2,1)S(1)}) custom-call(s32[1,576]{1,0:T(1,128)S(1)} %reshape.29.refs_0_, bf16[256,576]{1,0:T(8,128)(2,1)S(1)} %get-tuple-element.123.refs_1_, bf16[128,1152]{1,0:T(8,128)(2,1)S(1)} %bitcast.15, bf16[64,1152]{1,0:T(8,128)(2,1)S(1)} %collective-permute-done.5.refs_2_.refs_3_, ...), custom_call_target="tpu_custom_call" | custom-call | tf_op jit(solution)/shard_map/term/pallas_call | solution.py:406
  88.3 2.7 %middle_back.1.refs_1_.refs_3_ = f32[128,1152]{1,0:T(8,128)S(1)} custom-call(bf16[1152,1152]{1,0:T(8,128)(2,1)S(1)} %order.1.refs_0_.refs_1_.refs_3_, bf16[128,1152]{1,0:T(8,128)(2,1)S(1)} %bitcast.16, f32[2,1152]{1,0:T(2,128)S(1)} %bitcast.20, f32[128,1152]{1,0:T(8,128)S(1)} %get-tuple-element.109.refs_3_.refs_1_, ...), custom_call_target="tpu_custom_call" | custom-call | tf_op jit(solution)/shard_map/middle_back/pallas_call | solution.py:406
  91.2 0.9 collective-permute-start.24
  92.1 1.4 %space_grad.1.refs_3_ = bf16[128,576]{1,0:T(8,128)(2,1)S(1)} custom-call(s32[3,1152]{1,0:T(4,128)S(1)} %pad_add_fusion.refs_0_.refs_2_, f32[128,1152]{1,0:T(8,128)S(1)} %middle_back.1.refs_1_.refs_3_, bf16[288,4736]{1,0:T(8,128)(2,1)S(1)} %get-tuple-element.91.refs_1_.refs_4_.refs_5_.refs_9_.refs_2_.refs_8_.refs_3_, ...), custom_call_target="tpu_custom_call" | custom-call | tf_op jit(solution)/shard_map/space_grad/pallas_call | solution.py:406
  93.5 2.8 %space_back.1 = (bf16[128,576]{1,0:T(8,128)(2,1)S(1)}, f32[128,1152]{1,0:T(8,128)S(1)}, bf16[64,1152]{1,0:T(8,128)(2,1)S(1)}, bf16[64,1152]{1,0:T(8,128)(2,1)S(1)}) custom-call(bf16[128,576]{1,0:T(8,128)(2,1)S(1)} %get-tuple-element.115.refs_0_, bf16[256,1152]{1,0:T(8,128)(2,1)S(1)} %get-tuple-element.116.refs_1_, ...), custom_call_target="tpu_custom_call" | custom-call | tf_op jit(solution)/shard_map/space_back/pallas_call | solution.py:406
  96.3 2.1 %collective-permute-start.21 = (bf16[64,1152]{1,0:T(8,128)(2,1)S(1)}, bf16[64,1152]{1,0:T(8,128)(2,1)S(1)}, u32[]{:S(2)}, u32[]{:S(2)}) collective-permute-start(bf16[64,1152]{1,0:T(8,128)(2,1)S(1)} %get-tuple-element.120), channel_id=1, source_target_pairs={{0,1},{1,2},{2,3},{4,5},{5,6},{6,7},{8,9},{9,10},{10,11},{12,13},{... | collective-permute-start | bytes 442376 | tf_op jit(solution)/shard_map/ppermute | solution.py:667
  98.4 1.3 %collective-permute-start.22 = (bf16[64,1152]{1,0:T(8,128)(2,1)S(1)}, bf16[64,1152]{1,0:T(8,128)(2,1)S(1)}, u32[]{:S(2)}, u32[]{:S(2)}) collective-permute-start(bf16[64,1152]{1,0:T(8,128)(2,1)S(1)} %get-tuple-element.121), channel_id=1, source_target_pairs={{1,0},{2,1},{3,2},{5,4},{6,5},{7,6},{9,8},{10,9},{11,10},{13,12},{... | collective-permute-start | bytes 442376 | tf_op jit(solution)/shard_map/ppermute | solution.py:668
  99.7 1.7 %collective-permute-done.24 = bf16[144,1152]{1,0:T(8,128)(2,1)S(1)} collective-permute-done((bf16[144,1152]{1,0:T(8,128)(2,1)S(1)}, bf16[144,1152]{1,0:T(8,128)(2,1)S(1)}, u32[]{:S(2)}, u32[]{:S(2)}) %collective-permute-start.24) | collective-permute-done | bytes 331808 | tf_op jit(solution)/shard_map/ppermute | solution.py:420
  101.6 2.7 %collective-permute-start.26 = (bf16[36,1152]{1,0:T(8,128)(2,1)S(1)}, bf16[36,1152]{1,0:T(8,128)(2,1)S(1)}, u32[]{:S(2)}, u32[]{:S(2)}) collective-permute-start(bf16[36,1152]{1,0:T(8,128)(2,1)S(1)} %get-tuple-element.133), channel_id=1, source_target_pairs={{0,16},{8,24},{16,0},{24,8},{1,17},{9,25},{17,1},{25,9},{2,18},{10... | collective-permute-start | bytes 248840 | tf_op jit(solution)/shard_map/ppermute | solution.py:420
  104.2 1.3 %collective-permute-start.27 = (bf16[36,1152]{1,0:T(8,128)(2,1)S(1)}, bf16[36,1152]{1,0:T(8,128)(2,1)S(1)}, u32[]{:S(2)}, u32[]{:S(2)}) collective-permute-start(bf16[36,1152]{1,0:T(8,128)(2,1)S(1)} %get-tuple-element.132), channel_id=1, source_target_pairs={{0,24},{8,16},{16,8},{24,0},{1,25},{9,17},{17,9},{25,1},{2,26},{10... | collective-permute-start | bytes 248840 | tf_op jit(solution)/shard_map/ppermute | solution.py:420
  105.6 3.2 %start_back.1 = bf16[128,1152]{1,0:T(8,128)(2,1)} custom-call(bf16[1152,1152]{1,0:T(8,128)(2,1)S(1)} %order.1.refs_0_.refs_1_.refs_3_, bf16[128,1152]{1,0:T(8,128)(2,1)S(1)} %bitcast.11, f32[2,1152]{1,0:T(2,128)S(1)} %bitcast.21, f32[128,1152]{1,0:T(8,128)S(1)} %middle_back.1.refs_1_.refs_3_, bf16[128,576]{1,0:T(8,128)(2,1)S(1)} %get-tuple-element.118.refs_4_, ...), custom_call_target="tpu_custom_call" | custom-call | tf_op jit(solution)/shard_map/start_back/pallas_call | solution.py:406
  108.7 1.9 %result.1 = bf16[128,1152]{1,0:T(8,128)(2,1)} custom-call(s32[3,1152]{1,0:T(4,128)S(1)} %pad_add_fusion.refs_0_.refs_2_, f32[128,1152]{1,0:T(8,128)S(1)} %get-tuple-element.109.refs_3_.refs_1_, bf16[128,2304]{1,0:T(8,128)(2,1)S(1)} %get-tuple-element.122.refs_4_.refs_2_, ...), custom_call_target="tpu_custom_call" | custom-call | tf_op jit(solution)/shard_map/result/pallas_call | solution.py:406
  110.7 1.3 %collective-permute-done.26 = bf16[36,1152]{1,0:T(8,128)(2,1)S(1)} collective-permute-done((bf16[36,1152]{1,0:T(8,128)(2,1)S(1)}, bf16[36,1152]{1,0:T(8,128)(2,1)S(1)}, u32[]{:S(2)}, u32[]{:S(2)}) %collective-permute-start.26) | collective-permute-done | bytes 82976 | tf_op jit(solution)/shard_map/ppermute | solution.py:420
  (68 shorter events, 7.2 us)
Async XLA Ops:
  3.0 13.1 %collective-permute-start = (bf16[72,2304]{1,0:T(8,128)(2,1)}, bf16[72,2304]{1,0:T(8,128)(2,1)S(1)}, u32[]{:S(2)}, u32[]{:S(2)}) collective-permute-start(bf16[72,2304]{1,0:T(8,128)(2,1)} %get-tuple-element.67), channel_id=1, source_target_pairs={{0,8},{8,16},{16,24},{24,0},{1,9},{9,17},{17,25},{25,1},{2,10},{10... | collective-permute-start | bytes 995336 | tf_op jit(solution)/shard_map/ppermute | solution.py:510
  6.1 23.7 %collective-permute-start.4 = (bf16[72,4608]{1,0:T(8,128)(2,1)}, bf16[72,4608]{1,0:T(8,128)(2,1)S(1)}, u32[]{:S(2)}, u32[]{:S(2)}) collective-permute-start(bf16[72,4608]{1,0:T(8,128)(2,1)} %get-tuple-element.69.refs_4_), channel_id=1, source_target_pairs={{0,2},{1,3},{2,0},{3,1},{4,6},{5,7},{6,4},{7,5},{8,10},{9,11},{10,... | collective-permute-start | bytes 1990664 | tf_op jit(solution)/shard_map/ppermute | solution.py:420
  7.6 8.4 %collective-permute-start.1 = (bf16[128,1152]{1,0:T(8,128)(2,1)}, bf16[128,1152]{1,0:T(8,128)(2,1)S(1)}, u32[]{:S(2)}, u32[]{:S(2)}) collective-permute-start(bf16[128,1152]{1,0:T(8,128)(2,1)} %bitcast.7), channel_id=1, source_target_pairs={{0,4},{4,0},{1,5},{5,1},{2,6},{6,2},{3,7},{7,3},{8,12},{12,8},{9,1... | collective-permute-start | bytes 884744 | tf_op jit(solution)/shard_map/ppermute | solution.py:420
  16.0 15.3 %copy-start.5 = (bf16[128,1152]{1,0:T(8,128)(2,1)}, bf16[128,1152]{1,0:T(8,128)(2,1)S(1)}, u32[]{:S(2)}) copy-start(bf16[128,1152]{1,0:T(8,128)(2,1)S(1)} %collective-permute-done.1.refs_5_) | copy-start | bytes 884740
  16.1 15.2 %copy-start.3 = (bf16[72,2304]{1,0:T(8,128)(2,1)}, bf16[72,2304]{1,0:T(8,128)(2,1)S(1)}, u32[]{:S(2)}) copy-start(bf16[72,2304]{1,0:T(8,128)(2,1)S(1)} %collective-permute-done.refs_6_) | copy-start | bytes 995332
  16.1 13.7 %collective-permute-start.2 = (bf16[72,2304]{1,0:T(8,128)(2,1)S(1)}, bf16[72,2304]{1,0:T(8,128)(2,1)S(1)}, u32[]{:S(2)}, u32[]{:S(2)}) collective-permute-start(bf16[72,2304]{1,0:T(8,128)(2,1)S(1)} %collective-permute-done.refs_6_), channel_id=1, source_target_pairs={{0,2},{1,3},{2,0},{3,1},{4,6},{5,7},{6,4},{7,5},{8,10},{9,11},{10,... | collective-permute-start | bytes 995336 | tf_op jit(solution)/shard_map/ppermute | solution.py:420
  17.6 12.2 %collective-permute-start.3 = (bf16[72,2304]{1,0:T(8,128)(2,1)S(1)}, bf16[72,2304]{1,0:T(8,128)(2,1)S(1)}, u32[]{:S(2)}, u32[]{:S(2)}) collective-permute-start(bf16[72,2304]{1,0:T(8,128)(2,1)S(1)} %collective-permute-done.refs_6_), channel_id=1, source_target_pairs={{0,4},{4,0},{1,5},{5,1},{2,6},{6,2},{3,7},{7,3},{8,12},{12,8},{9,1... | collective-permute-start | bytes 995336 | tf_op jit(solution)/shard_map/ppermute | solution.py:420
  19.2 10.6 %collective-permute-start.6 = (bf16[72,2304]{1,0:T(8,128)(2,1)S(1)}, bf16[72,2304]{1,0:T(8,128)(2,1)S(1)}, u32[]{:S(2)}, u32[]{:S(2)}) collective-permute-start(bf16[72,2304]{1,0:T(8,128)(2,1)S(1)} %collective-permute-done.refs_6_), channel_id=1, source_target_pairs={{0,8},{8,16},{16,24},{24,0},{1,9},{9,17},{17,25},{25,1},{2,10},{10... | collective-permute-start | bytes 995336 | tf_op jit(solution)/shard_map/ppermute | solution.py:510
  19.7 25.0 %copy-start.2 = (bf16[72,4608]{1,0:T(8,128)(2,1)S(1)}, bf16[72,4608]{1,0:T(8,128)(2,1)}, u32[]{:S(2)}) copy-start(bf16[72,4608]{1,0:T(8,128)(2,1)} %get-tuple-element.69.refs_4_) | copy-start | bytes 1990660
  20.7 8.5 %collective-permute-start.5 = (bf16[64,1152]{1,0:T(8,128)(2,1)S(1)}, bf16[64,1152]{1,0:T(8,128)(2,1)S(1)}, u32[]{:S(2)}, u32[]{:S(2)}) collective-permute-start(bf16[64,1152]{1,0:T(8,128)(2,1)S(1)} %slice.30), channel_id=1, source_target_pairs={{0,4},{4,0},{1,5},{5,1},{2,6},{6,2},{3,7},{7,3},{8,12},{12,8},{9,1... | collective-permute-start | bytes 442376 | tf_op jit(solution)/shard_map/ppermute | solution.py:420
  31.3 12.1 %collective-permute-start.7 = (bf16[72,3456]{1,0:T(8,128)(2,1)}, bf16[72,3456]{1,0:T(8,128)(2,1)S(1)}, u32[]{:S(2)}, u32[]{:S(2)}) collective-permute-start(bf16[72,3456]{1,0:T(8,128)(2,1)} %get-tuple-element.76), channel_id=1, source_target_pairs={{0,2},{1,3},{2,0},{3,1},{4,6},{5,7},{6,4},{7,5},{8,10},{9,11},{10,... | collective-permute-start | bytes 1493000 | tf_op jit(solution)/shard_map/ppermute | solution.py:420
  32.8 11.8 %collective-permute-start.8 = (bf16[72,3456]{1,0:T(8,128)(2,1)}, bf16[72,3456]{1,0:T(8,128)(2,1)S(1)}, u32[]{:S(2)}, u32[]{:S(2)}) collective-permute-start(bf16[72,3456]{1,0:T(8,128)(2,1)} %get-tuple-element.77), channel_id=1, source_target_pairs={{0,4},{4,0},{1,5},{5,1},{2,6},{6,2},{3,7},{7,3},{8,12},{12,8},{9,1... | collective-permute-start | bytes 1493000 | tf_op jit(solution)/shard_map/ppermute | solution.py:420
  34.4 10.3 %copy-start.4 = (bf16[72,2304]{1,0:T(8,128)(2,1)S(1)}, bf16[72,2304]{1,0:T(8,128)(2,1)}, u32[]{:S(2)}) copy-start(bf16[72,2304]{1,0:T(8,128)(2,1)} %copy-done.3) | copy-start | bytes 995332
  34.4 10.3 %collective-permute-start.9 = (bf16[72,2304]{1,0:T(8,128)(2,1)S(1)}, bf16[72,2304]{1,0:T(8,128)(2,1)S(1)}, u32[]{:S(2)}, u32[]{:S(2)}) collective-permute-start(bf16[72,2304]{1,0:T(8,128)(2,1)S(1)} %collective-permute-done.6.refs_1_.refs_3_), channel_id=1, source_target_pairs={{0,8},{8,16},{16,24},{24,0},{1,9},{9,17},{17,25},{25,1},{2,10},{10... | collective-permute-start | bytes 995336 | tf_op jit(solution)/shard_map/ppermute | solution.py:510
  37.2 10.9 %copy-start = (bf16[1,1,128,1152]{3,2,1,0:T(8,128)(2,1)S(1)}, bf16[1,1,128,1152]{3,2,1,0:T(8,128)(2,1)}, u32[]{:S(2)}) copy-start(bf16[1,1,128,1152]{3,2,1,0:T(8,128)(2,1)} %param.15) | copy-start | bytes 884740
  45.9 14.1 %collective-permute-start.14 = (bf16[288,4736]{1,0:T(8,128)(2,1)S(1)}, bf16[288,4736]{1,0:T(8,128)(2,1)S(1)}, u32[]{:S(2)}, u32[]{:S(2)}) collective-permute-start(bf16[288,4736]{1,0:T(8,128)(2,1)S(1)} %get-tuple-element.91.refs_1_.refs_4_.refs_5_.refs_9_.refs_2_.refs_8_.refs_3_), channel_id=1, source_target_pairs={{0,1},{1,0},{2,3},{3,2},{4,5},{5,4},{6,7},{7,6},{8,9},{9,8},{10,11... | collective-permute-start | bytes 8183816 | tf_op jit(solution)/shard_map/ppermute | solution.py:420
  46.0 13.8 %collective-permute-start.10 = (bf16[72,3456]{1,0:T(8,128)(2,1)S(1)}, bf16[72,3456]{1,0:T(8,128)(2,1)S(1)}, u32[]{:S(2)}, u32[]{:S(2)}) collective-permute-start(bf16[72,3456]{1,0:T(8,128)(2,1)S(1)} %get-tuple-element.85), channel_id=1, source_target_pairs={{0,2},{1,3},{2,0},{3,1},{4,6},{5,7},{6,4},{7,5},{8,10},{9,11},{10,... | collective-permute-start | bytes 1493000 | tf_op jit(solution)/shard_map/ppermute | solution.py:420
  46.6 13.4 %collective-permute-start.11 = (bf16[72,3456]{1,0:T(8,128)(2,1)S(1)}, bf16[72,3456]{1,0:T(8,128)(2,1)S(1)}, u32[]{:S(2)}, u32[]{:S(2)}) collective-permute-start(bf16[72,3456]{1,0:T(8,128)(2,1)S(1)} %get-tuple-element.86), channel_id=1, source_target_pairs={{0,4},{4,0},{1,5},{5,1},{2,6},{6,2},{3,7},{7,3},{8,12},{12,8},{9,1... | collective-permute-start | bytes 1493000 | tf_op jit(solution)/shard_map/ppermute | solution.py:420
  48.1 3.1 %collective-permute-start.12 = (bf16[64,1152]{1,0:T(8,128)(2,1)S(1)}, bf16[64,1152]{1,0:T(8,128)(2,1)S(1)}, u32[]{:S(2)}, u32[]{:S(2)}) collective-permute-start(bf16[64,1152]{1,0:T(8,128)(2,1)S(1)} %get-tuple-element.135), channel_id=1, source_target_pairs={{0,1},{1,2},{2,3},{4,5},{5,6},{6,7},{8,9},{9,10},{10,11},{12,13},{... | collective-permute-start | bytes 442376 | tf_op jit(solution)/shard_map/ppermute | solution.py:485
  49.9 14.6 %copy-start.7 = (f32[1,2,1152]{2,1,0:T(2,128)S(1)}, f32[1,2,1152]{2,1,0:T(2,128)}, u32[]{:S(2)}) copy-start(f32[1,2,1152]{2,1,0:T(2,128)} %param.17) | copy-start | bytes 27652
  49.9 4.5 %collective-permute-start.13 = (bf16[64,1152]{1,0:T(8,128)(2,1)S(1)}, bf16[64,1152]{1,0:T(8,128)(2,1)S(1)}, u32[]{:S(2)}, u32[]{:S(2)}) collective-permute-start(bf16[64,1152]{1,0:T(8,128)(2,1)S(1)} %get-tuple-element.134), channel_id=1, source_target_pairs={{1,0},{2,1},{3,2},{5,4},{6,5},{7,6},{9,8},{10,9},{11,10},{13,12},{... | collective-permute-start | bytes 442376 | tf_op jit(solution)/shard_map/ppermute | solution.py:486
  61.0 8.3 %collective-permute-start.17 = (bf16[216,4736]{1,0:T(8,128)(2,1)S(1)}, bf16[216,4736]{1,0:T(8,128)(2,1)S(1)}, u32[]{:S(2)}, u32[]{:S(2)}) collective-permute-start(bf16[216,4736]{1,0:T(8,128)(2,1)S(1)} %get-tuple-element.98.refs_2_.refs_5_.refs_6_.refs_10_.refs_3_.refs_9_.refs_4_), channel_id=1, source_target_pairs={{0,1},{1,0},{2,3},{3,2},{4,5},{5,4},{6,7},{7,6},{8,9},{9,8},{10,11... | collective-permute-start | bytes 6137864 | tf_op jit(solution)/shard_map/ppermute | solution.py:420
  62.3 6.2 %collective-permute-start.15 = (bf16[72,1152]{1,0:T(8,128)(2,1)S(1)}, bf16[72,1152]{1,0:T(8,128)(2,1)S(1)}, u32[]{:S(2)}, u32[]{:S(2)}) collective-permute-start(bf16[72,1152]{1,0:T(8,128)(2,1)S(1)} %get-tuple-element.94), channel_id=1, source_target_pairs={{0,2},{1,3},{2,0},{3,1},{4,6},{5,7},{6,4},{7,5},{8,10},{9,11},{10,... | collective-permute-start | bytes 497672 | tf_op jit(solution)/shard_map/ppermute | solution.py:420
  63.1 6.3 %collective-permute-start.16 = (bf16[72,1152]{1,0:T(8,128)(2,1)S(1)}, bf16[72,1152]{1,0:T(8,128)(2,1)S(1)}, u32[]{:S(2)}, u32[]{:S(2)}) collective-permute-start(bf16[72,1152]{1,0:T(8,128)(2,1)S(1)} %get-tuple-element.95), channel_id=1, source_target_pairs={{0,4},{4,0},{1,5},{5,1},{2,6},{6,2},{3,7},{7,3},{8,12},{12,8},{9,1... | collective-permute-start | bytes 497672 | tf_op jit(solution)/shard_map/ppermute | solution.py:420
  65.7 4.7 %copy-start.1 = (bf16[1,1,128,1152]{3,2,1,0:T(8,128)(2,1)S(1)}, bf16[1,1,128,1152]{3,2,1,0:T(8,128)(2,1)}, u32[]{:S(2)}) copy-start(bf16[1,1,128,1152]{3,2,1,0:T(8,128)(2,1)} %param.16) | copy-start | bytes 884740
  65.7 6.8 %copy-start.8 = (s32[2,4]{1,0:T(2,128)S(1)}, s32[2,4]{1,0:T(2,128)}, u32[]{:S(2)}) copy-start(s32[2,4]{1,0:T(2,128)} %refs_1_.4) | copy-start | bytes 100
  70.3 2.2 %collective-permute-start.18 = (bf16[72,4736]{1,0:T(8,128)(2,1)S(1)}, bf16[72,4736]{1,0:T(8,128)(2,1)S(1)}, u32[]{:S(2)}, u32[]{:S(2)}) collective-permute-start(bf16[72,4736]{1,0:T(8,128)(2,1)S(1)} %join.1.refs_6_.refs_7_.refs_11_.refs_4_.refs_10_.refs_5_), channel_id=1, source_target_pairs={{0,1},{1,0},{2,3},{3,2},{4,5},{5,4},{6,7},{7,6},{8,9},{9,8},{10,11... | collective-permute-start | bytes 2045960 | tf_op jit(solution)/shard_map/ppermute | solution.py:420
  70.4 7.0 %copy-start.10 = (s32[576]{0:T(1024)S(1)}, s32[576]{0:T(1024)}, u32[]{:S(2)}) copy-start(s32[576]{0:T(1024)} %constant.75.clone) | copy-start | bytes 6916
  70.4 7.0 %copy-start.11 = (s32[576]{0:T(1024)S(1)}, s32[576]{0:T(1024)}, u32[]{:S(2)}) copy-start(s32[576]{0:T(1024)} %constant.74.clone) | copy-start | bytes 6916
  70.5 6.9 %copy-start.12 = (s32[576]{0:T(1024)S(1)}, s32[576]{0:T(1024)}, u32[]{:S(2)}) copy-start(s32[576]{0:T(1024)} %constant.73.clone) | copy-start | bytes 6916
  70.5 9.9 %collective-permute-start.20 = (bf16[64,1152]{1,0:T(8,128)(2,1)S(1)}, bf16[64,1152]{1,0:T(8,128)(2,1)S(1)}, u32[]{:S(2)}, u32[]{:S(2)}) collective-permute-start(bf16[64,1152]{1,0:T(8,128)(2,1)S(1)} %slice.33), channel_id=1, source_target_pairs={{0,4},{4,0},{1,5},{5,1},{2,6},{6,2},{3,7},{7,3},{8,12},{12,8},{9,1... | collective-permute-start | bytes 442376 | tf_op jit(solution)/shard_map/ppermute | solution.py:420
  75.8 6.3 %collective-permute-start.19 = (bf16[128,576]{1,0:T(8,128)(2,1)S(1)}, bf16[128,576]{1,0:T(8,128)(2,1)S(1)}, u32[]{:S(2)}, u32[]{:S(2)}) collective-permute-start(bf16[128,576]{1,0:T(8,128)(2,1)S(1)} %get-tuple-element.108.refs_4_), channel_id=1, source_target_pairs={{0,4},{4,0},{1,5},{5,1},{2,6},{6,2},{3,7},{7,3},{8,12},{12,8},{9,1... | collective-permute-start | bytes 442376 | tf_op jit(solution)/shard_map/ppermute | solution.py:420
  80.3 1.8 %copy-start.6 = (bf16[128,1152]{1,0:T(8,128)(2,1)S(1)}, bf16[128,1152]{1,0:T(8,128)(2,1)}, u32[]{:S(2)}) copy-start(bf16[128,1152]{1,0:T(8,128)(2,1)} %copy-done.5) | copy-start | bytes 884740
  80.4 1.8 %copy-start.9 = (s32[2,2]{1,0:T(2,128)S(1)}, s32[2,2]{1,0:T(2,128)}, u32[]{:S(2)}) copy-start(s32[2,2]{1,0:T(2,128)} %refs_1_.5) | copy-start | bytes 52
  88.2 2.8 %collective-permute-start.23 = (bf16[288,1152]{1,0:T(8,128)(2,1)S(1)}, bf16[288,1152]{1,0:T(8,128)(2,1)S(1)}, u32[]{:S(2)}, u32[]{:S(2)}) collective-permute-start(bf16[288,1152]{1,0:T(8,128)(2,1)S(1)} %get-tuple-element.125), channel_id=1, source_target_pairs={{0,1},{1,0},{2,3},{3,2},{4,5},{5,4},{6,7},{7,6},{8,9},{9,8},{10,11... | collective-permute-start | bytes 1990664 | tf_op jit(solution)/shard_map/ppermute | solution.py:420
  91.2 10.3 %collective-permute-start.24 = (bf16[144,1152]{1,0:T(8,128)(2,1)S(1)}, bf16[144,1152]{1,0:T(8,128)(2,1)S(1)}, u32[]{:S(2)}, u32[]{:S(2)}) collective-permute-start(bf16[144,1152]{1,0:T(8,128)(2,1)S(1)} %slice.41), channel_id=1, source_target_pairs={{0,2},{1,3},{2,0},{3,1},{4,6},{5,7},{6,4},{7,5},{8,10},{9,11},{10,... | collective-permute-start | bytes 995336 | tf_op jit(solution)/shard_map/ppermute | solution.py:420
  96.3 9.3 %collective-permute-start.21 = (bf16[64,1152]{1,0:T(8,128)(2,1)S(1)}, bf16[64,1152]{1,0:T(8,128)(2,1)S(1)}, u32[]{:S(2)}, u32[]{:S(2)}) collective-permute-start(bf16[64,1152]{1,0:T(8,128)(2,1)S(1)} %get-tuple-element.120), channel_id=1, source_target_pairs={{0,1},{1,2},{2,3},{4,5},{5,6},{6,7},{8,9},{9,10},{10,11},{12,13},{... | collective-permute-start | bytes 442376 | tf_op jit(solution)/shard_map/ppermute | solution.py:667
  98.4 7.2 %collective-permute-start.22 = (bf16[64,1152]{1,0:T(8,128)(2,1)S(1)}, bf16[64,1152]{1,0:T(8,128)(2,1)S(1)}, u32[]{:S(2)}, u32[]{:S(2)}) collective-permute-start(bf16[64,1152]{1,0:T(8,128)(2,1)S(1)} %get-tuple-element.121), channel_id=1, source_target_pairs={{1,0},{2,1},{3,2},{5,4},{6,5},{7,6},{9,8},{10,9},{11,10},{13,12},{... | collective-permute-start | bytes 442376 | tf_op jit(solution)/shard_map/ppermute | solution.py:668
  101.6 10.4 %collective-permute-start.26 = (bf16[36,1152]{1,0:T(8,128)(2,1)S(1)}, bf16[36,1152]{1,0:T(8,128)(2,1)S(1)}, u32[]{:S(2)}, u32[]{:S(2)}) collective-permute-start(bf16[36,1152]{1,0:T(8,128)(2,1)S(1)} %get-tuple-element.133), channel_id=1, source_target_pairs={{0,16},{8,24},{16,0},{24,8},{1,17},{9,25},{17,1},{25,9},{2,18},{10... | collective-permute-start | bytes 248840 | tf_op jit(solution)/shard_map/ppermute | solution.py:420
  104.2 7.7 %collective-permute-start.27 = (bf16[36,1152]{1,0:T(8,128)(2,1)S(1)}, bf16[36,1152]{1,0:T(8,128)(2,1)S(1)}, u32[]{:S(2)}, u32[]{:S(2)}) collective-permute-start(bf16[36,1152]{1,0:T(8,128)(2,1)S(1)} %get-tuple-element.132), channel_id=1, source_target_pairs={{0,24},{8,16},{16,8},{24,0},{1,25},{9,17},{17,9},{25,1},{2,26},{10... | collective-permute-start | bytes 248840 | tf_op jit(solution)/shard_map/ppermute | solution.py:420
  105.6 6.9 %collective-permute-start.25 = (bf16[36,1152]{1,0:T(8,128)(2,1)S(1)}, bf16[36,1152]{1,0:T(8,128)(2,1)S(1)}, u32[]{:S(2)}, u32[]{:S(2)}) collective-permute-start(bf16[36,1152]{1,0:T(8,128)(2,1)S(1)} %get-tuple-element.131), channel_id=1, source_target_pairs={{0,8},{8,0},{16,24},{24,16},{1,9},{9,1},{17,25},{25,17},{2,10},{10... | collective-permute-start | bytes 248840 | tf_op jit(solution)/shard_map/ppermute | solution.py:420
